TPU v7x, 256 devices: a whole 4x4x8 slice. The times are simulated.
256 devices in a mesh: fsdp: 32 (over x_lo, z, core), ep: 8 (over x_hi, y).
Axes of the slice: x: 4 (x_hi: 2, x_lo: 2; x = x_hi * 2 + x_lo), y: 4, z: 8, core: 2. Of those that a mesh axis runs over, the one named last changes fastest.
Arguments:
- tokens: bfloat16 [1024, 6144], P('ep'), may hold values from -6 to 6
- out_grad: bfloat16 [1024, 6144], P('ep'), may hold values from -6 to 6
- router_weight: float32 [6144, 8], replicated, may hold values from -0.15625 to 0.15625
- expert_in: bfloat16 [8, 6144, 5376], P('ep', None, 'fsdp'), may hold values from -0.078125 to 0.078125
- expert_out: bfloat16 [8, 5376, 6144], P('ep', 'fsdp'), may hold values from -0.078125 to 0.078125
- choices: int32 [1024, 2], P('ep'), may hold values from 0 to 7, as said below
- slots: int32 [1024, 2], P('ep'), may hold values from -1 to 31, as said below
Outputs:
- grad_tokens: bfloat16 [1024, 6144], P('ep', 'fsdp')
- grad_in: bfloat16 [8, 6144, 5376], P('ep', None, 'fsdp')
- grad_out: bfloat16 [8, 5376, 6144], P('ep', 'fsdp')
- grad_router: float32 [6144, 8], replicated
Inputs may be any that keep to these rules, and one draw needn't show every extreme that they name: `choices`: each row names two different experts. Within each aligned block of 128 rows, each slot value of 0 or more occurs at most once for each expert, and a choice is dropped only if all 32 slots of its expert are taken there; in every block some expert has all 32 slots taken.
All inputs are finite; a program needn't handle non-finite values.
Results may differ from a plain program's by a relative error of at most 0.019.
Values may be sent and summed in bfloat16 or wider, within the bound.
No kernel may reach another device: no remote copies, remote signals or barrier semaphores. Data moves between devices by JAX's collectives and lax.ppermute only.
A program may use at most 128 MiB of HBM per device.

v0:
```python
import jax
import jax.numpy as jnp
from jax import lax
from jax.sharding import PartitionSpec as P


def contract_last(left, right):
    return lax.dot_general(
        left, right, (((1,), (1,)), ((), ())), preferred_element_type=jnp.float32
    )


def per_device(tokens, out_grad, router_weight, expert_in, expert_out, choices, slots):
    tok_rows = tokens.shape[0]
    model_width = tokens.shape[1]
    expert_count = router_weight.shape[1]
    fsdp_size = lax.axis_size("fsdp")
    ep_size = lax.axis_size("ep")
    capacity = max(2, 2 * tok_rows // expert_count)
    slot_count = expert_count * capacity
    column_count = model_width // fsdp_size
    highest = lax.Precision.HIGHEST
    tokens_wide = tokens.astype(jnp.float32)
    logits = jnp.dot(tokens_wide, router_weight, precision=highest)
    chosen_hot = (choices[:, :, None] == jnp.arange(expert_count, dtype=jnp.int32)).astype(
        jnp.float32
    )
    chosen = jnp.sum(chosen_hot * logits[:, None, :], axis=2)
    first_gate = 1.0 / (1.0 + jnp.exp(chosen[:, 1] - chosen[:, 0]))
    second_gate = 1.0 / (1.0 + jnp.exp(chosen[:, 0] - chosen[:, 1]))
    gate_pair = jnp.stack([first_gate, second_gate], axis=1).astype(jnp.bfloat16)
    slot_keys = jnp.where(slots >= 0, choices * capacity + slots, -1)
    places = (slot_keys[:, :, None] == jnp.arange(slot_count, dtype=jnp.int32)).astype(jnp.float32)
    spread = jnp.sum(places, axis=1)
    spread_narrow = spread.astype(jnp.bfloat16)
    send_x = jnp.dot(spread_narrow.T, tokens, preferred_element_type=jnp.float32).astype(
        jnp.bfloat16
    )
    send_dy = jnp.dot(spread_narrow.T, out_grad, preferred_element_type=jnp.float32).astype(
        jnp.bfloat16
    )
    send_gate = jnp.einsum(
        "tks,tk->s", places, gate_pair.astype(jnp.float32), precision=highest
    ).astype(jnp.bfloat16)
    send_x = send_x.reshape(expert_count, capacity, model_width)
    send_dy = send_dy.reshape(expert_count, capacity, model_width)
    send_gate = send_gate.reshape(expert_count, capacity)
    arrived_x, arrived_dy, arrived_gate = (
        lax.all_to_all(send_x, "ep", split_axis=0, concat_axis=0, tiled=True),
        lax.all_to_all(send_dy, "ep", split_axis=0, concat_axis=0, tiled=True),
        lax.all_to_all(send_gate, "ep", split_axis=0, concat_axis=0, tiled=True),
    )
    rows_all = ep_size * capacity
    rows_x = arrived_x.reshape(rows_all, model_width)
    rows_dy = arrived_dy.reshape(rows_all, model_width)
    gate_wide = arrived_gate.reshape(rows_all, 1).astype(jnp.float32)
    w_in = expert_in[0]
    w_out = expert_out[0]
    pre_act = jnp.dot(rows_x, w_in, preferred_element_type=jnp.float32)
    back_proj = contract_last(rows_dy, w_out)
    sig_act = jax.nn.sigmoid(pre_act)
    hidden = (pre_act * sig_act).astype(jnp.bfloat16)
    hid_wide = hidden.astype(jnp.float32)
    row_score = jnp.sum(hid_wide * back_proj, axis=1)
    weighted = (hid_wide * gate_wide).astype(jnp.bfloat16)
    act_grad = (gate_wide * back_proj * sig_act * (1.0 + pre_act * (1.0 - sig_act))).astype(
        jnp.bfloat16
    )
    grad_out = jnp.dot(weighted.T, rows_dy, preferred_element_type=jnp.float32).astype(
        jnp.bfloat16
    )[None]
    grad_in = jnp.dot(rows_x.T, act_grad, preferred_element_type=jnp.float32).astype(jnp.bfloat16)[
        None
    ]
    row_partial = contract_last(act_grad, w_in)
    own_rows = lax.psum_scatter(row_partial, "fsdp", scatter_dimension=1, tiled=True)
    own_scores = lax.psum(row_score, "fsdp")
    returned, returned_scores = (
        lax.all_to_all(
            own_rows.reshape(ep_size, capacity, column_count),
            "ep",
            split_axis=0,
            concat_axis=0,
            tiled=True,
        ),
        lax.all_to_all(
            own_scores.reshape(ep_size, capacity), "ep", split_axis=0, concat_axis=0, tiled=True
        ),
    )
    expert_grad = jnp.dot(spread, returned.reshape(slot_count, column_count), precision=highest)
    taken_score = jnp.einsum(
        "tks,s->tk", places, returned_scores.reshape(slot_count), precision=highest
    )
    change = first_gate * second_gate * (taken_score[:, 0] - taken_score[:, 1])
    logit_grad = change[:, None] * (chosen_hot[:, 0, :] - chosen_hot[:, 1, :])
    first_column = lax.axis_index("fsdp") * column_count
    router_rows = lax.dynamic_slice_in_dim(router_weight, first_column, column_count, 0)
    grad_tokens = (expert_grad + jnp.dot(logit_grad, router_rows.T, precision=highest)).astype(
        jnp.bfloat16
    )
    router_part = jnp.dot(tokens_wide.T, logit_grad, precision=highest)
    grad_router = lax.psum(router_part.astype(jnp.bfloat16), "ep").astype(jnp.float32) / (
        tok_rows * ep_size
    )
    return (grad_tokens, grad_in, grad_out, grad_router)


def solution(mesh):
    placed = (
        P("ep", None),
        P("ep", None),
        P(),
        P("ep", None, "fsdp"),
        P("ep", "fsdp", None),
        P("ep", None),
        P("ep", None),
    )
    return jax.shard_map(
        per_device,
        mesh=mesh,
        in_specs=placed,
        out_specs=(P("ep", "fsdp"), P("ep", None, "fsdp"), P("ep", "fsdp", None), P()),
        check_vma=False,
    )
```

profile of v0, /device:TPU:1, one launch (start us, length us, event | category | flops | bytes accessed | tf_op | source)
XLA Modules:
  0.0 333.0 jit_solution(4675114679521939727)
XLA Ops:
  8.0 0.8 compare_select_fusion
  9.0 4.1 %convolution_convert_fusion = bf16[256,6144]{1,0:T(8,128)(2,1)} fusion(bf16[128,6144]{1,0:T(8,128)(2,1)} %param.7, f32[128,256]{1,0:T(8,128)S(1)} %convert_reduce_fusion), kind=kOutput, calls=%fused_computation | convolution fusion | flops 404258816 | bytes 4849664 | tf_op jit(solution)/shard_map/dot_general | solution.py:36
  13.0 7.5 %all-to-all-start.2 = ((bf16[8,32,6144]{2,1,0:T(8,128)(2,1)}), bf16[8,32,6144]{2,1,0:T(8,128)(2,1)}, u32[]{:S(2)}, u32[]{:S(2)}) async-start(bf16[8,32,6144]{2,1,0:T(8,128)(2,1)} %bitcast.51), calls=%async_computation.2 | async-start | bytes 6291456 | tf_op jit(solution)/shard_map/all_to_all | solution.py:49
  20.5 4.1 %convolution_convert_fusion.1 = bf16[256,6144]{1,0:T(8,128)(2,1)} fusion(bf16[128,6144]{1,0:T(8,128)(2,1)} %param.8, f32[128,256]{1,0:T(8,128)S(1)} %convert_reduce_fusion), kind=kOutput, calls=%fused_computation.1 | convolution fusion | flops 404258816 | bytes 4849664 | tf_op jit(solution)/shard_map/dot_general | solution.py:39
  24.6 33.4 %all-to-all-done.2 = bf16[8,32,6144]{2,1,0:T(8,128)(2,1)} async-done(((bf16[8,32,6144]{2,1,0:T(8,128)(2,1)}), bf16[8,32,6144]{2,1,0:T(8,128)(2,1)}, u32[]{:S(2)}, u32[]{:S(2)}) %all-to-all-start.2) | async-done | bytes 3145760 | tf_op jit(solution)/shard_map/all_to_all | solution.py:49
  58.0 5.3 %all-to-all-start.1 = ((bf16[8,32,6144]{2,1,0:T(8,128)(2,1)}), bf16[8,32,6144]{2,1,0:T(8,128)(2,1)}, u32[]{:S(2)}, u32[]{:S(2)}) async-start(bf16[8,32,6144]{2,1,0:T(8,128)(2,1)} %bitcast.50), calls=%async_computation.1 | async-start | bytes 6291456 | tf_op jit(solution)/shard_map/all_to_all | solution.py:50
  63.4 2.7 fusion.28
  66.1 3.1 fusion.5
  69.2 31.7 %all-to-all-done.1 = bf16[8,32,6144]{2,1,0:T(8,128)(2,1)} async-done(((bf16[8,32,6144]{2,1,0:T(8,128)(2,1)}), bf16[8,32,6144]{2,1,0:T(8,128)(2,1)}, u32[]{:S(2)}, u32[]{:S(2)}) %all-to-all-start.1) | async-done | bytes 3145760 | tf_op jit(solution)/shard_map/all_to_all | solution.py:50
  100.9 3.8 %fusion.12 = (f32[256]{0:T(256)S(1)}, f32[256,168]{0,1:T(8,128)S(1)}) fusion(f32[256,168]{0,1:T(8,128)S(1)} %fusion.5, bf16[256,6144]{1,0:T(8,128)(2,1)} %bitcast.3, bf16[1,168,6144]{2,1,0:T(8,128)(2,1)} %param.11), kind=kOutput, calls=%fused_computation.23 | convolution fusion | flops 528826112 | bytes 5555200 | tf_op jit(solution)/shard_map/dot_general | solution.py:8
  104.7 56.3 %psum.14 = f32[8,1,32]{2,1,0:T(1,128)} all-reduce(f32[8,1,32]{2,1,0:T(1,128)S(1)} %all_to_all.26), channel_id=1, replica_groups=mesh['fsdp'=32,'ep'=8] {'fsdp'}, use_global_device_ids=true, to_apply=%region_4.5 | all-reduce | flops 256 | bytes 2048 | tf_op jit(solution)/shard_map/psum | solution.py:77
  161.0 5.1 %all-to-all-start.4 = ((f32[8,1,32]{2,1,0:T(1,128)}), f32[8,1,32]{2,1,0:T(1,128)S(1)}, u32[]{:S(2)}, u32[]{:S(2)}) async-start(f32[8,1,32]{2,1,0:T(1,128)} %psum.14), calls=%async_computation.5 | async-start | bytes 8192 | tf_op jit(solution)/shard_map/all_to_all | solution.py:86
  166.1 6.4 %all-to-all-done.4 = f32[8,1,32]{2,1,0:T(1,128)S(1)} async-done(((f32[8,1,32]{2,1,0:T(1,128)}), f32[8,1,32]{2,1,0:T(1,128)S(1)}, u32[]{:S(2)}, u32[]{:S(2)}) %all-to-all-start.4) | async-done | bytes 1056 | tf_op jit(solution)/shard_map/all_to_all | solution.py:86
  174.4 8.9 %all_to_all.34 = bf16[8,1,32]{2,1,0:T(2,128)(2,1)S(1)} all-to-all(bf16[8,1,32]{2,1,0:T(2,128)(2,1)S(1)} %all_to_all.28), channel_id=1, replica_groups=mesh['fsdp'=32,'ep'=8] {'ep'}, dimensions={0} | all-to-all | bytes 1024 | tf_op jit(solution)/shard_map/all_to_all | solution.py:51
  183.5 4.0 %fusion.3 = f32[256,6144]{0,1:T(8,128)} fusion(bf16[256,168]{0,1:T(8,128)(2,1)S(1)} %multiply_convert_fusion.1, bf16[1,6144,168]{1,2,0:T(8,128)(2,1)S(1)} %copy-done), kind=kOutput, calls=%fused_computation.8 | convolution fusion | flops 528482304 | bytes 8441856 | tf_op jit(solution)/shard_map/dot_general | solution.py:8
  187.6 2.8 fusion.2
  190.4 3.9 %fusion.1 = bf16[1,168,6144]{2,1,0:T(8,128)(2,1)} fusion(bf16[256,6144]{1,0:T(8,128)(2,1)} %bitcast.3, f32[256]{0:T(256)S(1)} %reshape.60, f32[256,168]{0,1:T(8,128)S(1)} %fusion.5), kind=kOutput, calls=%fused_computation.5 | convolution fusion | flops 529858560 | bytes 5383168 | tf_op jit(solution)/shard_map/dot_general | solution.py:69
  194.3 3.9 %fusion = bf16[1,6144,168]{1,2,0:T(8,128)(2,1)} fusion(bf16[256,6144]{1,0:T(8,128)(2,1)} %bitcast.6, bf16[256,168]{0,1:T(8,128)(2,1)S(1)} %multiply_convert_fusion.1), kind=kOutput, calls=%fused_computation.4 | convolution fusion | flops 529514496 | bytes 5296128 | tf_op jit(solution)/shard_map/dot_general | solution.py:72
  198.2 110.3 %reduce-scatter.2.cloned.1.call-done = f32[256,192]{0,1:T(8,128)} async-done(((f32[256,6144]{0,1:T(8,128)}), f32[256,192]{0,1:T(8,128)}) %reduce-scatter.2.cloned.1.call-update) | async-done | bytes 196624 | tf_op jit(solution)/shard_map/reduce_scatter | solution.py:76
  308.5 1.8 copy.24
  310.3 6.0 %all-to-all-start.3 = ((f32[8,32,192]{2,1,0:T(8,128)}), f32[8,32,192]{2,1,0:T(8,128)S(1)}, u32[]{:S(2)}, u32[]{:S(2)}) async-start(f32[8,32,192]{2,1,0:T(8,128)} %bitcast.8), calls=%async_computation.4 | async-start | bytes 524288 | tf_op jit(solution)/shard_map/all_to_all | solution.py:79
  316.3 1.6 convert_multiply_fusion.2
  317.9 6.0 %all-to-all-done.3 = f32[8,32,192]{2,1,0:T(8,128)S(1)} async-done(((f32[8,32,192]{2,1,0:T(8,128)}), f32[8,32,192]{2,1,0:T(8,128)S(1)}, u32[]{:S(2)}, u32[]{:S(2)}) %all-to-all-start.3) | async-done | bytes 196640 | tf_op jit(solution)/shard_map/all_to_all | solution.py:79
  324.5 1.1 fusion.9
  (28 shorter events, 3.0 us)
Async XLA Ops:
  8.0 58.1 %copy-start = (bf16[1,6144,168]{1,2,0:T(8,128)(2,1)S(1)}, bf16[1,6144,168]{1,2,0:T(8,128)(2,1)}, u32[]{:S(2)}) copy-start(bf16[1,6144,168]{1,2,0:T(8,128)(2,1)} %param.10) | copy-start | bytes 6193156
  13.0 45.0 %all-to-all-start.2 = ((bf16[8,32,6144]{2,1,0:T(8,128)(2,1)}), bf16[8,32,6144]{2,1,0:T(8,128)(2,1)}, u32[]{:S(2)}, u32[]{:S(2)}) async-start(bf16[8,32,6144]{2,1,0:T(8,128)(2,1)} %bitcast.51), calls=%async_computation.2 | async-start | bytes 6291456 | tf_op jit(solution)/shard_map/all_to_all | solution.py:49
  58.0 5.3 %copy-start.1 = (f32[6144,8]{0,1:T(8,128)S(1)}, f32[6144,8]{0,1:T(8,128)}, u32[]{:S(2)}) copy-start(f32[6144,8]{0,1:T(8,128)} %param.9) | copy-start | bytes 589828
  58.0 42.9 %all-to-all-start.1 = ((bf16[8,32,6144]{2,1,0:T(8,128)(2,1)}), bf16[8,32,6144]{2,1,0:T(8,128)(2,1)}, u32[]{:S(2)}, u32[]{:S(2)}) async-start(bf16[8,32,6144]{2,1,0:T(8,128)(2,1)} %bitcast.50), calls=%async_computation.1 | async-start | bytes 6291456 | tf_op jit(solution)/shard_map/all_to_all | solution.py:50
  100.9 65.2 %copy-start.2 = (s32[128,2]{0,1:T(2,128)S(1)}, s32[128,2]{0,1:T(2,128)}, u32[]{:S(2)}) copy-start(s32[128,2]{0,1:T(2,128)} %param.12) | copy-start | bytes 3076
  161.0 11.5 %all-to-all-start.4 = ((f32[8,1,32]{2,1,0:T(1,128)}), f32[8,1,32]{2,1,0:T(1,128)S(1)}, u32[]{:S(2)}, u32[]{:S(2)}) async-start(f32[8,1,32]{2,1,0:T(1,128)} %psum.14), calls=%async_computation.5 | async-start | bytes 8192 | tf_op jit(solution)/shard_map/all_to_all | solution.py:86
  166.1 142.4 %reduce-scatter.2.cloned.1.call-start = ((), (), s32[]{:S(2)}) async-start(), calls=%async_computation.6 | async-start | bytes 6488064 | tf_op jit(solution)/shard_map/reduce_scatter | solution.py:76
  187.5 128.8 %all-reduce.2.cloned.1.call-start = ((), (), s32[]{:S(2)}) async-start(), calls=%async_computation.7 | async-start | bytes 196608 | tf_op jit(solution)/shard_map/psum | solution.py:102
  310.3 13.6 %all-to-all-start.3 = ((f32[8,32,192]{2,1,0:T(8,128)}), f32[8,32,192]{2,1,0:T(8,128)S(1)}, u32[]{:S(2)}, u32[]{:S(2)}) async-start(f32[8,32,192]{2,1,0:T(8,128)} %bitcast.8), calls=%async_computation.4 | async-start | bytes 524288 | tf_op jit(solution)/shard_map/all_to_all | solution.py:79
Sparse Core Ops, SparseCore 0:
  187.6 120.8 reduce-scatter.1
Sparse Core Ops, SparseCore 1:
  191.2 78.9 all-reduce.1
where the time goes:
time: 336 us; the launch traced here: 333 us
  waiting for transfers between devices  188 us (56%)
  blocking collectives  65.1 us (19%)
  matrix products  34.5 us (10%)
  starting transfers between devices  24 us (7%)
  between operations  15.6 us (5%)
  other arithmetic  3.42 us (1%)
    reduce_scatter x1, waiting for transfers between devices, per_device(): lax.psum_scatter(row_partial, 'fsdp', scatter_dimension=1, tiled=True)  110 us
    psum x1, blocking collectives, per_device(): own_scores = lax.psum(row_score, 'fsdp')  56.3 us
    all_to_all x1, waiting for transfers between devices, per_device(): lax.all_to_all(send_x, 'ep', split_axis=0, concat_axis=0, tiled=True)  33.4 us
    all_to_all x1, waiting for transfers between devices, per_device(): lax.all_to_all(send_dy, 'ep', split_axis=0, concat_axis=0, tiled=True)  31.7 us
    all_to_all x1, blocking collectives, per_device(): lax.all_to_all(send_gate, 'ep', split_axis=0, concat_axis=0, tiled=True)  8.87 us
    dot_general x2, matrix products, contract_last(): lax.dot_general(left, right, (((1,), (1,)), ((), ())), preferred_element_...  7.76 us
    all_to_all x1, starting transfers between devices, per_device(): lax.all_to_all(send_x, 'ep', split_axis=0, concat_axis=0, tiled=True)  7.48 us
  transfers between devices with their start and end apart: 6, of which 5 were waited for; matrix products, arithmetic and copies ran while one was open for 7% of the time, Pallas kernels for 0%

commit v1 on v0

v1 whole, which is shorter than its diff:
```python
import jax
import jax.numpy as jnp
from jax import lax
from jax.sharding import PartitionSpec as P

F32 = jnp.float32
BF16 = jnp.bfloat16
Z = 8
EP = 8


def fsdp_pairs(move):
    pairs = []
    for lo in range(2):
        for z in range(Z):
            for core in range(2):
                a, b, c = move(lo, z, core)
                pairs.append(((lo * Z + z) * 2 + core, ((a % 2) * Z + b % Z) * 2 + c % 2))
    return pairs


TO_CORE = fsdp_pairs(lambda lo, z, core: (lo, z, core + 1))
TO_UP = fsdp_pairs(lambda lo, z, core: (lo, z + 1, core))
TO_DOWN = fsdp_pairs(lambda lo, z, core: (lo, z - 1, core))
TO_SIDE = fsdp_pairs(lambda lo, z, core: (lo + 1, z, core))
TO_FLIP = {k: fsdp_pairs(lambda lo, z, core, k=k: (lo, z ^ k, core)) for k in (1, 2, 4)}
TO_EXPERT = {r: [(e, e ^ r) for e in range(EP)] for r in range(1, EP)}


def send(array, pairs):
    return lax.ppermute(array, "fsdp", pairs)


def send_ep(array, r):
    return lax.ppermute(array, "ep", TO_EXPERT[r])


def dot(left, right, dims):
    return lax.dot_general(left, right, (dims, ((), ())), preferred_element_type=F32)


def split3(array):
    high = lax.reduce_precision(array, 8, 7)
    rest = array - high
    mid = lax.reduce_precision(rest, 8, 7)
    low = rest - mid
    return high.astype(BF16), mid.astype(BF16), low.astype(BF16)


def columns(array, start, size):
    return lax.dynamic_slice_in_dim(array, start, size, 1)


def per_device(tokens, out_grad, router_weight, expert_in, expert_out, choices, slots):
    tok_rows, width = tokens.shape
    experts = router_weight.shape[1]
    capacity = max(2, 2 * tok_rows // experts)
    half = capacity // 2
    rows = experts * half
    fsdp_index = lax.axis_index("fsdp")
    me = lax.axis_index("ep")
    core = fsdp_index % 2
    z = (fsdp_index // 2) % Z
    lo = fsdp_index // (2 * Z)
    shard = width // Z
    seg = width // (2 * Z)
    own_cols = width // (4 * Z)

    w_in = expert_in[0].T
    w_out = expert_out[0]

    key = ((slots // half) ^ core) * rows + (choices ^ me) * half + slots % half
    key = jnp.where(slots >= 0, key, -1)
    places = key[:, :, None] == jnp.arange(2 * rows, dtype=jnp.int32)
    spread = (places[:, 0] | places[:, 1])[:, :rows].astype(BF16)

    picked = jnp.concatenate(
        [columns(out_grad, ((z + k) % Z) * shard, shard) for k in (5, 0, 3)], axis=1
    )
    send_dy = dot(spread, picked, ((0,), (0,))).astype(BF16)
    got_dy = [send_dy[:half]] + [
        send_ep(send_dy[r * half : (r + 1) * half], r) for r in range(1, experts)
    ]
    dy3 = jnp.concatenate(got_dy, axis=0)

    parts = split3(router_weight)
    logits = dot(tokens, jnp.concatenate(parts, axis=1), ((1,), (0,)))
    logits = (logits[:, :experts] + logits[:, experts : 2 * experts]) + logits[:, 2 * experts :]
    chosen_hot = (choices[:, :, None] == jnp.arange(experts, dtype=jnp.int32)).astype(F32)
    chosen = jnp.sum(chosen_hot * logits[:, None, :], axis=2)
    first_gate = 1.0 / (1.0 + jnp.exp(chosen[:, 1] - chosen[:, 0]))
    second_gate = 1.0 / (1.0 + jnp.exp(chosen[:, 0] - chosen[:, 1]))
    gate_pair = jnp.stack([first_gate, second_gate], axis=1).astype(BF16).astype(F32)
    near_hot = (choices ^ me)[:, :, None] == jnp.arange(128, dtype=jnp.int32)
    gate_cols = jnp.sum(jnp.where(near_hot, gate_pair[:, :, None], 0.0), axis=1).astype(BF16)

    send_x = dot(
        spread, jnp.concatenate([tokens, gate_cols], axis=1), ((0,), (0,))
    ).astype(BF16)
    got_x = [send_x[:half]] + [
        send_ep(send_x[r * half : (r + 1) * half], r) for r in range(1, experts)
    ]
    x_mine = jnp.concatenate(got_x, axis=0)

    cut = seg
    from_up = send(dy3[:, : 5 * cut], TO_DOWN)
    from_down = send(dy3[:, cut:], TO_UP)
    dy_mine = jnp.concatenate(
        [
            dy3[:, 2 * cut : 4 * cut],
            from_up[:, 2 * cut : 4 * cut],
            from_down[:, 3 * cut :],
            dy3[:, 4 * cut :],
            from_up[:, 4 * cut :],
            from_down[:, :cut],
            dy3[:, : 2 * cut],
            from_up[:, : 2 * cut],
            from_down[:, cut : 3 * cut],
        ],
        axis=1,
    )
    x_other = send(x_mine, TO_CORE)
    dy_other = send(dy_mine, TO_CORE)
    rows_x = jnp.concatenate([x_mine, x_other], axis=0)
    rows_dy = jnp.concatenate([dy_mine, dy_other], axis=0)
    w_out_near = jnp.concatenate(
        [columns(w_out, ((z + k) % Z) * shard, shard) for k in range(Z)], axis=1
    )
    block = (jnp.arange(2 * rows, dtype=jnp.int32) % rows) // half
    gate = jnp.sum(
        jnp.where(
            block[:, None] == jnp.arange(128, dtype=jnp.int32)[None, :],
            rows_x[:, width:].astype(F32),
            0.0,
        ),
        axis=1,
        keepdims=True,
    )
    rows_x = rows_x[:, :width]

    pre = dot(rows_x, w_in, ((1,), (1,)))
    back = dot(rows_dy, w_out_near, ((1,), (1,)))
    sig = jax.nn.sigmoid(pre)
    hidden = (pre * sig).astype(BF16)
    hid_wide = hidden.astype(F32)
    score = jnp.sum(hid_wide * back, axis=1)
    weighted = (hid_wide * gate).astype(BF16)
    act_grad = (gate * back * sig * (1.0 + pre * (1.0 - sig))).astype(BF16)

    part_other = dot(act_grad[rows:], w_in, ((1,), (0,))).astype(BF16)
    from_core = send(part_other, TO_CORE)
    part = (dot(act_grad[:rows], w_in, ((1,), (0,))) + from_core.astype(F32)).astype(BF16)

    def piece(k):
        at = (z + k) % Z
        return jnp.concatenate(
            [columns(part, ((lo ^ d) * Z + at) * seg, seg) for d in range(2)], axis=1
        ).astype(F32)

    up = send(piece(4).astype(BF16), TO_UP)
    down = send(piece(5).astype(BF16), TO_DOWN)
    up = send((up.astype(F32) + piece(3)).astype(BF16), TO_UP)
    down = send((down.astype(F32) + piece(6)).astype(BF16), TO_DOWN)
    up = send((up.astype(F32) + piece(2)).astype(BF16), TO_UP)
    down = send((down.astype(F32) + piece(7)).astype(BF16), TO_DOWN)
    up = send((up.astype(F32) + piece(1)).astype(BF16), TO_UP)
    total = up.astype(F32) + down.astype(F32) + piece(0)
    side = send(total[:, seg:].astype(BF16), TO_SIDE)
    own = (total[:, :seg] + side.astype(F32)).astype(BF16)
    returned = jnp.concatenate(
        [own[:half]]
        + [send_ep(own[r * half : (r + 1) * half], r) for r in range(1, experts)],
        axis=0,
    )
    merged = dot(spread, returned, ((1,), (0,)))
    low_cols, high_cols = merged[:, :own_cols], merged[:, own_cols:]
    keep = jnp.where(core == 0, low_cols, high_cols)
    give = jnp.where(core == 0, high_cols, low_cols)
    expert_grad = keep + send(give.astype(BF16), TO_CORE).astype(F32)

    pair = score.reshape(2, rows)
    pair = pair + send(pair, TO_CORE)[::-1]
    pair = pair + send(pair, TO_FLIP[1])
    pair = pair + send(pair, TO_FLIP[2])
    pair = pair + send(pair, TO_FLIP[4])
    pair = pair + send(pair, TO_SIDE)
    back_scores = jnp.concatenate(
        [pair[:, :half]]
        + [send_ep(pair, r)[:, r * half : (r + 1) * half] for r in range(1, experts)],
        axis=1,
    ).reshape(2 * rows)
    taken = jnp.sum(jnp.where(places, back_scores[None, None, :], 0.0), axis=2)
    change = first_gate * second_gate * (taken[:, 0] - taken[:, 1])
    logit_grad = change[:, None] * (chosen_hot[:, 0, :] - chosen_hot[:, 1, :])

    router_part = dot(jnp.concatenate(split3(logit_grad), axis=1), tokens, ((0,), (0,)))
    router_part = (router_part[:experts] + router_part[experts : 2 * experts]) + router_part[
        2 * experts :
    ]
    chunk = width // EP
    mine = columns(router_part, me * chunk, chunk)
    for r in range(1, EP):
        mine = mine + send_ep(columns(router_part, (me ^ r) * chunk, chunk), r)
    mine = mine / (tok_rows * EP)
    gathered = [mine] + [send_ep(mine, r) for r in range(1, EP)]
    grad_router = jnp.zeros((experts, width), F32)
    for r in range(EP):
        grad_router = lax.dynamic_update_slice_in_dim(
            grad_router, gathered[r], (me ^ r) * chunk, 1
        )

    grad_out_near = dot(weighted, rows_dy, ((0,), (0,))).astype(BF16)
    grad_out = jnp.concatenate(
        [columns(grad_out_near, ((k - z) % Z) * shard, shard) for k in range(Z)], axis=1
    )
    grad_in = dot(act_grad, rows_x, ((0,), (0,))).astype(BF16)

    router_rows = lax.dynamic_slice_in_dim(router_weight, fsdp_index * own_cols, own_cols, 0)
    grad_tokens = (
        expert_grad + jnp.dot(logit_grad, router_rows.T, precision=lax.Precision.HIGHEST)
    ).astype(BF16)
    return grad_tokens, grad_in.T[None], grad_out[None], grad_router.T


def solution(mesh):
    placed = (
        P("ep", None),
        P("ep", None),
        P(),
        P("ep", None, "fsdp"),
        P("ep", "fsdp", None),
        P("ep", None),
        P("ep", None),
    )
    return jax.shard_map(
        per_device,
        mesh=mesh,
        in_specs=placed,
        out_specs=(P("ep", "fsdp"), P("ep", None, "fsdp"), P("ep", "fsdp", None), P()),
        check_vma=False,
    )
```

time: 336 us -> 278 us (0.83)
  waiting for transfers between devices: 188 us -> 65.5 us
  starting transfers between devices: 24 us -> 143 us
  blocking collectives: 65.1 us -> 0 us
  local copies, waits for them, and re-layouts: 2.61 us -> 39.8 us
  matrix products: 34.5 us -> 19.6 us
  between operations: 15.6 us -> 1.59 us
    ppermute x0 -> x61, starting transfers between devices: none -> 143 us  [the longest x42 88.2 us: send_ep(): return lax.ppermute(array, 'ep', TO_EXPERT[r])]
    reduce_scatter x1 -> x0, waiting for transfers between devices: 110 us -> none  [per_device(): lax.psum_scatter(row_partial, 'fsdp', scatter_dimension=1, tiled=True)]
    all_to_all x4 -> x0, waiting for transfers between devices: 77.4 us -> none  [the longest x1 33.4 us: per_device(): lax.all_to_all(send_x, 'ep', split_axis=0, concat_axis=0, tiled=True)]
    ppermute x0 -> x61, waiting for transfers between devices: none -> 65.5 us  [the longest x19 36.2 us: send(): return lax.ppermute(array, 'fsdp', pairs)]
    psum x1 -> x0, blocking collectives: 56.3 us -> none  [per_device(): own_scores = lax.psum(row_score, 'fsdp')]
    unnamed x6 -> x60, local copies, waits for them, and re-layouts: 0.02 us -> 31.3 us
    all_to_all x4 -> x0, starting transfers between devices: 23.9 us -> none  [the longest x1 7.48 us: per_device(): lax.all_to_all(send_x, 'ep', split_axis=0, concat_axis=0, tiled=True)]
    dot_general x13 -> x12, matrix products: 34.5 us -> 19.6 us  [the longest x11 18.5 us: dot(): lax.dot_general(left, right, (dims, ((), ())), preferred_element_type=F32)]
  transfers between devices with their start and end apart: 6 -> 61, of which waited for: 5 -> 22; matrix products, arithmetic and copies ran while one was open for 7% -> 18% of each run, Pallas kernels for 0% -> 0%
where the time goes in v1:
time: 278 us; the launch traced here: 273 us
  starting transfers between devices  143 us (51%)
  waiting for transfers between devices  65.5 us (24%)
  local copies, waits for them, and re-layouts  39.8 us (14%)
  matrix products  19.6 us (7%)
  other arithmetic  3.38 us (1%)
    ppermute x42, starting transfers between devices, send_ep(): return lax.ppermute(array, 'ep', TO_EXPERT[r])  88.2 us
    ppermute x19, starting transfers between devices, send(): return lax.ppermute(array, 'fsdp', pairs)  54.6 us
    ppermute x19, waiting for transfers between devices, send(): return lax.ppermute(array, 'fsdp', pairs)  36.2 us
    unnamed x60, local copies, waits for them, and re-layouts  31.3 us
    ppermute x42, waiting for transfers between devices, send_ep(): return lax.ppermute(array, 'ep', TO_EXPERT[r])  29.3 us
    dot_general x11, matrix products, dot(): lax.dot_general(left, right, (dims, ((), ())), preferred_element_type=F32)  18.5 us
  transfers between devices with their start and end apart: 61, of which 22 were waited for; matrix products, arithmetic and copies ran while one was open for 18% of the time, Pallas kernels for 0%

profile of v1, /device:TPU:1, one launch (start us, length us, event | category | flops | bytes accessed | tf_op | source)
XLA Modules:
  0.0 272.6 jit_solution(10241684176288895057)
XLA Ops:
  30.7 3.8 %collective-permute-start.9 = (bf16[16,2304]{1,0:T(8,128)(2,1)}, bf16[16,2304]{1,0:T(8,128)(2,1)S(1)}, u32[]{:S(2)}, u32[]{:S(2)}) collective-permute-start(bf16[16,2304]{1,0:T(8,128)(2,1)} %get-tuple-element.65), channel_id=1, source_target_pairs={{0,2},{1,3},{2,0},{3,1},{4,6},{5,7},{6,4},{7,5},{8,10},{9,11},{10,... | collective-permute-start | bytes 221192 | tf_op jit(solution)/shard_map/ppermute | solution.py:35
  41.3 4.7 %collective-permute-done.11 = bf16[16,2304]{1,0:T(8,128)(2,1)S(1)} collective-permute-done((bf16[16,2304]{1,0:T(8,128)(2,1)}, bf16[16,2304]{1,0:T(8,128)(2,1)S(1)}, u32[]{:S(2)}, u32[]{:S(2)}) %collective-permute-start.11) | collective-permute-done | bytes 73760 | tf_op jit(solution)/shard_map/ppermute | solution.py:35
  46.7 5.1 %collective-permute-done.12 = bf16[16,2304]{1,0:T(8,128)(2,1)S(1)} collective-permute-done((bf16[16,2304]{1,0:T(8,128)(2,1)}, bf16[16,2304]{1,0:T(8,128)(2,1)S(1)}, u32[]{:S(2)}, u32[]{:S(2)}) %collective-permute-start.12) | collective-permute-done | bytes 73760 | tf_op jit(solution)/shard_map/ppermute | solution.py:35
  54.1 5.2 %collective-permute-done.13 = bf16[16,2304]{1,0:T(8,128)(2,1)S(1)} collective-permute-done((bf16[16,2304]{1,0:T(8,128)(2,1)}, bf16[16,2304]{1,0:T(8,128)(2,1)S(1)}, u32[]{:S(2)}, u32[]{:S(2)}) %collective-permute-start.13) | collective-permute-done | bytes 73760 | tf_op jit(solution)/shard_map/ppermute | solution.py:35
  61.4 5.0 %collective-permute-done.14 = bf16[16,2304]{1,0:T(8,128)(2,1)S(1)} collective-permute-done((bf16[16,2304]{1,0:T(8,128)(2,1)}, bf16[16,2304]{1,0:T(8,128)(2,1)S(1)}, u32[]{:S(2)}, u32[]{:S(2)}) %collective-permute-start.14) | collective-permute-done | bytes 73760 | tf_op jit(solution)/shard_map/ppermute | solution.py:35
  66.5 6.4 %collective-permute-start.5 = (bf16[16,6272]{1,0:T(8,128)(2,1)S(1)}, bf16[16,6272]{1,0:T(8,128)(2,1)S(1)}, u32[]{:S(2)}, u32[]{:S(2)}) collective-permute-start(bf16[16,6272]{1,0:T(8,128)(2,1)S(1)} %copy-done.2), channel_id=1, source_target_pairs={{0,6},{1,7},{2,4},{3,5},{4,2},{5,3},{6,0},{7,1},{8,14},{9,15},{10,... | collective-permute-start | bytes 602120 | tf_op jit(solution)/shard_map/ppermute | solution.py:35
  76.2 4.5 %collective-permute-start.15 = (bf16[128,1920]{1,0:T(8,128)(2,1)S(1)}, bf16[128,1920]{1,0:T(8,128)(2,1)S(1)}, u32[]{:S(2)}, u32[]{:S(2)}) collective-permute-start(bf16[128,1920]{1,0:T(8,128)(2,1)S(1)} %get-tuple-element.59), channel_id=1, source_target_pairs={{0,112},{8,120},{16,0},{24,8},{32,16},{40,24},{48,32},{56,40},{64,... | collective-permute-start | bytes 1474568 | tf_op jit(solution)/shard_map/ppermute | solution.py:31
  84.6 10.5 %collective-permute-start.7 = (bf16[128,6272]{1,0:T(8,128)(2,1)S(1)}, bf16[128,6272]{1,0:T(8,128)(2,1)S(1)}, u32[]{:S(2)}, u32[]{:S(2)}) collective-permute-start(bf16[128,6272]{1,0:T(8,128)(2,1)S(1)} %get-tuple-element.70), channel_id=1, source_target_pairs={{0,8},{8,0},{16,24},{24,16},{32,40},{40,32},{48,56},{56,48},{64,72... | collective-permute-start | bytes 4816904 | tf_op jit(solution)/shard_map/ppermute | solution.py:31
  95.3 7.2 %collective-permute-start.17 = (bf16[128,6144]{1,0:T(8,128)(2,1)S(1)}, bf16[128,6144]{1,0:T(8,128)(2,1)S(1)}, u32[]{:S(2)}, u32[]{:S(2)}) collective-permute-start(bf16[128,6144]{1,0:T(8,128)(2,1)S(1)} %slice_dynamic-update-slice_fusion), channel_id=1, source_target_pairs={{0,8},{8,0},{16,24},{24,16},{32,40},{40,32},{48,56},{56,48},{64,72... | collective-permute-start | bytes 4718600 | tf_op jit(solution)/shard_map/ppermute | solution.py:31
  130.9 3.5 %collective-permute-start.41 = (f32[2,128]{1,0:T(2,128)S(1)}, f32[2,128]{1,0:T(2,128)S(1)}, u32[]{:S(2)}, u32[]{:S(2)}) collective-permute-start(f32[2,128]{1,0:T(2,128)S(1)} %add.486), channel_id=1, source_target_pairs={{0,2},{1,3},{2,0},{3,1},{4,6},{5,7},{6,4},{7,5},{8,10},{9,11},{10,... | collective-permute-start | bytes 3080 | tf_op jit(solution)/shard_map/ppermute | solution.py:35
  139.4 6.3 %collective-permute-start.45 = (f32[2,128]{1,0:T(2,128)S(1)}, f32[2,128]{1,0:T(2,128)S(1)}, u32[]{:S(2)}, u32[]{:S(2)}) collective-permute-start(f32[2,128]{1,0:T(2,128)S(1)} %add.486), channel_id=1, source_target_pairs={{0,6},{1,7},{2,4},{3,5},{4,2},{5,3},{6,0},{7,1},{8,14},{9,15},{10,... | collective-permute-start | bytes 3080 | tf_op jit(solution)/shard_map/ppermute | solution.py:35
  145.6 8.6 %collective-permute-start.46 = (f32[2,128]{1,0:T(2,128)S(1)}, f32[2,128]{1,0:T(2,128)S(1)}, u32[]{:S(2)}, u32[]{:S(2)}) collective-permute-start(f32[2,128]{1,0:T(2,128)S(1)} %add.486), channel_id=1, source_target_pairs={{0,7},{1,6},{2,5},{3,4},{4,3},{5,2},{6,1},{7,0},{8,15},{9,14},{10,... | collective-permute-start | bytes 3080 | tf_op jit(solution)/shard_map/ppermute | solution.py:35
  156.0 6.5 %collective-permute-start.18 = (bf16[128,6144]{1,0:T(8,128)(2,1)}, bf16[128,6144]{1,0:T(8,128)(2,1)}, u32[]{:S(2)}, u32[]{:S(2)}) collective-permute-start(bf16[128,6144]{1,0:T(8,128)(2,1)} %convolution_convert_fusion.3), channel_id=1, source_target_pairs={{0,8},{8,0},{16,24},{24,16},{32,40},{40,32},{48,56},{56,48},{64,72... | collective-permute-start | bytes 4718600 | tf_op jit(solution)/shard_map/ppermute | solution.py:31
  165.0 5.4 %collective-permute-start.53 = (f32[8,768]{1,0:T(8,128)S(1)}, f32[8,768]{1,0:T(8,128)S(1)}, u32[]{:S(2)}, u32[]{:S(2)}) collective-permute-start(f32[8,768]{1,0:T(8,128)S(1)} %get-tuple-element.85), channel_id=1, source_target_pairs={{0,7},{1,6},{2,5},{3,4},{4,3},{5,2},{6,1},{7,0},{8,15},{9,14},{10,... | collective-permute-start | bytes 73736 | tf_op jit(solution)/shard_map/ppermute | solution.py:35
  190.1 4.4 %collective-permute-start.59 = (f32[8,768]{1,0:T(8,128)S(1)}, f32[8,768]{1,0:T(8,128)S(1)}, u32[]{:S(2)}, u32[]{:S(2)}) collective-permute-start(f32[8,768]{1,0:T(8,128)S(1)} %get-tuple-element.21), channel_id=1, source_target_pairs={{0,6},{1,7},{2,4},{3,5},{4,2},{5,3},{6,0},{7,1},{8,14},{9,15},{10,... | collective-permute-start | bytes 73736 | tf_op jit(solution)/shard_map/ppermute | solution.py:35
  196.9 6.0 %collective-permute-done.19 = bf16[128,768]{1,0:T(8,128)(2,1)S(1)} collective-permute-done((bf16[128,768]{1,0:T(8,128)(2,1)S(1)}, bf16[128,768]{1,0:T(8,128)(2,1)S(1)}, u32[]{:S(2)}, u32[]{:S(2)}) %collective-permute-start.19) | collective-permute-done | bytes 196640 | tf_op jit(solution)/shard_map/ppermute | solution.py:31
  203.0 4.8 %collective-permute-done.23 = bf16[128,768]{1,0:T(8,128)(2,1)S(1)} collective-permute-done((bf16[128,768]{1,0:T(8,128)(2,1)S(1)}, bf16[128,768]{1,0:T(8,128)(2,1)S(1)}, u32[]{:S(2)}, u32[]{:S(2)}) %collective-permute-start.23) | collective-permute-done | bytes 196640 | tf_op jit(solution)/shard_map/ppermute | solution.py:31
  207.8 5.7 %collective-permute-done.20 = bf16[128,768]{1,0:T(8,128)(2,1)S(1)} collective-permute-done((bf16[128,768]{1,0:T(8,128)(2,1)S(1)}, bf16[128,768]{1,0:T(8,128)(2,1)S(1)}, u32[]{:S(2)}, u32[]{:S(2)}) %collective-permute-start.20) | collective-permute-done | bytes 196640 | tf_op jit(solution)/shard_map/ppermute | solution.py:31
  213.8 4.4 %collective-permute-done.24 = bf16[128,768]{1,0:T(8,128)(2,1)S(1)} collective-permute-done((bf16[128,768]{1,0:T(8,128)(2,1)S(1)}, bf16[128,768]{1,0:T(8,128)(2,1)S(1)}, u32[]{:S(2)}, u32[]{:S(2)}) %collective-permute-start.24) | collective-permute-done | bytes 196640 | tf_op jit(solution)/shard_map/ppermute | solution.py:31
  218.2 5.7 %collective-permute-done.21 = bf16[128,768]{1,0:T(8,128)(2,1)S(1)} collective-permute-done((bf16[128,768]{1,0:T(8,128)(2,1)S(1)}, bf16[128,768]{1,0:T(8,128)(2,1)S(1)}, u32[]{:S(2)}, u32[]{:S(2)}) %collective-permute-start.21) | collective-permute-done | bytes 196640 | tf_op jit(solution)/shard_map/ppermute | solution.py:31
  237.8 3.3 %collective-permute-start.30 = (bf16[16,384]{1,0:T(8,128)(2,1)S(1)}, bf16[16,384]{1,0:T(8,128)(2,1)S(1)}, u32[]{:S(2)}, u32[]{:S(2)}) collective-permute-start(bf16[16,384]{1,0:T(8,128)(2,1)S(1)} %get-tuple-element.97), channel_id=1, source_target_pairs={{0,4},{1,5},{2,6},{3,7},{4,0},{5,1},{6,2},{7,3},{8,12},{9,13},{10,... | collective-permute-start | bytes 36872 | tf_op jit(solution)/shard_map/ppermute | solution.py:35
  241.1 3.6 %collective-permute-start.32 = (bf16[16,384]{1,0:T(8,128)(2,1)S(1)}, bf16[16,384]{1,0:T(8,128)(2,1)S(1)}, u32[]{:S(2)}, u32[]{:S(2)}) collective-permute-start(bf16[16,384]{1,0:T(8,128)(2,1)S(1)} %get-tuple-element.95), channel_id=1, source_target_pairs={{0,6},{1,7},{2,4},{3,5},{4,2},{5,3},{6,0},{7,1},{8,14},{9,15},{10,... | collective-permute-start | bytes 36872 | tf_op jit(solution)/shard_map/ppermute | solution.py:35
  247.6 3.3 %collective-permute-done.33 = bf16[16,384]{1,0:T(8,128)(2,1)S(1)} collective-permute-done((bf16[16,384]{1,0:T(8,128)(2,1)S(1)}, bf16[16,384]{1,0:T(8,128)(2,1)S(1)}, u32[]{:S(2)}, u32[]{:S(2)}) %collective-permute-start.33) | collective-permute-done | bytes 12320 | tf_op jit(solution)/shard_map/ppermute | solution.py:35
  251.3 19.4 %collective-permute-start.34 = (bf16[128,192]{1,0:T(8,128)(2,1)S(1)}, bf16[128,192]{1,0:T(8,128)(2,1)S(1)}, u32[]{:S(2)}, u32[]{:S(2)}) collective-permute-start(bf16[128,192]{1,0:T(8,128)(2,1)S(1)} %select_convert_fusion), channel_id=1, source_target_pairs={{0,8},{8,0},{16,24},{24,16},{32,40},{40,32},{48,56},{56,48},{64,72... | collective-permute-start | bytes 147464 | tf_op jit(solution)/shard_map/ppermute | solution.py:31
  (235 shorter events, 127.8 us)
Async XLA Ops:
  7.4 59.1 %collective-permute-start = (bf16[16,6272]{1,0:T(8,128)(2,1)}, bf16[16,6272]{1,0:T(8,128)(2,1)S(1)}, u32[]{:S(2)}, u32[]{:S(2)}) collective-permute-start(bf16[16,6272]{1,0:T(8,128)(2,1)} %get-tuple-element.38), channel_id=1, source_target_pairs={{0,1},{1,0},{2,3},{3,2},{4,5},{5,4},{6,7},{7,6},{8,9},{9,8},{10,11... | collective-permute-start | bytes 602120 | tf_op jit(solution)/shard_map/ppermute | solution.py:35
  9.6 64.1 %collective-permute-start.1 = (bf16[16,6272]{1,0:T(8,128)(2,1)}, bf16[16,6272]{1,0:T(8,128)(2,1)S(1)}, u32[]{:S(2)}, u32[]{:S(2)}) collective-permute-start(bf16[16,6272]{1,0:T(8,128)(2,1)} %get-tuple-element.37), channel_id=1, source_target_pairs={{0,2},{1,3},{2,0},{3,1},{4,6},{5,7},{6,4},{7,5},{8,10},{9,11},{10,... | collective-permute-start | bytes 602120 | tf_op jit(solution)/shard_map/ppermute | solution.py:35
  12.2 64.1 %collective-permute-start.2 = (bf16[16,6272]{1,0:T(8,128)(2,1)}, bf16[16,6272]{1,0:T(8,128)(2,1)S(1)}, u32[]{:S(2)}, u32[]{:S(2)}) collective-permute-start(bf16[16,6272]{1,0:T(8,128)(2,1)} %get-tuple-element.36), channel_id=1, source_target_pairs={{0,3},{1,2},{2,1},{3,0},{4,7},{5,6},{6,5},{7,4},{8,11},{9,10},{10,... | collective-permute-start | bytes 602120 | tf_op jit(solution)/shard_map/ppermute | solution.py:35
  12.2 69.3 %collective-permute-start.3 = (bf16[16,6272]{1,0:T(8,128)(2,1)}, bf16[16,6272]{1,0:T(8,128)(2,1)S(1)}, u32[]{:S(2)}, u32[]{:S(2)}) collective-permute-start(bf16[16,6272]{1,0:T(8,128)(2,1)} %get-tuple-element.35), channel_id=1, source_target_pairs={{0,4},{1,5},{2,6},{3,7},{4,0},{5,1},{6,2},{7,3},{8,12},{9,13},{10,... | collective-permute-start | bytes 602120 | tf_op jit(solution)/shard_map/ppermute | solution.py:35
  17.3 13.5 %collective-permute-start.8 = (bf16[16,2304]{1,0:T(8,128)(2,1)}, bf16[16,2304]{1,0:T(8,128)(2,1)}, u32[]{:S(2)}, u32[]{:S(2)}) collective-permute-start(bf16[16,2304]{1,0:T(8,128)(2,1)} %get-tuple-element.66), channel_id=1, source_target_pairs={{0,1},{1,0},{2,3},{3,2},{4,5},{5,4},{6,7},{7,6},{8,9},{9,8},{10,11... | collective-permute-start | bytes 221192 | tf_op jit(solution)/shard_map/ppermute | solution.py:35
  66.4 16.1 %collective-permute-start.4 = (bf16[16,6272]{1,0:T(8,128)(2,1)}, bf16[16,6272]{1,0:T(8,128)(2,1)S(1)}, u32[]{:S(2)}, u32[]{:S(2)}) collective-permute-start(bf16[16,6272]{1,0:T(8,128)(2,1)} %get-tuple-element.34), channel_id=1, source_target_pairs={{0,5},{1,4},{2,7},{3,6},{4,1},{5,0},{6,3},{7,2},{8,13},{9,12},{10,... | collective-permute-start | bytes 602120 | tf_op jit(solution)/shard_map/ppermute | solution.py:35
  66.5 16.6 %collective-permute-start.5 = (bf16[16,6272]{1,0:T(8,128)(2,1)S(1)}, bf16[16,6272]{1,0:T(8,128)(2,1)S(1)}, u32[]{:S(2)}, u32[]{:S(2)}) collective-permute-start(bf16[16,6272]{1,0:T(8,128)(2,1)S(1)} %copy-done.2), channel_id=1, source_target_pairs={{0,6},{1,7},{2,4},{3,5},{4,2},{5,3},{6,0},{7,1},{8,14},{9,15},{10,... | collective-permute-start | bytes 602120 | tf_op jit(solution)/shard_map/ppermute | solution.py:35
  76.2 18.9 %collective-permute-start.15 = (bf16[128,1920]{1,0:T(8,128)(2,1)S(1)}, bf16[128,1920]{1,0:T(8,128)(2,1)S(1)}, u32[]{:S(2)}, u32[]{:S(2)}) collective-permute-start(bf16[128,1920]{1,0:T(8,128)(2,1)S(1)} %get-tuple-element.59), channel_id=1, source_target_pairs={{0,112},{8,120},{16,0},{24,8},{32,16},{40,24},{48,32},{56,40},{64,... | collective-permute-start | bytes 1474568 | tf_op jit(solution)/shard_map/ppermute | solution.py:31
  81.5 13.7 %collective-permute-start.16 = (bf16[128,1920]{1,0:T(8,128)(2,1)S(1)}, bf16[128,1920]{1,0:T(8,128)(2,1)S(1)}, u32[]{:S(2)}, u32[]{:S(2)}) collective-permute-start(bf16[128,1920]{1,0:T(8,128)(2,1)S(1)} %get-tuple-element.58), channel_id=1, source_target_pairs={{0,16},{8,24},{16,32},{24,40},{32,48},{40,56},{48,64},{56,72},{64,... | collective-permute-start | bytes 1474568 | tf_op jit(solution)/shard_map/ppermute | solution.py:31
  84.6 18.0 %collective-permute-start.7 = (bf16[128,6272]{1,0:T(8,128)(2,1)S(1)}, bf16[128,6272]{1,0:T(8,128)(2,1)S(1)}, u32[]{:S(2)}, u32[]{:S(2)}) collective-permute-start(bf16[128,6272]{1,0:T(8,128)(2,1)S(1)} %get-tuple-element.70), channel_id=1, source_target_pairs={{0,8},{8,0},{16,24},{24,16},{32,40},{40,32},{48,56},{56,48},{64,72... | collective-permute-start | bytes 4816904 | tf_op jit(solution)/shard_map/ppermute | solution.py:31
  130.9 14.7 %collective-permute-start.41 = (f32[2,128]{1,0:T(2,128)S(1)}, f32[2,128]{1,0:T(2,128)S(1)}, u32[]{:S(2)}, u32[]{:S(2)}) collective-permute-start(f32[2,128]{1,0:T(2,128)S(1)} %add.486), channel_id=1, source_target_pairs={{0,2},{1,3},{2,0},{3,1},{4,6},{5,7},{6,4},{7,5},{8,10},{9,11},{10,... | collective-permute-start | bytes 3080 | tf_op jit(solution)/shard_map/ppermute | solution.py:35
  136.1 20.0 %collective-permute-start.42 = (f32[2,128]{1,0:T(2,128)S(1)}, f32[2,128]{1,0:T(2,128)S(1)}, u32[]{:S(2)}, u32[]{:S(2)}) collective-permute-start(f32[2,128]{1,0:T(2,128)S(1)} %add.486), channel_id=1, source_target_pairs={{0,3},{1,2},{2,1},{3,0},{4,7},{5,6},{6,5},{7,4},{8,11},{9,10},{10,... | collective-permute-start | bytes 3080 | tf_op jit(solution)/shard_map/ppermute | solution.py:35
  136.4 26.2 %collective-permute-start.43 = (f32[2,128]{1,0:T(2,128)S(1)}, f32[2,128]{1,0:T(2,128)S(1)}, u32[]{:S(2)}, u32[]{:S(2)}) collective-permute-start(f32[2,128]{1,0:T(2,128)S(1)} %add.486), channel_id=1, source_target_pairs={{0,4},{1,5},{2,6},{3,7},{4,0},{5,1},{6,2},{7,3},{8,12},{9,13},{10,... | collective-permute-start | bytes 3080 | tf_op jit(solution)/shard_map/ppermute | solution.py:35
  139.4 23.3 %collective-permute-start.44 = (f32[2,128]{1,0:T(2,128)S(1)}, f32[2,128]{1,0:T(2,128)S(1)}, u32[]{:S(2)}, u32[]{:S(2)}) collective-permute-start(f32[2,128]{1,0:T(2,128)S(1)} %add.486), channel_id=1, source_target_pairs={{0,5},{1,4},{2,7},{3,6},{4,1},{5,0},{6,3},{7,2},{8,13},{9,12},{10,... | collective-permute-start | bytes 3080 | tf_op jit(solution)/shard_map/ppermute | solution.py:35
  139.4 23.4 %collective-permute-start.45 = (f32[2,128]{1,0:T(2,128)S(1)}, f32[2,128]{1,0:T(2,128)S(1)}, u32[]{:S(2)}, u32[]{:S(2)}) collective-permute-start(f32[2,128]{1,0:T(2,128)S(1)} %add.486), channel_id=1, source_target_pairs={{0,6},{1,7},{2,4},{3,5},{4,2},{5,3},{6,0},{7,1},{8,14},{9,15},{10,... | collective-permute-start | bytes 3080 | tf_op jit(solution)/shard_map/ppermute | solution.py:35
  145.6 17.2 %collective-permute-start.46 = (f32[2,128]{1,0:T(2,128)S(1)}, f32[2,128]{1,0:T(2,128)S(1)}, u32[]{:S(2)}, u32[]{:S(2)}) collective-permute-start(f32[2,128]{1,0:T(2,128)S(1)} %add.486), channel_id=1, source_target_pairs={{0,7},{1,6},{2,5},{3,4},{4,3},{5,2},{6,1},{7,0},{8,15},{9,14},{10,... | collective-permute-start | bytes 3080 | tf_op jit(solution)/shard_map/ppermute | solution.py:35
  156.0 34.0 %collective-permute-start.18 = (bf16[128,6144]{1,0:T(8,128)(2,1)}, bf16[128,6144]{1,0:T(8,128)(2,1)}, u32[]{:S(2)}, u32[]{:S(2)}) collective-permute-start(bf16[128,6144]{1,0:T(8,128)(2,1)} %convolution_convert_fusion.3), channel_id=1, source_target_pairs={{0,8},{8,0},{16,24},{24,16},{32,40},{40,32},{48,56},{56,48},{64,72... | collective-permute-start | bytes 4718600 | tf_op jit(solution)/shard_map/ppermute | solution.py:31
  183.2 13.6 %collective-permute-start.55 = (f32[8,768]{1,0:T(8,128)S(1)}, f32[8,768]{1,0:T(8,128)S(1)}, u32[]{:S(2)}, u32[]{:S(2)}) collective-permute-start(f32[8,768]{1,0:T(8,128)S(1)} %get-tuple-element.21), channel_id=1, source_target_pairs={{0,2},{1,3},{2,0},{3,1},{4,6},{5,7},{6,4},{7,5},{8,10},{9,11},{10,... | collective-permute-start | bytes 73736 | tf_op jit(solution)/shard_map/ppermute | solution.py:35
  185.3 38.7 %collective-permute-start.56 = (f32[8,768]{1,0:T(8,128)S(1)}, f32[8,768]{1,0:T(8,128)S(1)}, u32[]{:S(2)}, u32[]{:S(2)}) collective-permute-start(f32[8,768]{1,0:T(8,128)S(1)} %get-tuple-element.21), channel_id=1, source_target_pairs={{0,3},{1,2},{2,1},{3,0},{4,7},{5,6},{6,5},{7,4},{8,11},{9,10},{10,... | collective-permute-start | bytes 73736 | tf_op jit(solution)/shard_map/ppermute | solution.py:35
  187.1 38.4 %collective-permute-start.57 = (f32[8,768]{1,0:T(8,128)S(1)}, f32[8,768]{1,0:T(8,128)S(1)}, u32[]{:S(2)}, u32[]{:S(2)}) collective-permute-start(f32[8,768]{1,0:T(8,128)S(1)} %get-tuple-element.21), channel_id=1, source_target_pairs={{0,4},{1,5},{2,6},{3,7},{4,0},{5,1},{6,2},{7,3},{8,12},{9,13},{10,... | collective-permute-start | bytes 73736 | tf_op jit(solution)/shard_map/ppermute | solution.py:35
  190.1 41.0 %collective-permute-start.58 = (f32[8,768]{1,0:T(8,128)S(1)}, f32[8,768]{1,0:T(8,128)S(1)}, u32[]{:S(2)}, u32[]{:S(2)}) collective-permute-start(f32[8,768]{1,0:T(8,128)S(1)} %get-tuple-element.21), channel_id=1, source_target_pairs={{0,5},{1,4},{2,7},{3,6},{4,1},{5,0},{6,3},{7,2},{8,13},{9,12},{10,... | collective-permute-start | bytes 73736 | tf_op jit(solution)/shard_map/ppermute | solution.py:35
  190.1 43.9 %collective-permute-start.59 = (f32[8,768]{1,0:T(8,128)S(1)}, f32[8,768]{1,0:T(8,128)S(1)}, u32[]{:S(2)}, u32[]{:S(2)}) collective-permute-start(f32[8,768]{1,0:T(8,128)S(1)} %get-tuple-element.21), channel_id=1, source_target_pairs={{0,6},{1,7},{2,4},{3,5},{4,2},{5,3},{6,0},{7,1},{8,14},{9,15},{10,... | collective-permute-start | bytes 73736 | tf_op jit(solution)/shard_map/ppermute | solution.py:35
  225.5 45.1 %collective-permute-start.60 = (f32[8,768]{1,0:T(8,128)S(1)}, f32[8,768]{1,0:T(8,128)S(1)}, u32[]{:S(2)}, u32[]{:S(2)}) collective-permute-start(f32[8,768]{1,0:T(8,128)S(1)} %get-tuple-element.21), channel_id=1, source_target_pairs={{0,7},{1,6},{2,5},{3,4},{4,3},{5,2},{6,1},{7,0},{8,15},{9,14},{10,... | collective-permute-start | bytes 73736 | tf_op jit(solution)/shard_map/ppermute | solution.py:35
  251.3 20.3 %collective-permute-start.34 = (bf16[128,192]{1,0:T(8,128)(2,1)S(1)}, bf16[128,192]{1,0:T(8,128)(2,1)S(1)}, u32[]{:S(2)}, u32[]{:S(2)}) collective-permute-start(bf16[128,192]{1,0:T(8,128)(2,1)S(1)} %select_convert_fusion), channel_id=1, source_target_pairs={{0,8},{8,0},{16,24},{24,16},{32,40},{40,32},{48,56},{56,48},{64,72... | collective-permute-start | bytes 147464 | tf_op jit(solution)/shard_map/ppermute | solution.py:31
  (46 other events, 467.2 us)

commit v2 on v1

v2 whole, which is shorter than its diff:
```python
import jax
import jax.numpy as jnp
from jax import lax
from jax.sharding import PartitionSpec as P

F32 = jnp.float32
BF16 = jnp.bfloat16
Z = 8
EP = 8


def fsdp_pairs(move):
    pairs = []
    for lo in range(2):
        for z in range(Z):
            for core in range(2):
                a, b, c = move(lo, z, core)
                pairs.append(((lo * Z + z) * 2 + core, ((a % 2) * Z + b % Z) * 2 + c % 2))
    return pairs


TO_CORE = fsdp_pairs(lambda lo, z, core: (lo, z, core + 1))
TO_UP = fsdp_pairs(lambda lo, z, core: (lo, z + 1, core))
TO_DOWN = fsdp_pairs(lambda lo, z, core: (lo, z - 1, core))
TO_SIDE = fsdp_pairs(lambda lo, z, core: (lo + 1, z, core))


def send(array, pairs):
    return lax.ppermute(array, "fsdp", pairs)


def dot(left, right, dims):
    return lax.dot_general(left, right, (dims, ((), ())), preferred_element_type=F32)


def split3(array):
    high = lax.reduce_precision(array, 8, 7)
    rest = array - high
    mid = lax.reduce_precision(rest, 8, 7)
    low = rest - mid
    return high.astype(BF16), mid.astype(BF16), low.astype(BF16)


def columns(array, start, size):
    return lax.dynamic_slice_in_dim(array, start, size, 1)


def per_device(tokens, out_grad, router_weight, expert_in, expert_out, choices, slots):
    tok_rows, width = tokens.shape
    experts = router_weight.shape[1]
    capacity = max(2, 2 * tok_rows // experts)
    half = capacity // 2
    rows = experts * half
    fsdp_index = lax.axis_index("fsdp")
    me = lax.axis_index("ep")
    core = fsdp_index % 2
    z = (fsdp_index // 2) % Z
    lo = fsdp_index // (2 * Z)
    seg = width // (2 * Z)
    own_cols = width // (4 * Z)

    w_in = expert_in[0].T
    w_out = expert_out[0]

    parts = split3(router_weight)
    logits = dot(tokens, jnp.concatenate(parts, axis=1), ((1,), (0,)))
    logits = (logits[:, :experts] + logits[:, experts : 2 * experts]) + logits[:, 2 * experts :]
    chosen_hot = (choices[:, :, None] == jnp.arange(experts, dtype=jnp.int32)).astype(F32)
    chosen = jnp.sum(chosen_hot * logits[:, None, :], axis=2)
    first_gate = 1.0 / (1.0 + jnp.exp(chosen[:, 1] - chosen[:, 0]))
    second_gate = 1.0 / (1.0 + jnp.exp(chosen[:, 0] - chosen[:, 1]))
    gate_pair = jnp.stack([first_gate, second_gate], axis=1).astype(BF16).astype(F32)
    expert_hot = choices[:, :, None] == jnp.arange(128, dtype=jnp.int32)
    gate_cols = jnp.sum(jnp.where(expert_hot, gate_pair[:, :, None], 0.0), axis=1).astype(BF16)

    key_abs = jnp.where((slots // half == core) & (slots >= 0), choices * half + slots % half, -1)
    places_abs = key_abs[:, :, None] == jnp.arange(rows, dtype=jnp.int32)
    spread_abs = (places_abs[:, 0] | places_abs[:, 1]).astype(BF16)
    packed = jnp.concatenate([out_grad, tokens, gate_cols], axis=1)
    send_rows = dot(spread_abs, packed, ((0,), (0,))).astype(BF16)
    mine_rows = lax.all_to_all(
        send_rows.reshape(experts, half, 2 * width + 128), "ep", 0, 0, tiled=True
    ).reshape(rows, 2 * width + 128)
    other_rows = send(mine_rows, TO_CORE)
    both = jnp.concatenate([mine_rows, other_rows], axis=0)
    rows_dy = both[:, :width]
    rows_x = both[:, width : 2 * width]
    gate = jnp.sum(
        jnp.where(
            jnp.arange(128, dtype=jnp.int32)[None, :] == me,
            both[:, 2 * width :].astype(F32),
            0.0,
        ),
        axis=1,
        keepdims=True,
    )

    pre = dot(rows_x, w_in, ((1,), (1,)))
    back = dot(rows_dy, w_out, ((1,), (1,)))
    sig = jax.nn.sigmoid(pre)
    hidden = (pre * sig).astype(BF16)
    hid_wide = hidden.astype(F32)
    score = jnp.sum(hid_wide * back, axis=1)
    weighted = (hid_wide * gate).astype(BF16)
    act_grad = (gate * back * sig * (1.0 + pre * (1.0 - sig))).astype(BF16)

    part_other = dot(act_grad[rows:], w_in, ((1,), (0,))).astype(BF16)
    from_core = send(part_other, TO_CORE)
    part = (dot(act_grad[:rows], w_in, ((1,), (0,))) + from_core.astype(F32)).astype(BF16)

    def piece(k):
        at = (z + k) % Z
        return jnp.concatenate(
            [columns(part, ((lo ^ d) * Z + at) * seg, seg) for d in range(2)], axis=1
        ).astype(F32)

    up, down = piece(4), piece(5)
    for step in range(3):
        up, down = lax.optimization_barrier((up.astype(BF16), down.astype(BF16)))
        up, down = send(up, TO_UP), send(down, TO_DOWN)
        up = up.astype(F32) + piece(3 - step)
        down = down.astype(F32) + piece((6 + step) % Z)
    total = send(up.astype(BF16), TO_UP).astype(F32) + down
    side = send(total[:, seg:].astype(BF16), TO_SIDE)
    own = (total[:, :seg] + side.astype(F32)).astype(BF16)
    returned = lax.all_to_all(own.reshape(experts, half, seg), "ep", 0, 0, tiled=True).reshape(
        rows, seg
    )
    merged = dot(spread_abs, returned, ((1,), (0,)))
    low_cols, high_cols = merged[:, :own_cols], merged[:, own_cols:]
    keep = jnp.where(core == 0, low_cols, high_cols)
    give = jnp.where(core == 0, high_cols, low_cols)
    expert_grad = keep + send(give.astype(BF16), TO_CORE).astype(F32)

    pair = score.reshape(2, rows)
    pair = jnp.where(core == 0, pair, pair[::-1]).reshape(2, experts, half)
    blocks = jnp.transpose(pair, (1, 0, 2)).reshape(experts, 1, capacity)
    fsdp_size = lax.axis_size("fsdp")
    parts = lax.all_to_all(
        jnp.broadcast_to(blocks[None], (fsdp_size,) + blocks.shape).reshape(-1, 1, capacity),
        ("fsdp", "ep"),
        0,
        0,
        tiled=True,
    )
    all_scores = jnp.sum(parts.reshape(fsdp_size, experts, capacity), axis=0).reshape(-1)
    slot_key = jnp.where(slots >= 0, choices * capacity + slots, -1)
    slot_hot = slot_key[:, :, None] == jnp.arange(experts * capacity, dtype=jnp.int32)
    taken = jnp.sum(jnp.where(slot_hot, all_scores[None, None, :], 0.0), axis=2)
    change = first_gate * second_gate * (taken[:, 0] - taken[:, 1])
    logit_grad = change[:, None] * (chosen_hot[:, 0, :] - chosen_hot[:, 1, :])

    router_part = dot(jnp.concatenate(split3(logit_grad), axis=1), tokens, ((0,), (0,)))
    router_part = (router_part[:experts] + router_part[experts : 2 * experts]) + router_part[
        2 * experts :
    ]
    chunk = width // EP
    chunks = jnp.transpose(router_part.reshape(experts, EP, chunk), (1, 0, 2))
    mine = jnp.sum(lax.all_to_all(chunks, "ep", 0, 0, tiled=True), axis=0) / (tok_rows * EP)
    gathered = lax.all_to_all(
        jnp.broadcast_to(mine[None], (EP, experts, chunk)), "ep", 0, 0, tiled=True
    )
    grad_router = jnp.transpose(gathered, (1, 0, 2)).reshape(experts, width)

    grad_out = dot(weighted, rows_dy, ((0,), (0,))).astype(BF16)
    grad_in = dot(act_grad, rows_x, ((0,), (0,))).astype(BF16)

    router_rows = lax.dynamic_slice_in_dim(router_weight, fsdp_index * own_cols, own_cols, 0)
    grad_tokens = (
        expert_grad + jnp.dot(logit_grad, router_rows.T, precision=lax.Precision.HIGHEST)
    ).astype(BF16)
    return grad_tokens, grad_in.T[None], grad_out[None], grad_router.T


def solution(mesh):
    placed = (
        P("ep", None),
        P("ep", None),
        P(),
        P("ep", None, "fsdp"),
        P("ep", "fsdp", None),
        P("ep", None),
        P("ep", None),
    )
    return jax.shard_map(
        per_device,
        mesh=mesh,
        in_specs=placed,
        out_specs=(P("ep", "fsdp"), P("ep", None, "fsdp"), P("ep", "fsdp", None), P()),
        check_vma=False,
    )
```

time: 278 us -> 162 us (0.58); the launches traced: 273 us -> 160 us
  starting transfers between devices: 143 us -> 40.2 us
  blocking collectives: 0 us -> 46.3 us
  local copies, waits for them, and re-layouts: 39.8 us -> 3.96 us
  waiting for transfers between devices: 65.5 us -> 37.1 us
  matrix products: 19.6 us -> 24.2 us
  other arithmetic: 3.38 us -> 6.6 us
    ppermute x42 -> x0, starting transfers between devices: 88.2 us -> none  [send_ep(): return lax.ppermute(array, 'ep', TO_EXPERT[r])]
    all_to_all x0 -> x1, blocking collectives: none -> 46.3 us  [per_device(): lax.all_to_all(send_rows.reshape(experts, half, 2 * width + 128), 'ep', 0...]
    ppermute x19 -> x11, starting transfers between devices: 54.6 us -> 17 us  [send(): return lax.ppermute(array, 'fsdp', pairs)]
    unnamed x60 -> x10, local copies, waits for them, and re-layouts: 31.3 us -> 2 us
    ppermute x42 -> x0, waiting for transfers between devices: 29.3 us -> none  [send_ep(): return lax.ppermute(array, 'ep', TO_EXPERT[r])]
    all_to_all x0 -> x4, starting transfers between devices: none -> 23.3 us  [the longest x1 10.3 us: per_device(): lax.all_to_all(jnp.broadcast_to(blocks[None], (fsdp_size,) + blocks.shape...]
    all_to_all x0 -> x4, waiting for transfers between devices: none -> 21.5 us  [the longest x1 12.4 us: per_device(): lax.all_to_all(jnp.broadcast_to(blocks[None], (fsdp_size,) + blocks.shape...]
    ppermute x19 -> x11, waiting for transfers between devices: 36.2 us -> 15.6 us  [send(): return lax.ppermute(array, 'fsdp', pairs)]
  transfers between devices with their start and end apart: 61 -> 15, of which waited for: 22 -> 8; matrix products, arithmetic and copies ran while one was open for 18% -> 7% of each run, Pallas kernels for 0% -> 0%
where the time goes in v2:
time: 162 us; the launch traced here: 160 us
  blocking collectives  46.3 us (29%)
  starting transfers between devices  40.2 us (25%)
  waiting for transfers between devices  37.1 us (23%)
  matrix products  24.2 us (15%)
  other arithmetic  6.6 us (4%)
  local copies, waits for them, and re-layouts  3.96 us (2%)
    all_to_all x1, blocking collectives, per_device(): lax.all_to_all(send_rows.reshape(experts, half, 2 * width + 128), 'ep', 0...  46.3 us
    dot_general x10, matrix products, dot(): lax.dot_general(left, right, (dims, ((), ())), preferred_element_type=F32)  23.1 us
    ppermute x11, starting transfers between devices, send(): return lax.ppermute(array, 'fsdp', pairs)  17 us
    ppermute x11, waiting for transfers between devices, send(): return lax.ppermute(array, 'fsdp', pairs)  15.6 us
    all_to_all x1, waiting for transfers between devices, per_device(): lax.all_to_all(jnp.broadcast_to(blocks[None], (fsdp_size,) + blocks.shape...  12.4 us
    all_to_all x1, starting transfers between devices, per_device(): lax.all_to_all(jnp.broadcast_to(blocks[None], (fsdp_size,) + blocks.shape...  10.3 us
    all_to_all x1, waiting for transfers between devices, per_device(): lax.all_to_all(own.reshape(experts, half, seg), 'ep', 0, 0, tiled=True)  6.78 us
    all_to_all x1, starting transfers between devices, per_device(): lax.all_to_all(own.reshape(experts, half, seg), 'ep', 0, 0, tiled=True)  4.92 us
  transfers between devices with their start and end apart: 15, of which 8 were waited for; matrix products, arithmetic and copies ran while one was open for 7% of the time, Pallas kernels for 0%

profile of v2, /device:TPU:1, one launch (start us, length us, event | category | flops | bytes accessed | tf_op | source)
XLA Modules:
  0.0 159.6 jit_solution(12178045620303756526)
XLA Ops:
  1.8 1.9 %convolution_bitcast_fusion = f32[128,24]{0,1:T(8,128)S(1)} fusion(bf16[128,6144]{1,0:T(8,128)(2,1)} %param.7, bf16[6144,8]{0,1:T(8,128)(2,1)S(1)} %get-tuple-element.61, bf16[6144,8]{0,1:T(8,128)(2,1)S(1)} %get-tuple-element.62, bf16[6144,8]{0,1:T(8,128)(2,1)S(1)} %get-tuple-element.60), kind=kOutput, calls=%fused_computation.21 | convolution fusion | flops 38633472 | bytes 1880064 | tf_op jit(solution)/shard_map/dot_general | solution.py:33
  6.1 2.9 %convolution_convert_fusion = bf16[128,12416]{1,0:T(8,128)(2,1)S(1)} fusion(bf16[128,128]{1,0:T(8,128)(2,1)S(1)} %select_reduce_fusion.2, bf16[128,6144]{1,0:T(8,128)(2,1)} %param.7, bf16[128,6144]{1,0:T(8,128)(2,1)} %param.8, pred[128,2,128]{2,0,1:T(32,128)(4,1)S(1)} %iota_compare_fusion.2), kind=kOutput, calls=%fused_computation | convolution fusion | flops 417988608 | bytes 6389760 | tf_op jit(solution)/shard_map/dot_general | solution.py:33
  9.0 46.3 %all_to_all.25 = bf16[8,16,12416]{2,1,0:T(8,128)(2,1)} all-to-all(bf16[8,16,12416]{2,1,0:T(8,128)(2,1)S(1)} %bitcast.55), channel_id=1, replica_groups=mesh['fsdp'=32,'ep'=8] {'ep'}, dimensions={0} | all-to-all | bytes 6356992 | tf_op jit(solution)/shard_map/all_to_all | solution.py:81
  55.3 2.2 %collective-permute-start = (bf16[128,12416]{1,0:T(8,128)(2,1)}, bf16[128,12416]{1,0:T(8,128)(2,1)}, u32[]{:S(2)}, u32[]{:S(2)}) collective-permute-start(bf16[128,12416]{1,0:T(8,128)(2,1)} %bitcast.3), channel_id=1, source_target_pairs={{0,8},{8,0},{16,24},{24,16},{32,40},{40,32},{48,56},{56,48},{64,72... | collective-permute-start | bytes 9535496 | tf_op jit(solution)/shard_map/ppermute | solution.py:29
  57.6 5.7 %collective-permute-done = bf16[128,12416]{1,0:T(8,128)(2,1)} collective-permute-done((bf16[128,12416]{1,0:T(8,128)(2,1)}, bf16[128,12416]{1,0:T(8,128)(2,1)}, u32[]{:S(2)}, u32[]{:S(2)}) %collective-permute-start) | collective-permute-done | bytes 3178528 | tf_op jit(solution)/shard_map/ppermute | solution.py:29
  63.3 3.1 %fusion.10 = f32[256,168]{0,1:T(8,128)S(1)} fusion(bf16[1,6144,168]{1,2,0:T(8,128)(2,1)S(1)} %copy-done, bf16[128,12416]{1,0:T(8,128)(2,1)} %collective-permute-done, bf16[128,12416]{1,0:T(8,128)(2,1)} %bitcast.3), kind=kOutput, calls=%fused_computation.17 | convolution fusion | flops 534773760 | bytes 8593408 | tf_op jit(solution)/shard_map/dot_general | solution.py:33
  68.0 3.1 %fusion.23 = (f32[256]{0:T(256)S(1)}, bf16[256,168]{0,1:T(8,128)(2,1)S(1)}) fusion(f32[256,168]{0,1:T(8,128)S(1)} %fusion.10, f32[256]{0:T(256)S(1)} %select_reduce_fusion.1, bf16[1,168,6144]{2,1,0:T(8,128)(2,1)S(1)} %copy-done.3, bf16[128,12416]{1,0:T(8,128)(2,1)} %collective-permute-done, bf16[128,12416]{1,0:T(8,128)(2,1)} %bitcast.3), kind=kOutput, calls=%fused_computation.49 | convolution fusion | flops 535418624 | bytes 8681472 | tf_op jit(solution)/shard_map/dot_general | solution.py:33
  74.1 10.3 %all-to-all-start.2 = ((f32[256,1,32]{2,1,0:T(1,128)}), f32[256,1,32]{2,1,0:T(1,128)S(1)}, u32[]{:S(2)}, u32[]{:S(2)}) async-start(f32[256,1,32]{2,1,0:T(1,128)} %bitcast.10), calls=%async_computation.2 | async-start | bytes 262144 | tf_op jit(solution)/shard_map/all_to_all | solution.py:139
  84.7 12.4 %all-to-all-done.2 = f32[256,1,32]{2,1,0:T(1,128)S(1)} async-done(((f32[256,1,32]{2,1,0:T(1,128)}), f32[256,1,32]{2,1,0:T(1,128)S(1)}, u32[]{:S(2)}, u32[]{:S(2)}) %all-to-all-start.2) | async-done | bytes 32800 | tf_op jit(solution)/shard_map/all_to_all | solution.py:139
  97.4 2.0 %add_convert_fusion = bf16[128,6144]{1,0:T(8,128)(2,1)S(1)} fusion(bf16[128,6144]{1,0:T(8,128)(2,1)} %collective-permute-done.1, bf16[1,6144,168]{1,2,0:T(8,128)(2,1)S(1)} %copy-done, bf16[256,168]{0,1:T(8,128)(2,1)S(1)} %get-tuple-element.59), kind=kOutput, calls=%fused_computation.13 | convolution fusion | flops 266600448 | bytes 5253120 | tf_op jit(solution)/shard_map/dot_general | solution.py:33
  100.6 2.0 %collective-permute-start.3 = (bf16[128,768]{1,0:T(8,128)(2,1)S(1)}, bf16[128,768]{1,0:T(8,128)(2,1)S(1)}, u32[]{:S(2)}, u32[]{:S(2)}) collective-permute-start(bf16[128,768]{1,0:T(8,128)(2,1)S(1)} %get-tuple-element.11), channel_id=1, source_target_pairs={{0,112},{8,120},{16,0},{24,8},{32,16},{40,24},{48,32},{56,40},{64,... | collective-permute-start | bytes 589832 | tf_op jit(solution)/shard_map/ppermute | solution.py:29
  102.6 3.9 %collective-permute-done.2 = bf16[128,768]{1,0:T(8,128)(2,1)S(1)} collective-permute-done((bf16[128,768]{1,0:T(8,128)(2,1)S(1)}, bf16[128,768]{1,0:T(8,128)(2,1)S(1)}, u32[]{:S(2)}, u32[]{:S(2)}) %collective-permute-start.2) | collective-permute-done | bytes 196640 | tf_op jit(solution)/shard_map/ppermute | solution.py:29
  106.7 2.7 %collective-permute-start.5 = (bf16[128,768]{1,0:T(8,128)(2,1)S(1)}, bf16[128,768]{1,0:T(8,128)(2,1)S(1)}, u32[]{:S(2)}, u32[]{:S(2)}) collective-permute-start(bf16[128,768]{1,0:T(8,128)(2,1)S(1)} %add_convert_fusion.4), channel_id=1, source_target_pairs={{0,112},{8,120},{16,0},{24,8},{32,16},{40,24},{48,32},{56,40},{64,... | collective-permute-start | bytes 589832 | tf_op jit(solution)/shard_map/ppermute | solution.py:29
  109.4 3.0 %collective-permute-done.4 = bf16[128,768]{1,0:T(8,128)(2,1)S(1)} collective-permute-done((bf16[128,768]{1,0:T(8,128)(2,1)S(1)}, bf16[128,768]{1,0:T(8,128)(2,1)S(1)}, u32[]{:S(2)}, u32[]{:S(2)}) %collective-permute-start.4) | collective-permute-done | bytes 196640 | tf_op jit(solution)/shard_map/ppermute | solution.py:29
  113.1 2.7 %collective-permute-start.8 = (bf16[128,768]{1,0:T(8,128)(2,1)S(1)}, bf16[128,768]{1,0:T(8,128)(2,1)S(1)}, u32[]{:S(2)}, u32[]{:S(2)}) collective-permute-start(bf16[128,768]{1,0:T(8,128)(2,1)S(1)} %add_convert_fusion.2), channel_id=1, source_target_pairs={{0,112},{8,120},{16,0},{24,8},{32,16},{40,24},{48,32},{56,40},{64,... | collective-permute-start | bytes 589832 | tf_op jit(solution)/shard_map/ppermute | solution.py:29
  115.9 2.7 %collective-permute-done.6 = bf16[128,768]{1,0:T(8,128)(2,1)S(1)} collective-permute-done((bf16[128,768]{1,0:T(8,128)(2,1)S(1)}, bf16[128,768]{1,0:T(8,128)(2,1)S(1)}, u32[]{:S(2)}, u32[]{:S(2)}) %collective-permute-start.6) | collective-permute-done | bytes 196640 | tf_op jit(solution)/shard_map/ppermute | solution.py:29
  119.4 4.7 %all-to-all-start.3 = ((f32[8,8,768]{2,1,0:T(8,128)}), f32[8,8,768]{2,1,0:T(8,128)S(1)}, u32[]{:S(2)}, u32[]{:S(2)}) async-start(f32[8,8,768]{2,1,0:T(8,128)} %bitcast.17), calls=%async_computation.3 | async-start | bytes 393216 | tf_op jit(solution)/shard_map/all_to_all | solution.py:159
  125.1 3.9 %fusion.1 = bf16[1,168,6144]{2,1,0:T(8,128)(2,1)} fusion(bf16[128,12416]{1,0:T(8,128)(2,1)} %collective-permute-done, bf16[128,12416]{1,0:T(8,128)(2,1)} %bitcast.3, f32[256]{0:T(256)S(1)} %select_reduce_fusion.1, f32[256,168]{0,1:T(8,128)S(1)} %fusion.10), kind=kOutput, calls=%fused_computation.5 | convolution fusion | flops 536150016 | bytes 8594432 | tf_op jit(solution)/shard_map/dot_general | solution.py:33
  129.0 2.3 %all-to-all-done.3 = f32[8,8,768]{2,1,0:T(8,128)S(1)} async-done(((f32[8,8,768]{2,1,0:T(8,128)}), f32[8,8,768]{2,1,0:T(8,128)S(1)}, u32[]{:S(2)}, u32[]{:S(2)}) %all-to-all-start.3) | async-done | bytes 196640 | tf_op jit(solution)/shard_map/all_to_all | solution.py:159
  132.0 4.9 %all-to-all-start.1 = ((bf16[8,16,384]{2,1,0:T(8,128)(2,1)}), bf16[8,16,384]{2,1,0:T(8,128)(2,1)S(1)}, u32[]{:S(2)}, u32[]{:S(2)}) async-start(bf16[8,16,384]{2,1,0:T(8,128)(2,1)} %bitcast.6), calls=%async_computation.1 | async-start | bytes 196608 | tf_op jit(solution)/shard_map/all_to_all | solution.py:126
  136.9 6.8 %all-to-all-done.1 = bf16[8,16,384]{2,1,0:T(8,128)(2,1)S(1)} async-done(((bf16[8,16,384]{2,1,0:T(8,128)(2,1)}), bf16[8,16,384]{2,1,0:T(8,128)(2,1)S(1)}, u32[]{:S(2)}, u32[]{:S(2)}) %all-to-all-start.1) | async-done | bytes 98336 | tf_op jit(solution)/shard_map/all_to_all | solution.py:126
  144.4 3.4 %all-to-all-start.4 = ((f32[8,8,768]{2,1,0:T(8,128)}), f32[8,8,768]{2,1,0:T(8,128)S(1)}, u32[]{:S(2)}, u32[]{:S(2)}) async-start(f32[8,8,768]{2,1,0:T(8,128)} %broadcast_in_dim.87), calls=%async_computation.4 | async-start | bytes 393216 | tf_op jit(solution)/shard_map/all_to_all | solution.py:160
  148.1 5.2 %collective-permute-start.10 = (bf16[128,192]{1,0:T(8,128)(2,1)S(1)}, bf16[128,192]{1,0:T(8,128)(2,1)S(1)}, u32[]{:S(2)}, u32[]{:S(2)}) collective-permute-start(bf16[128,192]{1,0:T(8,128)(2,1)S(1)} %select_convert_fusion), channel_id=1, source_target_pairs={{0,8},{8,0},{16,24},{24,16},{32,40},{40,32},{48,56},{56,48},{64,72... | collective-permute-start | bytes 147464 | tf_op jit(solution)/shard_map/ppermute | solution.py:29
  153.3 3.9 %fusion = bf16[1,6144,168]{1,2,0:T(8,128)(2,1)} fusion(bf16[256,168]{0,1:T(8,128)(2,1)S(1)} %get-tuple-element.59, bf16[128,12416]{1,0:T(8,128)(2,1)} %collective-permute-done, bf16[128,12416]{1,0:T(8,128)(2,1)} %bitcast.3), kind=kOutput, calls=%fused_computation.4 | convolution fusion | flops 535805952 | bytes 8507392 | tf_op jit(solution)/shard_map/dot_general | solution.py:33
  (66 shorter events, 16.4 us)
Async XLA Ops:
  0.6 62.6 %copy-start = (bf16[1,6144,168]{1,2,0:T(8,128)(2,1)S(1)}, bf16[1,6144,168]{1,2,0:T(8,128)(2,1)}, u32[]{:S(2)}) copy-start(bf16[1,6144,168]{1,2,0:T(8,128)(2,1)} %param.10) | copy-start | bytes 6193156
  55.3 7.9 %collective-permute-start = (bf16[128,12416]{1,0:T(8,128)(2,1)}, bf16[128,12416]{1,0:T(8,128)(2,1)}, u32[]{:S(2)}, u32[]{:S(2)}) collective-permute-start(bf16[128,12416]{1,0:T(8,128)(2,1)} %bitcast.3), channel_id=1, source_target_pairs={{0,8},{8,0},{16,24},{24,16},{32,40},{40,32},{48,56},{56,48},{64,72... | collective-permute-start | bytes 9535496 | tf_op jit(solution)/shard_map/ppermute | solution.py:29
  66.4 1.6 %copy-start.3 = (bf16[1,168,6144]{2,1,0:T(8,128)(2,1)S(1)}, bf16[1,168,6144]{2,1,0:T(8,128)(2,1)}, u32[]{:S(2)}) copy-start(bf16[1,168,6144]{2,1,0:T(8,128)(2,1)} %param.11) | copy-start | bytes 6193156
  71.1 13.3 %copy-start.2 = (s32[128,2]{0,1:T(2,128)S(1)}, s32[128,2]{0,1:T(2,128)}, u32[]{:S(2)}) copy-start(s32[128,2]{0,1:T(2,128)} %param.12) | copy-start | bytes 3076
  72.9 24.5 %collective-permute-start.1 = (bf16[128,6144]{1,0:T(8,128)(2,1)}, bf16[128,6144]{1,0:T(8,128)(2,1)}, u32[]{:S(2)}, u32[]{:S(2)}) collective-permute-start(bf16[128,6144]{1,0:T(8,128)(2,1)} %convolution_convert_fusion.3), channel_id=1, source_target_pairs={{0,8},{8,0},{16,24},{24,16},{32,40},{40,32},{48,56},{56,48},{64,72... | collective-permute-start | bytes 4718600 | tf_op jit(solution)/shard_map/ppermute | solution.py:29
  74.1 23.0 %all-to-all-start.2 = ((f32[256,1,32]{2,1,0:T(1,128)}), f32[256,1,32]{2,1,0:T(1,128)S(1)}, u32[]{:S(2)}, u32[]{:S(2)}) async-start(f32[256,1,32]{2,1,0:T(1,128)} %bitcast.10), calls=%async_computation.2 | async-start | bytes 262144 | tf_op jit(solution)/shard_map/all_to_all | solution.py:139
  99.4 13.4 %copy-start.1 = (bf16[128,6144]{1,0:T(8,128)(2,1)S(1)}, bf16[128,6144]{1,0:T(8,128)(2,1)}, u32[]{:S(2)}) copy-start(bf16[128,6144]{1,0:T(8,128)(2,1)} %param.7) | copy-start | bytes 4718596
  99.8 6.7 %collective-permute-start.2 = (bf16[128,768]{1,0:T(8,128)(2,1)S(1)}, bf16[128,768]{1,0:T(8,128)(2,1)S(1)}, u32[]{:S(2)}, u32[]{:S(2)}) collective-permute-start(bf16[128,768]{1,0:T(8,128)(2,1)S(1)} %get-tuple-element.10), channel_id=1, source_target_pairs={{0,16},{8,24},{16,32},{24,40},{32,48},{40,56},{48,64},{56,72},{64,... | collective-permute-start | bytes 589832 | tf_op jit(solution)/shard_map/ppermute | solution.py:29
  100.6 6.0 %collective-permute-start.3 = (bf16[128,768]{1,0:T(8,128)(2,1)S(1)}, bf16[128,768]{1,0:T(8,128)(2,1)S(1)}, u32[]{:S(2)}, u32[]{:S(2)}) collective-permute-start(bf16[128,768]{1,0:T(8,128)(2,1)S(1)} %get-tuple-element.11), channel_id=1, source_target_pairs={{0,112},{8,120},{16,0},{24,8},{32,16},{40,24},{48,32},{56,40},{64,... | collective-permute-start | bytes 589832 | tf_op jit(solution)/shard_map/ppermute | solution.py:29
  106.6 5.8 %collective-permute-start.4 = (bf16[128,768]{1,0:T(8,128)(2,1)S(1)}, bf16[128,768]{1,0:T(8,128)(2,1)S(1)}, u32[]{:S(2)}, u32[]{:S(2)}) collective-permute-start(bf16[128,768]{1,0:T(8,128)(2,1)S(1)} %add_convert_fusion.5), channel_id=1, source_target_pairs={{0,16},{8,24},{16,32},{24,40},{32,48},{40,56},{48,64},{56,72},{64,... | collective-permute-start | bytes 589832 | tf_op jit(solution)/shard_map/ppermute | solution.py:29
  106.7 5.8 %collective-permute-start.5 = (bf16[128,768]{1,0:T(8,128)(2,1)S(1)}, bf16[128,768]{1,0:T(8,128)(2,1)S(1)}, u32[]{:S(2)}, u32[]{:S(2)}) collective-permute-start(bf16[128,768]{1,0:T(8,128)(2,1)S(1)} %add_convert_fusion.4), channel_id=1, source_target_pairs={{0,112},{8,120},{16,0},{24,8},{32,16},{40,24},{48,32},{56,40},{64,... | collective-permute-start | bytes 589832 | tf_op jit(solution)/shard_map/ppermute | solution.py:29
  112.5 6.0 %collective-permute-start.6 = (bf16[128,768]{1,0:T(8,128)(2,1)S(1)}, bf16[128,768]{1,0:T(8,128)(2,1)S(1)}, u32[]{:S(2)}, u32[]{:S(2)}) collective-permute-start(bf16[128,768]{1,0:T(8,128)(2,1)S(1)} %add_convert_fusion.3), channel_id=1, source_target_pairs={{0,16},{8,24},{16,32},{24,40},{32,48},{40,56},{48,64},{56,72},{64,... | collective-permute-start | bytes 589832 | tf_op jit(solution)/shard_map/ppermute | solution.py:29
  113.1 10.9 %collective-permute-start.8 = (bf16[128,768]{1,0:T(8,128)(2,1)S(1)}, bf16[128,768]{1,0:T(8,128)(2,1)S(1)}, u32[]{:S(2)}, u32[]{:S(2)}) collective-permute-start(bf16[128,768]{1,0:T(8,128)(2,1)S(1)} %add_convert_fusion.2), channel_id=1, source_target_pairs={{0,112},{8,120},{16,0},{24,8},{32,16},{40,24},{48,32},{56,40},{64,... | collective-permute-start | bytes 589832 | tf_op jit(solution)/shard_map/ppermute | solution.py:29
  118.6 5.8 %collective-permute-start.7 = (bf16[128,768]{1,0:T(8,128)(2,1)S(1)}, bf16[128,768]{1,0:T(8,128)(2,1)S(1)}, u32[]{:S(2)}, u32[]{:S(2)}) collective-permute-start(bf16[128,768]{1,0:T(8,128)(2,1)S(1)} %add_convert_fusion.1), channel_id=1, source_target_pairs={{0,16},{8,24},{16,32},{24,40},{32,48},{40,56},{48,64},{56,72},{64,... | collective-permute-start | bytes 589832 | tf_op jit(solution)/shard_map/ppermute | solution.py:29
  119.4 11.9 %all-to-all-start.3 = ((f32[8,8,768]{2,1,0:T(8,128)}), f32[8,8,768]{2,1,0:T(8,128)S(1)}, u32[]{:S(2)}, u32[]{:S(2)}) async-start(f32[8,8,768]{2,1,0:T(8,128)} %bitcast.17), calls=%async_computation.3 | async-start | bytes 393216 | tf_op jit(solution)/shard_map/all_to_all | solution.py:159
  124.5 6.9 %collective-permute-start.9 = (bf16[128,384]{1,0:T(8,128)(2,1)S(1)}, bf16[128,384]{1,0:T(8,128)(2,1)S(1)}, u32[]{:S(2)}, u32[]{:S(2)}) collective-permute-start(bf16[128,384]{1,0:T(8,128)(2,1)S(1)} %slice.153), channel_id=1, source_target_pairs={{0,128},{8,136},{16,144},{24,152},{32,160},{40,168},{48,176},{56,1... | collective-permute-start | bytes 294920 | tf_op jit(solution)/shard_map/ppermute | solution.py:29
  132.0 11.7 %all-to-all-start.1 = ((bf16[8,16,384]{2,1,0:T(8,128)(2,1)}), bf16[8,16,384]{2,1,0:T(8,128)(2,1)S(1)}, u32[]{:S(2)}, u32[]{:S(2)}) async-start(bf16[8,16,384]{2,1,0:T(8,128)(2,1)} %bitcast.6), calls=%async_computation.1 | async-start | bytes 196608 | tf_op jit(solution)/shard_map/all_to_all | solution.py:126
  144.4 12.7 %all-to-all-start.4 = ((f32[8,8,768]{2,1,0:T(8,128)}), f32[8,8,768]{2,1,0:T(8,128)S(1)}, u32[]{:S(2)}, u32[]{:S(2)}) async-start(f32[8,8,768]{2,1,0:T(8,128)} %broadcast_in_dim.87), calls=%async_computation.4 | async-start | bytes 393216 | tf_op jit(solution)/shard_map/all_to_all | solution.py:160
  148.1 9.1 %collective-permute-start.10 = (bf16[128,192]{1,0:T(8,128)(2,1)S(1)}, bf16[128,192]{1,0:T(8,128)(2,1)S(1)}, u32[]{:S(2)}, u32[]{:S(2)}) collective-permute-start(bf16[128,192]{1,0:T(8,128)(2,1)S(1)} %select_convert_fusion), channel_id=1, source_target_pairs={{0,8},{8,0},{16,24},{24,16},{32,40},{40,32},{48,56},{56,48},{64,72... | collective-permute-start | bytes 147464 | tf_op jit(solution)/shard_map/ppermute | solution.py:29

commit v3 on v2

v3 whole, which is shorter than its diff:
```python
import jax
import jax.numpy as jnp
from jax import lax
from jax.sharding import PartitionSpec as P

F32 = jnp.float32
BF16 = jnp.bfloat16
Z = 8
EP = 8


def fsdp_pairs(move):
    pairs = []
    for lo in range(2):
        for z in range(Z):
            for core in range(2):
                a, b, c = move(lo, z, core)
                pairs.append(((lo * Z + z) * 2 + core, ((a % 2) * Z + b % Z) * 2 + c % 2))
    return pairs


TO_CORE = fsdp_pairs(lambda lo, z, core: (lo, z, core + 1))
TO_UP = fsdp_pairs(lambda lo, z, core: (lo, z + 1, core))
TO_DOWN = fsdp_pairs(lambda lo, z, core: (lo, z - 1, core))
TO_SIDE = fsdp_pairs(lambda lo, z, core: (lo + 1, z, core))


def send(array, pairs):
    return lax.ppermute(array, "fsdp", pairs)


def dot(left, right, dims):
    return lax.dot_general(left, right, (dims, ((), ())), preferred_element_type=F32)


def split3(array):
    high = lax.reduce_precision(array, 8, 7)
    rest = array - high
    mid = lax.reduce_precision(rest, 8, 7)
    low = rest - mid
    return high.astype(BF16), mid.astype(BF16), low.astype(BF16)


def columns(array, start, size):
    return lax.dynamic_slice_in_dim(array, start, size, 1)


def per_device(tokens, out_grad, router_weight, expert_in, expert_out, choices, slots):
    tok_rows, width = tokens.shape
    experts = router_weight.shape[1]
    capacity = max(2, 2 * tok_rows // experts)
    half = capacity // 2
    rows = experts * half
    fsdp_index = lax.axis_index("fsdp")
    me = lax.axis_index("ep")
    core = fsdp_index % 2
    z = (fsdp_index // 2) % Z
    lo = fsdp_index // (2 * Z)
    seg = width // (2 * Z)
    own_cols = width // (4 * Z)

    w_in = expert_in[0].T
    w_out = expert_out[0]

    router_parts = jnp.concatenate(split3(router_weight), axis=1)
    logits = dot(tokens, router_parts, ((1,), (0,)))
    logits = (logits[:, :experts] + logits[:, experts : 2 * experts]) + logits[:, 2 * experts :]
    chosen_hot = (choices[:, :, None] == jnp.arange(experts, dtype=jnp.int32)).astype(F32)
    chosen = jnp.sum(chosen_hot * logits[:, None, :], axis=2)
    first_gate = 1.0 / (1.0 + jnp.exp(chosen[:, 1] - chosen[:, 0]))
    second_gate = 1.0 / (1.0 + jnp.exp(chosen[:, 0] - chosen[:, 1]))

    key_abs = jnp.where((slots // half == core) & (slots >= 0), choices * half + slots % half, -1)
    places_abs = key_abs[:, :, None] == jnp.arange(rows, dtype=jnp.int32)
    spread_abs = (places_abs[:, 0] | places_abs[:, 1]).astype(BF16)
    both_choices = jnp.broadcast_to(
        jnp.sum(choices, axis=1, keepdims=True).astype(BF16), (tok_rows, 128)
    )
    packed = jnp.concatenate([out_grad, tokens, both_choices], axis=1)
    send_rows = dot(spread_abs, packed, ((0,), (0,))).astype(BF16)
    mine_rows = lax.all_to_all(
        send_rows.reshape(experts, half, 2 * width + 128), "ep", 0, 0, tiled=True
    ).reshape(rows, 2 * width + 128)
    other_rows = send(mine_rows, TO_CORE)
    w_ext = jnp.concatenate([w_in, router_parts.T], axis=0)
    hidden_count = w_in.shape[0]

    def act(part_rows):
        ext = dot(part_rows[:, width : 2 * width], w_ext, ((1,), (1,)))
        back = dot(part_rows[:, :width], w_out, ((1,), (1,)))
        pre = ext[:, :hidden_count]
        row_logits = ext[:, hidden_count : hidden_count + experts] + (
            ext[:, hidden_count + experts : hidden_count + 2 * experts]
            + ext[:, hidden_count + 2 * experts :]
        )
        second = part_rows[:, 2 * width : 2 * width + 1].astype(jnp.int32) - me
        ids = jnp.arange(experts, dtype=jnp.int32)[None, :]
        gap = jnp.sum(
            jnp.where(ids == second, row_logits, 0.0) - jnp.where(ids == me, row_logits, 0.0),
            axis=1,
            keepdims=True,
        )
        gate_wide = 1.0 / (1.0 + jnp.exp(gap))
        slope = gate_wide * (1.0 / (1.0 + jnp.exp(-gap)))
        gate = gate_wide.astype(BF16).astype(F32)
        sig = jax.nn.sigmoid(pre)
        hidden = (pre * sig).astype(BF16)
        hid_wide = hidden.astype(F32)
        score = jnp.sum(hid_wide * back, axis=1, keepdims=True)
        weighted = (hid_wide * gate).astype(BF16)
        act_grad = (gate * back * sig * (1.0 + pre * (1.0 - sig))).astype(BF16)
        slopes = slope * ((ids == me).astype(F32) - (ids == second).astype(F32))
        return score, weighted, act_grad, slopes

    score_mine, weighted_mine, act_mine, slopes_mine = act(mine_rows)
    score_other, weighted_other, act_other, _ = act(other_rows)

    def weights(k):
        at = (z + k) % Z
        return [columns(w_in, ((lo ^ d) * Z + at) * seg, seg) for d in range(2)]

    orders = [(4, 5), (3, 6), (2, 7), (1, 0)]
    near = [jnp.concatenate(weights(a) + weights(b), axis=1) for a, b in orders]

    def pack(grads, score):
        high = lax.reduce_precision(score, 8, 7)
        lane = lax.broadcasted_iota(jnp.int32, (rows, 128), 1)
        block = jnp.where(lane == 0, high, jnp.where(lane == 1, score - high, 0.0))
        return jnp.concatenate([grads.astype(BF16), block.astype(BF16)], axis=1)

    def unpack(packed):
        wide = packed.astype(F32)
        return wide[:, :-128], jnp.sum(wide[:, -128:], axis=1, keepdims=True)

    first_other = dot(act_other, near[0], ((1,), (0,)))
    got, got_score = unpack(send(pack(first_other, score_other), TO_CORE))
    score = score_mine + got_score
    part = dot(act_mine, near[0], ((1,), (0,))) + got
    up, down = part[:, : 2 * seg], part[:, 2 * seg :]
    up_score = down_score = score
    for step in range(3):
        going_up, going_down = lax.optimization_barrier(
            (pack(up, up_score), pack(down, down_score))
        )
        up, up_score = unpack(send(going_up, TO_UP))
        down, down_score = unpack(send(going_down, TO_DOWN))
        other = dot(act_other, near[step + 1], ((1,), (0,))).astype(BF16)
        got = send(other, TO_CORE)
        part = dot(act_mine, near[step + 1], ((1,), (0,))) + got.astype(F32)
        up, up_score = up + part[:, : 2 * seg], up_score + score
        down, down_score = down + part[:, 2 * seg :], down_score + score
    last, last_score = unpack(send(pack(up, up_score), TO_UP))
    total, total_score = last + down, last_score + down_score
    side, side_score = unpack(send(pack(total[:, seg:], total_score), TO_SIDE))
    own, own_score = total[:, :seg] + side, total_score + side_score

    router_part = dot(
        jnp.concatenate(split3(slopes_mine * own_score), axis=1),
        mine_rows[:, width : 2 * width],
        ((0,), (0,)),
    )
    router_part = (router_part[:experts] + router_part[experts : 2 * experts]) + router_part[
        2 * experts :
    ]
    chunk = width // EP

    def two(array):
        high = lax.reduce_precision(array, 8, 7)
        return jnp.stack([high, array - high]).astype(BF16)

    chunks = jnp.transpose(two(router_part).reshape(2, experts, EP, chunk), (2, 0, 1, 3))

    home = lax.all_to_all(
        jnp.concatenate(
            [
                pack(own, own_score).reshape(experts, half, seg + 128),
                jnp.concatenate(
                    [
                        chunks.reshape(EP, -1, seg),
                        jnp.zeros((EP, 2 * experts * chunk // seg, 128), BF16),
                    ],
                    axis=2,
                ),
            ],
            axis=1,
        ),
        "ep",
        0,
        0,
        tiled=True,
    )
    returned, back_scores = unpack(home[:, :half].reshape(rows, seg + 128))
    router_mine = jnp.sum(
        home[:, half:, :seg].reshape(EP, 2, experts, chunk).astype(F32), axis=(0, 1)
    ) / (tok_rows * EP)
    merged = dot(spread_abs, returned, ((1,), (0,)))
    taken = jnp.sum(
        jnp.where(places_abs, back_scores.reshape(1, 1, rows), 0.0), axis=2
    )
    low_cols, high_cols = merged[:, :own_cols], merged[:, own_cols:]
    keep = jnp.where(core == 0, low_cols, high_cols)
    give = jnp.where(core == 0, high_cols, low_cols)
    expert_grad = keep + send(give.astype(BF16), TO_CORE).astype(F32)
    small = jnp.concatenate([router_mine, jnp.pad(taken.T, ((0, 6), (0, 0)))], axis=1)
    small = small + send(small, TO_CORE)
    router_mine, taken = small[:, :chunk], small[:2, chunk:].T
    change = first_gate * second_gate * (taken[:, 0] - taken[:, 1])
    logit_grad = change[:, None] * (chosen_hot[:, 0, :] - chosen_hot[:, 1, :])
    gathered = lax.all_to_all(
        jnp.broadcast_to(router_mine[None], (EP, experts, chunk)), "ep", 0, 0, tiled=True
    )
    grad_router = jnp.transpose(gathered, (1, 0, 2)).reshape(experts, width)

    both = jnp.concatenate([mine_rows, other_rows], axis=0)
    weighted = jnp.concatenate([weighted_mine, weighted_other], axis=0)
    act_grad = jnp.concatenate([act_mine, act_other], axis=0)
    grad_out = dot(weighted, both[:, :width], ((0,), (0,))).astype(BF16)
    grad_in = dot(act_grad, both[:, width : 2 * width], ((0,), (0,))).astype(BF16)

    router_rows = lax.dynamic_slice_in_dim(router_weight, fsdp_index * own_cols, own_cols, 0)
    grad_tokens = (
        expert_grad + jnp.dot(logit_grad, router_rows.T, precision=lax.Precision.HIGHEST)
    ).astype(BF16)
    return grad_tokens, grad_in.T[None], grad_out[None], grad_router.T


def solution(mesh):
    placed = (
        P("ep", None),
        P("ep", None),
        P(),
        P("ep", None, "fsdp"),
        P("ep", "fsdp", None),
        P("ep", None),
        P("ep", None),
    )
    return jax.shard_map(
        per_device,
        mesh=mesh,
        in_specs=placed,
        out_specs=(P("ep", "fsdp"), P("ep", None, "fsdp"), P("ep", "fsdp", None), P()),
        check_vma=False,
    )
```

time: 162 us -> 147 us (0.907)
  starting transfers between devices: 40.2 us -> 30.4 us
  waiting for transfers between devices: 37.1 us -> 32.2 us
    all_to_all x4 -> x2, waiting for transfers between devices: 21.5 us -> 6.38 us  [the longest x1 6.16 us: per_device(): lax.all_to_all(jnp.broadcast_to(router_mine[None], (EP, experts, chunk)),...]
    all_to_all x4 -> x2, starting transfers between devices: 23.3 us -> 8.94 us  [the longest x1 5.48 us: per_device(): lax.all_to_all(jnp.broadcast_to(router_mine[None], (EP, experts, chunk)),...]
    ppermute x11 -> x15, waiting for transfers between devices: 15.6 us -> 25.8 us  [send(): return lax.ppermute(array, 'fsdp', pairs)]
    ppermute x11 -> x15, starting transfers between devices: 17 us -> 21.5 us  [send(): return lax.ppermute(array, 'fsdp', pairs)]
    dynamic_slice x1, local copies, waits for them, and re-layouts: 0.31 us -> 2.16 us  [columns(): return lax.dynamic_slice_in_dim(array, start, size, 1)]
    sub x0 -> x5, other arithmetic: none -> 1.75 us  [the longest x2 1.73 us: act(): second = part_rows[:, 2 * width:2 * width + 1].astype(jnp.int32) - me]
    dot_general x10 -> x18, matrix products: 23.1 us -> 24 us  [dot(): lax.dot_general(left, right, (dims, ((), ())), preferred_element_type=F32)]
  transfers between devices with their start and end apart: 15 -> 17, of which waited for: 8 -> 10; matrix products, arithmetic and copies ran while one was open for 7% -> 15% of each run, Pallas kernels for 0% -> 0%
where the time goes in v3:
time: 147 us; the launch traced here: 146 us
  blocking collectives  46.3 us (31%)
  waiting for transfers between devices  32.2 us (22%)
  starting transfers between devices  30.4 us (21%)
  matrix products  24.4 us (17%)
  other arithmetic  6.96 us (5%)
  local copies, waits for them, and re-layouts  4.5 us (3%)
    all_to_all x1, blocking collectives, per_device(): lax.all_to_all(send_rows.reshape(experts, half, 2 * width + 128), 'ep', 0...  46.3 us
    ppermute x15, waiting for transfers between devices, send(): return lax.ppermute(array, 'fsdp', pairs)  25.8 us
    dot_general x18, matrix products, dot(): lax.dot_general(left, right, (dims, ((), ())), preferred_element_type=F32)  24 us
    ppermute x15, starting transfers between devices, send(): return lax.ppermute(array, 'fsdp', pairs)  21.5 us
    all_to_all x1, waiting for transfers between devices, per_device(): lax.all_to_all(jnp.broadcast_to(router_mine[None], (EP, experts, chunk)),...  6.16 us
    all_to_all x1, starting transfers between devices, per_device(): lax.all_to_all(jnp.broadcast_to(router_mine[None], (EP, experts, chunk)),...  5.48 us
    all_to_all x1, starting transfers between devices, per_device(): lax.all_to_all(jnp.concatenate([pack(own, own_score).reshape(experts, hal...  3.45 us
  transfers between devices with their start and end apart: 17, of which 10 were waited for; matrix products, arithmetic and copies ran while one was open for 15% of the time, Pallas kernels for 0%

profile of v3, /device:TPU:1, one launch (start us, length us, event | category | flops | bytes accessed | tf_op | source)
XLA Modules:
  0.0 146.1 jit_solution(6228269637769424483)
XLA Ops:
  1.7 2.9 %convolution_convert_fusion = bf16[128,12416]{1,0:T(8,128)(2,1)S(1)} fusion(bf16[128,128]{1,0:T(8,128)(2,1)S(1)} %broadcast_in_dim.188, bf16[128,6144]{1,0:T(8,128)(2,1)} %param.7, bf16[128,6144]{1,0:T(8,128)(2,1)} %param.8, pred[128,2,128]{2,0,1:T(32,128)(4,1)S(1)} %iota_compare_fusion.1), kind=kOutput, calls=%fused_computation | convolution fusion | flops 417988608 | bytes 6389760 | tf_op jit(solution)/shard_map/dot_general | solution.py:33
  4.6 46.3 %all_to_all.15 = bf16[8,16,12416]{2,1,0:T(8,128)(2,1)} all-to-all(bf16[8,16,12416]{2,1,0:T(8,128)(2,1)S(1)} %bitcast.126), channel_id=1, replica_groups=mesh['fsdp'=32,'ep'=8] {'ep'}, dimensions={0} | all-to-all | bytes 6356992 | tf_op jit(solution)/shard_map/all_to_all | solution.py:81
  51.0 2.2 %collective-permute-start = (bf16[128,12416]{1,0:T(8,128)(2,1)}, bf16[128,12416]{1,0:T(8,128)(2,1)}, u32[]{:S(2)}, u32[]{:S(2)}) collective-permute-start(bf16[128,12416]{1,0:T(8,128)(2,1)} %bitcast.2), channel_id=1, source_target_pairs={{0,8},{8,0},{16,24},{24,16},{32,40},{40,32},{48,56},{56,48},{64,72... | collective-permute-start | bytes 9535496 | tf_op jit(solution)/shard_map/ppermute | solution.py:29
  53.2 2.2 %dynamic-slice_bitcast_fusion.3 = (bf16[168,384]{1,0:T(8,128)(2,1)S(1)}, bf16[168,384]{1,0:T(8,128)(2,1)S(1)}, bf16[168,384]{1,0:T(8,128)(2,1)S(1)}, bf16[168,38...) fusion(bf16[1,6144,168]{1,2,0:T(8,128)(2,1)} %param.10, ...), kind=kLoop, calls=%fused_computation.90 | loop fusion | bytes 4128832 | tf_op jit(solution)/shard_map/dynamic_slice | solution.py:45
  56.9 2.2 %fusion.19 = f32[128,192]{0,1:T(8,128)S(1)} fusion(bf16[24,6144]{1,0:T(8,128)(2,1)S(1)} %fusion.35, bf16[168,6144]{1,0:T(8,128)(2,1)S(1)} %bitcast.127, bf16[128,12416]{1,0:T(8,128)(2,1)} %bitcast.2), kind=kOutput, calls=%fused_computation.28 | convolution fusion | flops 306708480 | bytes 4030464 | tf_op jit(solution)/shard_map/dot_general | solution.py:33
  59.1 2.2 %fusion.16 = f32[128,192]{0,1:T(8,128)S(1)} fusion(bf16[128,12416]{1,0:T(8,128)(2,1)} %collective-permute-done, bf16[24,6144]{1,0:T(8,128)(2,1)S(1)} %fusion.35, bf16[168,6144]{1,0:T(8,128)(2,1)S(1)} %bitcast.128), kind=kOutput, calls=%fused_computation.25 | convolution fusion | flops 306708480 | bytes 4030464 | tf_op jit(solution)/shard_map/dot_general | solution.py:33
  62.3 2.1 %fusion.43 = (bf16[128,168]{0,1:T(8,128)(2,1)S(1)}, bf16[128,168]{0,1:T(8,128)(2,1)S(1)}, bf16[128,168]{0,1:T(8,128)(2,1)S(1)}, f32[128,168]{0,1:T(8,128)S(1)}) fusion(f32[128]{0:T(128)S(1)} %get-tuple-element.104, f32[128,192]{0,1:T(8,128)S(1)} %fusion.16, bf16[1,168,6144]{2,1,0:T(8,128)(2,1)S(1)} %copy-done, bf16[128,12416]{1,0:T(8,128)(2,1)} %collective-permute-done), kind=kOutput, calls=%fused_computation.115 | convolution fusion | flops 264563712 | bytes 3938816 | tf_op jit(solution)/shard_map/dot_general | solution.py:33
  67.2 2.1 %fusion.45 = (bf16[128,168]{0,1:T(8,128)(2,1)S(1)}, bf16[128,168]{0,1:T(8,128)(2,1)S(1)}, bf16[128,168]{0,1:T(8,128)(2,1)S(1)}, f32[128,168]{0,1:T(8,128)S(1)}) fusion(f32[128]{0:T(128)S(1)} %convert_element_type.366, f32[128,192]{0,1:T(8,128)S(1)} %fusion.19, bf16[1,168,6144]{2,1,0:T(8,128)(2,1)S(1)} %copy-done, bf16[128,12416]{1,0:T(8,128)(2,1)} %bitcast.2), kind=kOutput, calls=%fused_computation.117 | convolution fusion | flops 264563712 | bytes 3938816 | tf_op jit(solution)/shard_map/dot_general | solution.py:33
  70.0 5.6 %collective-permute-start.4 = (bf16[128,896]{1,0:T(8,128)(2,1)S(1)}, bf16[128,896]{1,0:T(8,128)(2,1)S(1)}, u32[]{:S(2)}, u32[]{:S(2)}) collective-permute-start(bf16[128,896]{1,0:T(8,128)(2,1)S(1)} %get-tuple-element.11), channel_id=1, source_target_pairs={{0,112},{8,120},{16,0},{24,8},{32,16},{40,24},{48,32},{56,40},{64,... | collective-permute-start | bytes 688136 | tf_op jit(solution)/shard_map/ppermute | solution.py:29
  76.0 4.6 %collective-permute-done.4 = bf16[128,896]{1,0:T(8,128)(2,1)S(1)} collective-permute-done((bf16[128,896]{1,0:T(8,128)(2,1)S(1)}, bf16[128,896]{1,0:T(8,128)(2,1)S(1)}, u32[]{:S(2)}, u32[]{:S(2)}) %collective-permute-start.4) | collective-permute-done | bytes 229408 | tf_op jit(solution)/shard_map/ppermute | solution.py:29
  80.7 3.0 %collective-permute-done.2 = bf16[128,896]{1,0:T(8,128)(2,1)S(1)} collective-permute-done((bf16[128,896]{1,0:T(8,128)(2,1)S(1)}, bf16[128,896]{1,0:T(8,128)(2,1)S(1)}, u32[]{:S(2)}, u32[]{:S(2)}) %collective-permute-start.2) | collective-permute-done | bytes 229408 | tf_op jit(solution)/shard_map/ppermute | solution.py:29
  85.9 4.1 %collective-permute-done.7 = bf16[128,896]{1,0:T(8,128)(2,1)S(1)} collective-permute-done((bf16[128,896]{1,0:T(8,128)(2,1)S(1)}, bf16[128,896]{1,0:T(8,128)(2,1)S(1)}, u32[]{:S(2)}, u32[]{:S(2)}) %collective-permute-start.7) | collective-permute-done | bytes 229408 | tf_op jit(solution)/shard_map/ppermute | solution.py:29
  90.1 1.6 %collective-permute-done.5 = bf16[128,896]{1,0:T(8,128)(2,1)S(1)} collective-permute-done((bf16[128,896]{1,0:T(8,128)(2,1)S(1)}, bf16[128,896]{1,0:T(8,128)(2,1)S(1)}, u32[]{:S(2)}, u32[]{:S(2)}) %collective-permute-start.5) | collective-permute-done | bytes 229408 | tf_op jit(solution)/shard_map/ppermute | solution.py:29
  92.6 2.7 %collective-permute-start.11 = (bf16[128,896]{1,0:T(8,128)(2,1)S(1)}, bf16[128,896]{1,0:T(8,128)(2,1)S(1)}, u32[]{:S(2)}, u32[]{:S(2)}) collective-permute-start(bf16[128,896]{1,0:T(8,128)(2,1)S(1)} %pad_maximum_fusion.16), channel_id=1, source_target_pairs={{0,112},{8,120},{16,0},{24,8},{32,16},{40,24},{48,32},{56,40},{64,... | collective-permute-start | bytes 688136 | tf_op jit(solution)/shard_map/ppermute | solution.py:29
  95.3 3.0 %collective-permute-done.8 = bf16[128,896]{1,0:T(8,128)(2,1)S(1)} collective-permute-done((bf16[128,896]{1,0:T(8,128)(2,1)S(1)}, bf16[128,896]{1,0:T(8,128)(2,1)S(1)}, u32[]{:S(2)}, u32[]{:S(2)}) %collective-permute-start.8) | collective-permute-done | bytes 229408 | tf_op jit(solution)/shard_map/ppermute | solution.py:29
  98.9 5.9 %collective-permute-done.10 = bf16[128,896]{1,0:T(8,128)(2,1)S(1)} collective-permute-done((bf16[128,896]{1,0:T(8,128)(2,1)S(1)}, bf16[128,896]{1,0:T(8,128)(2,1)S(1)}, u32[]{:S(2)}, u32[]{:S(2)}) %collective-permute-start.10) | collective-permute-done | bytes 229408 | tf_op jit(solution)/shard_map/ppermute | solution.py:29
  106.1 3.1 %collective-permute-done.12 = bf16[128,512]{1,0:T(8,128)(2,1)S(1)} collective-permute-done((bf16[128,512]{1,0:T(8,128)(2,1)S(1)}, bf16[128,512]{1,0:T(8,128)(2,1)S(1)}, u32[]{:S(2)}, u32[]{:S(2)}) %collective-permute-start.12) | collective-permute-done | bytes 131104 | tf_op jit(solution)/shard_map/ppermute | solution.py:29
  109.4 1.7 %fusion.20 = f32[24,6144]{1,0:T(8,128)S(1)} fusion(bf16[128,12416]{1,0:T(8,128)(2,1)} %bitcast.2, bf16[128,8]{0,1:T(8,128)(2,1)S(1)} %get-tuple-element.78, bf16[128,8]{0,1:T(8,128)(2,1)S(1)} %get-tuple-element.79, bf16[128,8]{0,1:T(8,128)(2,1)S(1)} %get-tuple-element.77), kind=kOutput, calls=%fused_computation.29 | convolution fusion | flops 37767168 | bytes 2168832 | tf_op jit(solution)/shard_map/dot_general | solution.py:33
  112.2 3.5 %all-to-all-start.1 = ((bf16[8,48,512]{2,1,0:T(8,128)(2,1)}), bf16[8,48,512]{2,1,0:T(8,128)(2,1)S(1)}, u32[]{:S(2)}, u32[]{:S(2)}) async-start(bf16[8,48,512]{2,1,0:T(8,128)(2,1)} %fusion.25), calls=%async_computation.1 | async-start | bytes 786432 | tf_op jit(solution)/shard_map/all_to_all | solution.py:173
  115.7 3.9 %fusion.1 = bf16[1,168,6144]{2,1,0:T(8,128)(2,1)} fusion(bf16[128,12416]{1,0:T(8,128)(2,1)} %collective-permute-done, bf16[128,12416]{1,0:T(8,128)(2,1)} %bitcast.2, bf16[128,168]{0,1:T(8,128)(2,1)S(1)} %get-tuple-element.36, bf16[128,168]{0,1:T(8,128)(2,1)S(1)} %get-tuple-element.34), kind=kOutput, calls=%fused_computation.4 | convolution fusion | flops 535977984 | bytes 8507392 | tf_op jit(solution)/shard_map/dot_general | solution.py:33
  119.6 3.9 %fusion = bf16[1,6144,168]{1,2,0:T(8,128)(2,1)} fusion(bf16[128,12416]{1,0:T(8,128)(2,1)} %collective-permute-done, bf16[128,12416]{1,0:T(8,128)(2,1)} %bitcast.2, bf16[128,168]{0,1:T(8,128)(2,1)S(1)} %get-tuple-element.74, bf16[128,168]{0,1:T(8,128)(2,1)S(1)} %get-tuple-element.73), kind=kOutput, calls=%fused_computation.3 | convolution fusion | flops 535977984 | bytes 8507392 | tf_op jit(solution)/shard_map/dot_general | solution.py:33
  124.3 6.8 %collective-permute-start.14 = (f32[8,896]{1,0:T(8,128)S(1)}, f32[8,896]{1,0:T(8,128)S(1)}, u32[]{:S(2)}, u32[]{:S(2)}) collective-permute-start(f32[8,896]{1,0:T(8,128)S(1)} %select_maximum_fusion), channel_id=1, source_target_pairs={{0,8},{8,0},{16,24},{24,16},{32,40},{40,32},{48,56},{56,48},{64,72... | collective-permute-start | bytes 86024 | tf_op jit(solution)/shard_map/ppermute | solution.py:29
  132.7 5.5 %all-to-all-start.2 = ((f32[8,8,768]{2,1,0:T(8,128)}), f32[8,8,768]{2,1,0:T(8,128)S(1)}, u32[]{:S(2)}, u32[]{:S(2)}) async-start(f32[8,8,768]{2,1,0:T(8,128)} %broadcast_in_dim.214), calls=%async_computation.2 | async-start | bytes 393216 | tf_op jit(solution)/shard_map/all_to_all | solution.py:209
  139.3 6.2 %all-to-all-done.2 = f32[8,8,768]{2,1,0:T(8,128)S(1)} async-done(((f32[8,8,768]{2,1,0:T(8,128)}), f32[8,8,768]{2,1,0:T(8,128)S(1)}, u32[]{:S(2)}, u32[]{:S(2)}) %all-to-all-start.2) | async-done | bytes 196640 | tf_op jit(solution)/shard_map/all_to_all | solution.py:209
  (132 shorter events, 17.6 us)
Async XLA Ops:
  0.6 61.7 %copy-start = (bf16[1,168,6144]{2,1,0:T(8,128)(2,1)S(1)}, bf16[1,168,6144]{2,1,0:T(8,128)(2,1)}, u32[]{:S(2)}) copy-start(bf16[1,168,6144]{2,1,0:T(8,128)(2,1)} %param.11) | copy-start | bytes 6193156
  51.0 4.4 %copy-start.3 = (f32[6144,8]{0,1:T(8,128)S(1)}, f32[6144,8]{0,1:T(8,128)}, u32[]{:S(2)}) copy-start(f32[6144,8]{0,1:T(8,128)} %param.9) | copy-start | bytes 589828
  51.0 8.2 %collective-permute-start = (bf16[128,12416]{1,0:T(8,128)(2,1)}, bf16[128,12416]{1,0:T(8,128)(2,1)}, u32[]{:S(2)}, u32[]{:S(2)}) collective-permute-start(bf16[128,12416]{1,0:T(8,128)(2,1)} %bitcast.2), channel_id=1, source_target_pairs={{0,8},{8,0},{16,24},{24,16},{32,40},{40,32},{48,56},{56,48},{64,72... | collective-permute-start | bytes 9535496 | tf_op jit(solution)/shard_map/ppermute | solution.py:29
  53.2 2.3 %copy-start.2 = (bf16[128,6144]{1,0:T(8,128)(2,1)S(1)}, bf16[128,6144]{1,0:T(8,128)(2,1)}, u32[]{:S(2)}) copy-start(bf16[128,6144]{1,0:T(8,128)(2,1)} %param.7) | copy-start | bytes 4718596
  53.2 3.7 %copy-start.1 = (bf16[1,6144,168]{1,2,0:T(8,128)(2,1)S(1)}, bf16[1,6144,168]{1,2,0:T(8,128)(2,1)}, u32[]{:S(2)}) copy-start(bf16[1,6144,168]{1,2,0:T(8,128)(2,1)} %param.10) | copy-start | bytes 6193156
  64.9 4.4 %collective-permute-start.1 = (bf16[128,1664]{1,0:T(8,128)(2,1)S(1)}, bf16[128,1664]{1,0:T(8,128)(2,1)S(1)}, u32[]{:S(2)}, u32[]{:S(2)}) collective-permute-start(bf16[128,1664]{1,0:T(8,128)(2,1)S(1)} %pad_maximum_fusion.9), channel_id=1, source_target_pairs={{0,8},{8,0},{16,24},{24,16},{32,40},{40,32},{48,56},{56,48},{64,72... | collective-permute-start | bytes 1277960 | tf_op jit(solution)/shard_map/ppermute | solution.py:29
  65.4 10.2 %collective-permute-start.3 = (bf16[128,1536]{1,0:T(8,128)(2,1)S(1)}, bf16[128,1536]{1,0:T(8,128)(2,1)S(1)}, u32[]{:S(2)}, u32[]{:S(2)}) collective-permute-start(bf16[128,1536]{1,0:T(8,128)(2,1)S(1)} %convolution_convert_fusion.5), channel_id=1, source_target_pairs={{0,8},{8,0},{16,24},{24,16},{32,40},{40,32},{48,56},{56,48},{64,72... | collective-permute-start | bytes 1179656 | tf_op jit(solution)/shard_map/ppermute | solution.py:29
  66.2 19.4 %collective-permute-start.6 = (bf16[128,1536]{1,0:T(8,128)(2,1)S(1)}, bf16[128,1536]{1,0:T(8,128)(2,1)S(1)}, u32[]{:S(2)}, u32[]{:S(2)}) collective-permute-start(bf16[128,1536]{1,0:T(8,128)(2,1)S(1)} %convolution_convert_fusion.4), channel_id=1, source_target_pairs={{0,8},{8,0},{16,24},{24,16},{32,40},{40,32},{48,56},{56,48},{64,72... | collective-permute-start | bytes 1179656 | tf_op jit(solution)/shard_map/ppermute | solution.py:29
  66.7 25.5 %collective-permute-start.9 = (bf16[128,1536]{1,0:T(8,128)(2,1)S(1)}, bf16[128,1536]{1,0:T(8,128)(2,1)S(1)}, u32[]{:S(2)}, u32[]{:S(2)}) collective-permute-start(bf16[128,1536]{1,0:T(8,128)(2,1)S(1)} %convolution_convert_fusion.3), channel_id=1, source_target_pairs={{0,8},{8,0},{16,24},{24,16},{32,40},{40,32},{48,56},{56,48},{64,72... | collective-permute-start | bytes 1179656 | tf_op jit(solution)/shard_map/ppermute | solution.py:29
  70.0 10.5 %collective-permute-start.4 = (bf16[128,896]{1,0:T(8,128)(2,1)S(1)}, bf16[128,896]{1,0:T(8,128)(2,1)S(1)}, u32[]{:S(2)}, u32[]{:S(2)}) collective-permute-start(bf16[128,896]{1,0:T(8,128)(2,1)S(1)} %get-tuple-element.11), channel_id=1, source_target_pairs={{0,112},{8,120},{16,0},{24,8},{32,16},{40,24},{48,32},{56,40},{64,... | collective-permute-start | bytes 688136 | tf_op jit(solution)/shard_map/ppermute | solution.py:29
  75.7 8.0 %collective-permute-start.2 = (bf16[128,896]{1,0:T(8,128)(2,1)S(1)}, bf16[128,896]{1,0:T(8,128)(2,1)S(1)}, u32[]{:S(2)}, u32[]{:S(2)}) collective-permute-start(bf16[128,896]{1,0:T(8,128)(2,1)S(1)} %get-tuple-element.10), channel_id=1, source_target_pairs={{0,16},{8,24},{16,32},{24,40},{32,48},{40,56},{48,64},{56,72},{64,... | collective-permute-start | bytes 688136 | tf_op jit(solution)/shard_map/ppermute | solution.py:29
  84.1 5.9 %collective-permute-start.7 = (bf16[128,896]{1,0:T(8,128)(2,1)S(1)}, bf16[128,896]{1,0:T(8,128)(2,1)S(1)}, u32[]{:S(2)}, u32[]{:S(2)}) collective-permute-start(bf16[128,896]{1,0:T(8,128)(2,1)S(1)} %pad_maximum_fusion.14), channel_id=1, source_target_pairs={{0,112},{8,120},{16,0},{24,8},{32,16},{40,24},{48,32},{56,40},{64,... | collective-permute-start | bytes 688136 | tf_op jit(solution)/shard_map/ppermute | solution.py:29
  84.6 7.1 %collective-permute-start.5 = (bf16[128,896]{1,0:T(8,128)(2,1)S(1)}, bf16[128,896]{1,0:T(8,128)(2,1)S(1)}, u32[]{:S(2)}, u32[]{:S(2)}) collective-permute-start(bf16[128,896]{1,0:T(8,128)(2,1)S(1)} %pad_maximum_fusion.13), channel_id=1, source_target_pairs={{0,16},{8,24},{16,32},{24,40},{32,48},{40,56},{48,64},{56,72},{64,... | collective-permute-start | bytes 688136 | tf_op jit(solution)/shard_map/ppermute | solution.py:29
  91.9 6.8 %copy-start.4 = (s32[128,2]{0,1:T(2,128)S(1)}, s32[128,2]{0,1:T(2,128)}, u32[]{:S(2)}) copy-start(s32[128,2]{0,1:T(2,128)} %param.12) | copy-start | bytes 3076
  92.2 6.2 %collective-permute-start.8 = (bf16[128,896]{1,0:T(8,128)(2,1)S(1)}, bf16[128,896]{1,0:T(8,128)(2,1)S(1)}, u32[]{:S(2)}, u32[]{:S(2)}) collective-permute-start(bf16[128,896]{1,0:T(8,128)(2,1)S(1)} %pad_maximum_fusion.15), channel_id=1, source_target_pairs={{0,16},{8,24},{16,32},{24,40},{32,48},{40,56},{48,64},{56,72},{64,... | collective-permute-start | bytes 688136 | tf_op jit(solution)/shard_map/ppermute | solution.py:29
  92.6 6.2 %collective-permute-start.11 = (bf16[128,896]{1,0:T(8,128)(2,1)S(1)}, bf16[128,896]{1,0:T(8,128)(2,1)S(1)}, u32[]{:S(2)}, u32[]{:S(2)}) collective-permute-start(bf16[128,896]{1,0:T(8,128)(2,1)S(1)} %pad_maximum_fusion.16), channel_id=1, source_target_pairs={{0,112},{8,120},{16,0},{24,8},{32,16},{40,24},{48,32},{56,40},{64,... | collective-permute-start | bytes 688136 | tf_op jit(solution)/shard_map/ppermute | solution.py:29
  98.7 6.2 %collective-permute-start.10 = (bf16[128,896]{1,0:T(8,128)(2,1)S(1)}, bf16[128,896]{1,0:T(8,128)(2,1)S(1)}, u32[]{:S(2)}, u32[]{:S(2)}) collective-permute-start(bf16[128,896]{1,0:T(8,128)(2,1)S(1)} %pad_maximum_fusion.17), channel_id=1, source_target_pairs={{0,16},{8,24},{16,32},{24,40},{32,48},{40,56},{48,64},{56,72},{64,... | collective-permute-start | bytes 688136 | tf_op jit(solution)/shard_map/ppermute | solution.py:29
  105.2 3.9 %collective-permute-start.12 = (bf16[128,512]{1,0:T(8,128)(2,1)S(1)}, bf16[128,512]{1,0:T(8,128)(2,1)S(1)}, u32[]{:S(2)}, u32[]{:S(2)}) collective-permute-start(bf16[128,512]{1,0:T(8,128)(2,1)S(1)} %pad_maximum_fusion.18), channel_id=1, source_target_pairs={{0,128},{8,136},{16,144},{24,152},{32,160},{40,168},{48,176},{56,1... | collective-permute-start | bytes 393224 | tf_op jit(solution)/shard_map/ppermute | solution.py:29
  112.2 11.5 %all-to-all-start.1 = ((bf16[8,48,512]{2,1,0:T(8,128)(2,1)}), bf16[8,48,512]{2,1,0:T(8,128)(2,1)S(1)}, u32[]{:S(2)}, u32[]{:S(2)}) async-start(bf16[8,48,512]{2,1,0:T(8,128)(2,1)} %fusion.25), calls=%async_computation.1 | async-start | bytes 786432 | tf_op jit(solution)/shard_map/all_to_all | solution.py:173
  124.3 7.7 %collective-permute-start.14 = (f32[8,896]{1,0:T(8,128)S(1)}, f32[8,896]{1,0:T(8,128)S(1)}, u32[]{:S(2)}, u32[]{:S(2)}) collective-permute-start(f32[8,896]{1,0:T(8,128)S(1)} %select_maximum_fusion), channel_id=1, source_target_pairs={{0,8},{8,0},{16,24},{24,16},{32,40},{40,32},{48,56},{56,48},{64,72... | collective-permute-start | bytes 86024 | tf_op jit(solution)/shard_map/ppermute | solution.py:29
  131.2 7.0 %collective-permute-start.13 = (bf16[128,192]{1,0:T(8,128)(2,1)S(1)}, bf16[128,192]{1,0:T(8,128)(2,1)S(1)}, u32[]{:S(2)}, u32[]{:S(2)}) collective-permute-start(bf16[128,192]{1,0:T(8,128)(2,1)S(1)} %select_convert_fusion), channel_id=1, source_target_pairs={{0,8},{8,0},{16,24},{24,16},{32,40},{40,32},{48,56},{56,48},{64,72... | collective-permute-start | bytes 147464 | tf_op jit(solution)/shard_map/ppermute | solution.py:29
  132.7 12.8 %all-to-all-start.2 = ((f32[8,8,768]{2,1,0:T(8,128)}), f32[8,8,768]{2,1,0:T(8,128)S(1)}, u32[]{:S(2)}, u32[]{:S(2)}) async-start(f32[8,8,768]{2,1,0:T(8,128)} %broadcast_in_dim.214), calls=%async_computation.2 | async-start | bytes 393216 | tf_op jit(solution)/shard_map/all_to_all | solution.py:209

commit v4 on v3

--- a/solution.py
+++ b/solution.py
@@ -23,6 +23,8 @@
 TO_UP = fsdp_pairs(lambda lo, z, core: (lo, z + 1, core))
 TO_DOWN = fsdp_pairs(lambda lo, z, core: (lo, z - 1, core))
 TO_SIDE = fsdp_pairs(lambda lo, z, core: (lo + 1, z, core))
+
+TO_CROSS = fsdp_pairs(lambda lo, z, core: (lo + 1, z, core + 1))
 
 
 def send(array, pairs):
@@ -62,6 +64,18 @@
     w_in = expert_in[0].T
     w_out = expert_out[0]
 
+    key_abs = jnp.where((slots // half == core) & (slots >= 0), choices * half + slots % half, -1)
+    places_abs = key_abs[:, :, None] == jnp.arange(rows, dtype=jnp.int32)
+    spread_abs = (places_abs[:, 0] | places_abs[:, 1]).astype(BF16)
+    both_choices = jnp.broadcast_to(
+        jnp.sum(choices, axis=1, keepdims=True).astype(BF16), (tok_rows, 128)
+    )
+    packed = jnp.concatenate([out_grad, tokens, both_choices], axis=1)
+    send_rows = dot(spread_abs, packed, ((0,), (0,))).astype(BF16)
+    send_rows, w_in, router_weight = lax.optimization_barrier((send_rows, w_in, router_weight))
+    mine_rows = lax.all_to_all(
+        send_rows.reshape(experts, half, 2 * width + 128), "ep", 0, 0, tiled=True
+    ).reshape(rows, 2 * width + 128)
     router_parts = jnp.concatenate(split3(router_weight), axis=1)
     logits = dot(tokens, router_parts, ((1,), (0,)))
     logits = (logits[:, :experts] + logits[:, experts : 2 * experts]) + logits[:, 2 * experts :]
@@ -70,19 +84,19 @@
     first_gate = 1.0 / (1.0 + jnp.exp(chosen[:, 1] - chosen[:, 0]))
     second_gate = 1.0 / (1.0 + jnp.exp(chosen[:, 0] - chosen[:, 1]))
 
-    key_abs = jnp.where((slots // half == core) & (slots >= 0), choices * half + slots % half, -1)
-    places_abs = key_abs[:, :, None] == jnp.arange(rows, dtype=jnp.int32)
-    spread_abs = (places_abs[:, 0] | places_abs[:, 1]).astype(BF16)
-    both_choices = jnp.broadcast_to(
-        jnp.sum(choices, axis=1, keepdims=True).astype(BF16), (tok_rows, 128)
-    )
-    packed = jnp.concatenate([out_grad, tokens, both_choices], axis=1)
-    send_rows = dot(spread_abs, packed, ((0,), (0,))).astype(BF16)
-    mine_rows = lax.all_to_all(
-        send_rows.reshape(experts, half, 2 * width + 128), "ep", 0, 0, tiled=True
-    ).reshape(rows, 2 * width + 128)
+    w_ext = jnp.concatenate([w_in, router_parts.T], axis=0)
+
+    def weights(k):
+        at = (z + k) % Z
+        return [columns(w_in, ((lo ^ d) * Z + at) * seg, seg) for d in range(2)]
+
+    orders = [(4, 5), (3, 6), (2, 7), (1, 0)]
+    near = [jnp.concatenate(weights(a) + weights(b), axis=1) for a, b in orders]
+
+    mine_rows, w_ext, near, first_gate, second_gate, chosen_hot = lax.optimization_barrier(
+        (mine_rows, w_ext, near, first_gate, second_gate, chosen_hot)
+    )
     other_rows = send(mine_rows, TO_CORE)
-    w_ext = jnp.concatenate([w_in, router_parts.T], axis=0)
     hidden_count = w_in.shape[0]
 
     def act(part_rows):
@@ -106,31 +120,26 @@
         sig = jax.nn.sigmoid(pre)
         hidden = (pre * sig).astype(BF16)
         hid_wide = hidden.astype(F32)
-        score = jnp.sum(hid_wide * back, axis=1, keepdims=True)
+        score = jnp.sum(hid_wide * back, axis=1)[None]
         weighted = (hid_wide * gate).astype(BF16)
         act_grad = (gate * back * sig * (1.0 + pre * (1.0 - sig))).astype(BF16)
         slopes = slope * ((ids == me).astype(F32) - (ids == second).astype(F32))
         return score, weighted, act_grad, slopes
 
-    score_mine, weighted_mine, act_mine, slopes_mine = act(mine_rows)
-    score_other, weighted_other, act_other, _ = act(other_rows)
-
-    def weights(k):
-        at = (z + k) % Z
-        return [columns(w_in, ((lo ^ d) * Z + at) * seg, seg) for d in range(2)]
-
-    orders = [(4, 5), (3, 6), (2, 7), (1, 0)]
-    near = [jnp.concatenate(weights(a) + weights(b), axis=1) for a, b in orders]
+    done_mine = act(mine_rows)
+    other_rows, done_mine = lax.optimization_barrier((other_rows, done_mine))
+    score_mine, weighted_mine, act_mine, slopes_mine = done_mine
+    score_other, weighted_other, act_other, slopes_other = act(other_rows)
 
     def pack(grads, score):
         high = lax.reduce_precision(score, 8, 7)
-        lane = lax.broadcasted_iota(jnp.int32, (rows, 128), 1)
-        block = jnp.where(lane == 0, high, jnp.where(lane == 1, score - high, 0.0))
-        return jnp.concatenate([grads.astype(BF16), block.astype(BF16)], axis=1)
+        block = jnp.concatenate([high, score - high], axis=0)
+        block = jnp.pad(block, ((0, 6), (0, grads.shape[1] - rows)))
+        return jnp.concatenate([grads, block], axis=0).astype(BF16)
 
     def unpack(packed):
         wide = packed.astype(F32)
-        return wide[:, :-128], jnp.sum(wide[:, -128:], axis=1, keepdims=True)
+        return wide[:rows], jnp.sum(wide[rows:, :rows], axis=0, keepdims=True)
 
     first_other = dot(act_other, near[0], ((1,), (0,)))
     got, got_score = unpack(send(pack(first_other, score_other), TO_CORE))
@@ -153,34 +162,32 @@
     total, total_score = last + down, last_score + down_score
     side, side_score = unpack(send(pack(total[:, seg:], total_score), TO_SIDE))
     own, own_score = total[:, :seg] + side, total_score + side_score
-
+    other_score = send(total_score, TO_CORE) + send(total_score, TO_CROSS)
+
+    row_scores = jnp.concatenate([own_score, other_score], axis=1).reshape(2 * rows, 1)
+    slopes = jnp.concatenate([slopes_mine, slopes_other], axis=0)
+    both = jnp.concatenate([mine_rows, other_rows], axis=0)
+    core_cols = width // 2
     router_part = dot(
-        jnp.concatenate(split3(slopes_mine * own_score), axis=1),
-        mine_rows[:, width : 2 * width],
+        jnp.concatenate(split3(slopes * row_scores), axis=1),
+        columns(both, width + core * core_cols, core_cols),
         ((0,), (0,)),
     )
     router_part = (router_part[:experts] + router_part[experts : 2 * experts]) + router_part[
         2 * experts :
     ]
-    chunk = width // EP
-
-    def two(array):
-        high = lax.reduce_precision(array, 8, 7)
-        return jnp.stack([high, array - high]).astype(BF16)
-
-    chunks = jnp.transpose(two(router_part).reshape(2, experts, EP, chunk), (2, 0, 1, 3))
-
+
+    score_high = lax.reduce_precision(own_score, 8, 7)
+    score_rows = jnp.concatenate([score_high, own_score - score_high], axis=0)
+    score_rows = jnp.transpose(score_rows.reshape(2, experts, half), (1, 0, 2))
+    score_rows = jnp.pad(score_rows, ((0, 0), (0, 6), (0, seg - half))).astype(BF16)
+    router_rows = router_part.astype(BF16).reshape(-1, seg)
     home = lax.all_to_all(
         jnp.concatenate(
             [
-                pack(own, own_score).reshape(experts, half, seg + 128),
-                jnp.concatenate(
-                    [
-                        chunks.reshape(EP, -1, seg),
-                        jnp.zeros((EP, 2 * experts * chunk // seg, 128), BF16),
-                    ],
-                    axis=2,
-                ),
+                own.astype(BF16).reshape(experts, half, seg),
+                score_rows,
+                jnp.broadcast_to(router_rows[None], (EP,) + router_rows.shape),
             ],
             axis=1,
         ),
@@ -189,10 +196,10 @@
         0,
         tiled=True,
     )
-    returned, back_scores = unpack(home[:, :half].reshape(rows, seg + 128))
-    router_mine = jnp.sum(
-        home[:, half:, :seg].reshape(EP, 2, experts, chunk).astype(F32), axis=(0, 1)
-    ) / (tok_rows * EP)
+    returned = home[:, :half].reshape(rows, seg)
+    back_scores = jnp.sum(home[:, half : half + 8, :half].astype(F32), axis=1)
+    router_mine = jnp.sum(home[:, half + 8 :].astype(F32), axis=0) / (tok_rows * EP)
+    router_mine = router_mine.reshape(experts, core_cols)
     merged = dot(spread_abs, returned, ((1,), (0,)))
     taken = jnp.sum(
         jnp.where(places_abs, back_scores.reshape(1, 1, rows), 0.0), axis=2
@@ -202,16 +209,19 @@
     give = jnp.where(core == 0, high_cols, low_cols)
     expert_grad = keep + send(give.astype(BF16), TO_CORE).astype(F32)
     small = jnp.concatenate([router_mine, jnp.pad(taken.T, ((0, 6), (0, 0)))], axis=1)
-    small = small + send(small, TO_CORE)
-    router_mine, taken = small[:, :chunk], small[:2, chunk:].T
+    got_small = send(small, TO_CORE)
+    taken = (taken.T + got_small[:2, core_cols:]).T
+    router_other = got_small[:, :core_cols]
+    grad_router = jnp.concatenate(
+        [
+            jnp.where(core == 0, router_mine, router_other),
+            jnp.where(core == 0, router_other, router_mine),
+        ],
+        axis=1,
+    )
     change = first_gate * second_gate * (taken[:, 0] - taken[:, 1])
     logit_grad = change[:, None] * (chosen_hot[:, 0, :] - chosen_hot[:, 1, :])
-    gathered = lax.all_to_all(
-        jnp.broadcast_to(router_mine[None], (EP, experts, chunk)), "ep", 0, 0, tiled=True
-    )
-    grad_router = jnp.transpose(gathered, (1, 0, 2)).reshape(experts, width)
-
-    both = jnp.concatenate([mine_rows, other_rows], axis=0)
+
     weighted = jnp.concatenate([weighted_mine, weighted_other], axis=0)
     act_grad = jnp.concatenate([act_mine, act_other], axis=0)
     grad_out = dot(weighted, both[:, :width], ((0,), (0,))).astype(BF16)

time: 147 us -> 133 us (0.905)
  blocking collectives: 46.3 us -> 0 us
  waiting for transfers between devices: 32.2 us -> 55 us
  starting transfers between devices: 30.4 us -> 35.5 us
  local copies, waits for them, and re-layouts: 4.5 us -> 6.97 us
  other arithmetic: 6.96 us -> 8.5 us
    all_to_all x1 -> x0, blocking collectives: 46.3 us -> none  [per_device(): lax.all_to_all(send_rows.reshape(experts, half, 2 * width + 128), 'ep', 0...]
    all_to_all x2, waiting for transfers between devices: 6.38 us -> 30.8 us  [the longest x1 29.8 us: per_device(): lax.all_to_all(send_rows.reshape(experts, half, 2 * width + 128), 'ep', 0...]
    all_to_all x2, starting transfers between devices: 8.94 us -> 12.7 us  [the longest x1 7.61 us: per_device(): lax.all_to_all(send_rows.reshape(experts, half, 2 * width + 128), 'ep', 0...]
    concatenate x10 -> x21, other arithmetic: 0.99 us -> 3.92 us  [the longest x1 1.67 us: per_device(): w_ext = jnp.concatenate([w_in, router_parts.T], axis=0)]
    unnamed x12 -> x18, local copies, waits for them, and re-layouts: 1.43 us -> 4.15 us
    ppermute x15 -> x17, waiting for transfers between devices: 25.8 us -> 24.2 us  [send(): return lax.ppermute(array, 'fsdp', pairs)]
    ppermute x15 -> x17, starting transfers between devices: 21.5 us -> 22.9 us  [send(): return lax.ppermute(array, 'fsdp', pairs)]
  transfers between devices with their start and end apart: 17 -> 19, of which waited for: 10 -> 13; matrix products, arithmetic and copies ran while one was open for 15% -> 20% of each run, Pallas kernels for 0% -> 0%
where the time goes in v4:
time: 133 us; the launch traced here: 132 us
  waiting for transfers between devices  55 us (41%)
  starting transfers between devices  35.5 us (27%)
  matrix products  24.8 us (19%)
  other arithmetic  8.5 us (6%)
  local copies, waits for them, and re-layouts  6.97 us (5%)
  between operations  1.65 us (1%)
    all_to_all x1, waiting for transfers between devices, per_device(): lax.all_to_all(send_rows.reshape(experts, half, 2 * width + 128), 'ep', 0...  29.8 us
    ppermute x17, waiting for transfers between devices, send(): return lax.ppermute(array, 'fsdp', pairs)  24.2 us
    dot_general x18, matrix products, dot(): lax.dot_general(left, right, (dims, ((), ())), preferred_element_type=F32)  23.7 us
    ppermute x17, starting transfers between devices, send(): return lax.ppermute(array, 'fsdp', pairs)  22.9 us
    all_to_all x1, starting transfers between devices, per_device(): lax.all_to_all(send_rows.reshape(experts, half, 2 * width + 128), 'ep', 0...  7.61 us
    all_to_all x1, starting transfers between devices, per_device(): lax.all_to_all(jnp.concatenate([own.astype(BF16).reshape(experts, half, s...  5.08 us
    unnamed x18, local copies, waits for them, and re-layouts  4.15 us
  transfers between devices with their start and end apart: 19, of which 13 were waited for; matrix products, arithmetic and copies ran while one was open for 20% of the time, Pallas kernels for 0%

profile of v4, /device:TPU:1, one launch (start us, length us, event | category | flops | bytes accessed | tf_op | source)
XLA Modules:
  0.0 132.5 jit_solution(5217096175856673090)
XLA Ops:
  1.7 4.6 %convolution_convert_fusion = bf16[128,12416]{1,0:T(8,128)(2,1)} fusion(bf16[128,128]{1,0:T(8,128)(2,1)S(1)} %broadcast_in_dim.95, bf16[128,6144]{1,0:T(8,128)(2,1)} %param.7, bf16[128,6144]{1,0:T(8,128)(2,1)} %param.8, pred[128,2,128]{2,0,1:T(32,128)(4,1)S(1)} %iota_compare_fusion.2), kind=kOutput, calls=%fused_computation | convolution fusion | flops 417988608 | bytes 6389760 | tf_op jit(solution)/shard_map/dot_general | solution.py:35
  6.3 7.6 %all-to-all-start = ((bf16[8,16,12416]{2,1,0:T(8,128)(2,1)}), bf16[8,16,12416]{2,1,0:T(8,128)(2,1)}, u32[]{:S(2)}, u32[]{:S(2)}) async-start(bf16[8,16,12416]{2,1,0:T(8,128)(2,1)} %bitcast.117), calls=%async_computation | async-start | bytes 6356992 | tf_op jit(solution)/shard_map/all_to_all | solution.py:76
  14.3 1.9 %convolution_bitcast_fusion = f32[128,24]{0,1:T(8,128)S(1)} fusion(bf16[128,6144]{1,0:T(8,128)(2,1)} %param.7, bf16[6144,8]{0,1:T(8,128)(2,1)S(1)} %get-tuple-element.105, bf16[6144,8]{0,1:T(8,128)(2,1)S(1)} %get-tuple-element.106, bf16[6144,8]{0,1:T(8,128)(2,1)S(1)} %get-tuple-element.104), kind=kOutput, calls=%fused_computation.36 | convolution fusion | flops 38633472 | bytes 1880064 | tf_op jit(solution)/shard_map/dot_general | solution.py:35
  16.3 2.0 %constant_dynamic-slice_fusion.3 = (bf16[168,384]{1,0:T(8,128)(2,1)S(1)}, bf16[168,384]{1,0:T(8,128)(2,1)S(1)}, bf16[168,384]{1,0:T(8,128)(2,1)S(1)}, bf16[168,3...) fusion(bf16[168,6144]{1,0:T(8,128)(2,1)} %bitcast.115, ...), kind=kLoop, calls=%fused_computation.184 | loop fusion | bytes 4128832 | tf_op jit(solution)/shard_map/dynamic_slice | solution.py:47
  20.3 1.7 %pad_maximum_fusion = bf16[192,6144]{1,0:T(8,128)(2,1)} fusion(bf16[24,6144]{1,0:T(8,128)(2,1)S(1)} %fusion.34, bf16[168,6144]{1,0:T(8,128)(2,1)S(1)} %bitcast.116), kind=kLoop, calls=%fused_computation.21 | loop fusion | flops 4718592 | bytes 4718592 | tf_op jit(solution)/shard_map/concatenate | solution.py:87
  22.0 29.8 %all-to-all-done = bf16[8,16,12416]{2,1,0:T(8,128)(2,1)} async-done(((bf16[8,16,12416]{2,1,0:T(8,128)(2,1)}), bf16[8,16,12416]{2,1,0:T(8,128)(2,1)}, u32[]{:S(2)}, u32[]{:S(2)}) %all-to-all-start) | async-done | bytes 3178528 | tf_op jit(solution)/shard_map/all_to_all | solution.py:76
  53.9 2.9 %fusion.20 = f32[128,192]{0,1:T(8,128)S(1)} fusion(bf16[192,6144]{1,0:T(8,128)(2,1)} %pad_maximum_fusion, bf16[128,12416]{1,0:T(8,128)(2,1)} %bitcast.4), kind=kOutput, calls=%fused_computation.34 | convolution fusion | flops 301989888 | bytes 4030464 | tf_op jit(solution)/shard_map/dot_general | solution.py:35
  56.9 2.1 %fusion.37 = (bf16[128,168]{0,1:T(8,128)(2,1)S(1)}, bf16[128,168]{0,1:T(8,128)(2,1)S(1)}, bf16[128,168]{0,1:T(8,128)(2,1)S(1)}, f32[128,168]{0,1:T(8,128)S(1)}) fusion(f32[128]{0:T(128)S(1)} %convert_element_type.316, f32[128,192]{0,1:T(8,128)S(1)} %fusion.20, bf16[1,168,6144]{2,1,0:T(8,128)(2,1)S(1)} %copy-done, bf16[128,12416]{1,0:T(8,128)(2,1)} %bitcast.4), kind=kOutput, calls=%fused_computation.94 | convolution fusion | flops 264563712 | bytes 3938816 | tf_op jit(solution)/shard_map/dot_general | solution.py:35
  59.2 2.3 %constant_dynamic-update-slice_fusion.1 = bf16[256,12416]{1,0:T(8,128)(2,1)S(1)} fusion(bf16[128,12416]{1,0:T(8,128)(2,1)} %bitcast.4), kind=kLoop, calls=%fused_computation.178 | loop fusion | bytes 6356992
  66.9 5.7 %collective-permute-start.4 = (bf16[136,768]{1,0:T(8,128)(2,1)S(1)}, bf16[136,768]{1,0:T(8,128)(2,1)S(1)}, u32[]{:S(2)}, u32[]{:S(2)}) collective-permute-start(bf16[136,768]{1,0:T(8,128)(2,1)S(1)} %get-tuple-element.38), channel_id=1, source_target_pairs={{0,112},{8,120},{16,0},{24,8},{32,16},{40,24},{48,32},{56,40},{64,... | collective-permute-start | bytes 626696 | tf_op jit(solution)/shard_map/ppermute | solution.py:31
  72.8 3.9 %collective-permute-done.4 = bf16[136,768]{1,0:T(8,128)(2,1)S(1)} collective-permute-done((bf16[136,768]{1,0:T(8,128)(2,1)S(1)}, bf16[136,768]{1,0:T(8,128)(2,1)S(1)}, u32[]{:S(2)}, u32[]{:S(2)}) %collective-permute-start.4) | collective-permute-done | bytes 208928 | tf_op jit(solution)/shard_map/ppermute | solution.py:31
  76.8 3.0 %collective-permute-done.2 = bf16[136,768]{1,0:T(8,128)(2,1)S(1)} collective-permute-done((bf16[136,768]{1,0:T(8,128)(2,1)S(1)}, bf16[136,768]{1,0:T(8,128)(2,1)S(1)}, u32[]{:S(2)}, u32[]{:S(2)}) %collective-permute-start.2) | collective-permute-done | bytes 208928 | tf_op jit(solution)/shard_map/ppermute | solution.py:31
  82.1 3.4 %collective-permute-done.7 = bf16[136,768]{1,0:T(8,128)(2,1)S(1)} collective-permute-done((bf16[136,768]{1,0:T(8,128)(2,1)S(1)}, bf16[136,768]{1,0:T(8,128)(2,1)S(1)}, u32[]{:S(2)}, u32[]{:S(2)}) %collective-permute-start.7) | collective-permute-done | bytes 208928 | tf_op jit(solution)/shard_map/ppermute | solution.py:31
  85.5 1.6 %collective-permute-done.5 = bf16[136,768]{1,0:T(8,128)(2,1)S(1)} collective-permute-done((bf16[136,768]{1,0:T(8,128)(2,1)S(1)}, bf16[136,768]{1,0:T(8,128)(2,1)S(1)}, u32[]{:S(2)}, u32[]{:S(2)}) %collective-permute-start.5) | collective-permute-done | bytes 208928 | tf_op jit(solution)/shard_map/ppermute | solution.py:31
  87.8 2.7 %collective-permute-start.11 = (bf16[136,768]{1,0:T(8,128)(2,1)S(1)}, bf16[136,768]{1,0:T(8,128)(2,1)S(1)}, u32[]{:S(2)}, u32[]{:S(2)}) collective-permute-start(bf16[136,768]{1,0:T(8,128)(2,1)S(1)} %pad_maximum_fusion.12), channel_id=1, source_target_pairs={{0,112},{8,120},{16,0},{24,8},{32,16},{40,24},{48,32},{56,40},{64,... | collective-permute-start | bytes 626696 | tf_op jit(solution)/shard_map/ppermute | solution.py:31
  90.5 2.8 %collective-permute-done.8 = bf16[136,768]{1,0:T(8,128)(2,1)S(1)} collective-permute-done((bf16[136,768]{1,0:T(8,128)(2,1)S(1)}, bf16[136,768]{1,0:T(8,128)(2,1)S(1)}, u32[]{:S(2)}, u32[]{:S(2)}) %collective-permute-start.8) | collective-permute-done | bytes 208928 | tf_op jit(solution)/shard_map/ppermute | solution.py:31
  94.1 5.4 %collective-permute-done.10 = bf16[136,768]{1,0:T(8,128)(2,1)S(1)} collective-permute-done((bf16[136,768]{1,0:T(8,128)(2,1)S(1)}, bf16[136,768]{1,0:T(8,128)(2,1)S(1)}, u32[]{:S(2)}, u32[]{:S(2)}) %collective-permute-start.10) | collective-permute-done | bytes 208928 | tf_op jit(solution)/shard_map/ppermute | solution.py:31
  99.6 4.8 %collective-permute-start.13 = (f32[1,128]{1,0:T(1,128)S(1)}, f32[1,128]{1,0:T(1,128)S(1)}, u32[]{:S(2)}, u32[]{:S(2)}) collective-permute-start(f32[1,128]{1,0:T(1,128)S(1)} %get-tuple-element.73), channel_id=1, source_target_pairs={{0,8},{8,0},{16,24},{24,16},{32,40},{40,32},{48,56},{56,48},{64,72... | collective-permute-start | bytes 1544 | tf_op jit(solution)/shard_map/ppermute | solution.py:31
  106.1 1.3 collective-permute-done.14
  107.4 1.5 %collective-permute-done.12 = bf16[136,384]{1,0:T(8,128)(2,1)S(1)} collective-permute-done((bf16[136,384]{1,0:T(8,128)(2,1)S(1)}, bf16[136,384]{1,0:T(8,128)(2,1)S(1)}, u32[]{:S(2)}, u32[]{:S(2)}) %collective-permute-start.12) | collective-permute-done | bytes 104480 | tf_op jit(solution)/shard_map/ppermute | solution.py:31
  110.5 5.1 %all-to-all-start.1 = ((bf16[8,88,384]{2,1,0:T(8,128)(2,1)}), bf16[8,88,384]{2,1,0:T(8,128)(2,1)S(1)}, u32[]{:S(2)}, u32[]{:S(2)}) async-start(bf16[8,88,384]{2,1,0:T(8,128)(2,1)} %fusion.25), calls=%async_computation.1 | async-start | bytes 1081344 | tf_op jit(solution)/shard_map/all_to_all | solution.py:185
  115.5 3.9 %fusion.1 = bf16[1,168,6144]{2,1,0:T(8,128)(2,1)} fusion(bf16[256,12416]{1,0:T(8,128)(2,1)} %copy-done.1, bf16[128,168]{0,1:T(8,128)(2,1)S(1)} %get-tuple-element.66, bf16[128,168]{0,1:T(8,128)(2,1)S(1)} %get-tuple-element.49), kind=kOutput, calls=%fused_computation.4 | convolution fusion | flops 529686528 | bytes 5296128 | tf_op jit(solution)/shard_map/dot_general | solution.py:35
  119.4 3.9 %fusion = bf16[1,6144,168]{1,2,0:T(8,128)(2,1)} fusion(bf16[256,12416]{1,0:T(8,128)(2,1)} %copy-done.1, bf16[128,168]{0,1:T(8,128)(2,1)S(1)} %get-tuple-element.107, bf16[128,168]{0,1:T(8,128)(2,1)S(1)} %get-tuple-element.32), kind=kOutput, calls=%fused_computation.3 | convolution fusion | flops 529686528 | bytes 5296128 | tf_op jit(solution)/shard_map/dot_general | solution.py:35
  124.7 3.6 %collective-permute-start.16 = (f32[8,3200]{1,0:T(8,128)S(1)}, f32[8,3200]{1,0:T(8,128)S(1)}, u32[]{:S(2)}, u32[]{:S(2)}) collective-permute-start(f32[8,3200]{1,0:T(8,128)S(1)} %select_maximum_fusion), channel_id=1, source_target_pairs={{0,8},{8,0},{16,24},{24,16},{32,40},{40,32},{48,56},{56,48},{64,72... | collective-permute-start | bytes 307208 | tf_op jit(solution)/shard_map/ppermute | solution.py:31
  (154 shorter events, 23.4 us)
Async XLA Ops:
  0.6 56.3 %copy-start = (bf16[1,168,6144]{2,1,0:T(8,128)(2,1)S(1)}, bf16[1,168,6144]{2,1,0:T(8,128)(2,1)}, u32[]{:S(2)}) copy-start(bf16[1,168,6144]{2,1,0:T(8,128)(2,1)} %param.11) | copy-start | bytes 6193156
  6.3 7.9 %copy-start.6 = (f32[6144,8]{0,1:T(8,128)S(1)}, f32[6144,8]{0,1:T(8,128)}, u32[]{:S(2)}) copy-start(f32[6144,8]{0,1:T(8,128)} %param.9) | copy-start | bytes 589828
  6.3 45.4 %all-to-all-start = ((bf16[8,16,12416]{2,1,0:T(8,128)(2,1)}), bf16[8,16,12416]{2,1,0:T(8,128)(2,1)}, u32[]{:S(2)}, u32[]{:S(2)}) async-start(bf16[8,16,12416]{2,1,0:T(8,128)(2,1)} %bitcast.117), calls=%async_computation | async-start | bytes 6356992 | tf_op jit(solution)/shard_map/all_to_all | solution.py:76
  13.9 2.3 %copy-start.7 = (s32[128,2]{0,1:T(2,128)S(1)}, s32[128,2]{0,1:T(2,128)}, u32[]{:S(2)}) copy-start(s32[128,2]{0,1:T(2,128)} %param.12) | copy-start | bytes 3076
  51.8 9.7 %collective-permute-start = (bf16[128,12416]{1,0:T(8,128)(2,1)}, bf16[128,12416]{1,0:T(8,128)(2,1)S(1)}, u32[]{:S(2)}, u32[]{:S(2)}) collective-permute-start(bf16[128,12416]{1,0:T(8,128)(2,1)} %bitcast.4), channel_id=1, source_target_pairs={{0,8},{8,0},{16,24},{24,16},{32,40},{40,32},{48,56},{56,48},{64,72... | collective-permute-start | bytes 9535496 | tf_op jit(solution)/shard_map/ppermute | solution.py:31
  59.2 2.6 %copy-start.5 = (bf16[192,6144]{1,0:T(8,128)(2,1)S(1)}, bf16[192,6144]{1,0:T(8,128)(2,1)}, u32[]{:S(2)}) copy-start(bf16[192,6144]{1,0:T(8,128)(2,1)} %pad_maximum_fusion) | copy-start | bytes 7077892
  63.9 23.6 %collective-permute-start.9 = (bf16[128,1536]{1,0:T(8,128)(2,1)S(1)}, bf16[128,1536]{1,0:T(8,128)(2,1)S(1)}, u32[]{:S(2)}, u32[]{:S(2)}) collective-permute-start(bf16[128,1536]{1,0:T(8,128)(2,1)S(1)} %convolution_convert_fusion.3), channel_id=1, source_target_pairs={{0,8},{8,0},{16,24},{24,16},{32,40},{40,32},{48,56},{56,48},{64,72... | collective-permute-start | bytes 1179656 | tf_op jit(solution)/shard_map/ppermute | solution.py:31
  64.4 2.0 %collective-permute-start.1 = (bf16[136,1536]{1,0:T(8,128)(2,1)S(1)}, bf16[136,1536]{1,0:T(8,128)(2,1)S(1)}, u32[]{:S(2)}, u32[]{:S(2)}) collective-permute-start(bf16[136,1536]{1,0:T(8,128)(2,1)S(1)} %pad_maximum_fusion.5), channel_id=1, source_target_pairs={{0,8},{8,0},{16,24},{24,16},{32,40},{40,32},{48,56},{56,48},{64,72... | collective-permute-start | bytes 1253384 | tf_op jit(solution)/shard_map/ppermute | solution.py:31
  65.3 7.3 %collective-permute-start.3 = (bf16[128,1536]{1,0:T(8,128)(2,1)S(1)}, bf16[128,1536]{1,0:T(8,128)(2,1)S(1)}, u32[]{:S(2)}, u32[]{:S(2)}) collective-permute-start(bf16[128,1536]{1,0:T(8,128)(2,1)S(1)} %convolution_convert_fusion.5), channel_id=1, source_target_pairs={{0,8},{8,0},{16,24},{24,16},{32,40},{40,32},{48,56},{56,48},{64,72... | collective-permute-start | bytes 1179656 | tf_op jit(solution)/shard_map/ppermute | solution.py:31
  65.7 16.1 %collective-permute-start.6 = (bf16[128,1536]{1,0:T(8,128)(2,1)S(1)}, bf16[128,1536]{1,0:T(8,128)(2,1)S(1)}, u32[]{:S(2)}, u32[]{:S(2)}) collective-permute-start(bf16[128,1536]{1,0:T(8,128)(2,1)S(1)} %convolution_convert_fusion.4), channel_id=1, source_target_pairs={{0,8},{8,0},{16,24},{24,16},{32,40},{40,32},{48,56},{56,48},{64,72... | collective-permute-start | bytes 1179656 | tf_op jit(solution)/shard_map/ppermute | solution.py:31
  66.9 9.8 %collective-permute-start.4 = (bf16[136,768]{1,0:T(8,128)(2,1)S(1)}, bf16[136,768]{1,0:T(8,128)(2,1)S(1)}, u32[]{:S(2)}, u32[]{:S(2)}) collective-permute-start(bf16[136,768]{1,0:T(8,128)(2,1)S(1)} %get-tuple-element.38), channel_id=1, source_target_pairs={{0,112},{8,120},{16,0},{24,8},{32,16},{40,24},{48,32},{56,40},{64,... | collective-permute-start | bytes 626696 | tf_op jit(solution)/shard_map/ppermute | solution.py:31
  72.5 7.3 %collective-permute-start.2 = (bf16[136,768]{1,0:T(8,128)(2,1)S(1)}, bf16[136,768]{1,0:T(8,128)(2,1)S(1)}, u32[]{:S(2)}, u32[]{:S(2)}) collective-permute-start(bf16[136,768]{1,0:T(8,128)(2,1)S(1)} %get-tuple-element.36), channel_id=1, source_target_pairs={{0,16},{8,24},{16,32},{24,40},{32,48},{40,56},{48,64},{56,72},{64,... | collective-permute-start | bytes 626696 | tf_op jit(solution)/shard_map/ppermute | solution.py:31
  80.1 5.4 %collective-permute-start.7 = (bf16[136,768]{1,0:T(8,128)(2,1)S(1)}, bf16[136,768]{1,0:T(8,128)(2,1)S(1)}, u32[]{:S(2)}, u32[]{:S(2)}) collective-permute-start(bf16[136,768]{1,0:T(8,128)(2,1)S(1)} %pad_maximum_fusion.10), channel_id=1, source_target_pairs={{0,112},{8,120},{16,0},{24,8},{32,16},{40,24},{48,32},{56,40},{64,... | collective-permute-start | bytes 626696 | tf_op jit(solution)/shard_map/ppermute | solution.py:31
  80.7 6.4 %collective-permute-start.5 = (bf16[136,768]{1,0:T(8,128)(2,1)S(1)}, bf16[136,768]{1,0:T(8,128)(2,1)S(1)}, u32[]{:S(2)}, u32[]{:S(2)}) collective-permute-start(bf16[136,768]{1,0:T(8,128)(2,1)S(1)} %pad_maximum_fusion.9), channel_id=1, source_target_pairs={{0,16},{8,24},{16,32},{24,40},{32,48},{40,56},{48,64},{56,72},{64,... | collective-permute-start | bytes 626696 | tf_op jit(solution)/shard_map/ppermute | solution.py:31
  87.4 5.9 %collective-permute-start.8 = (bf16[136,768]{1,0:T(8,128)(2,1)S(1)}, bf16[136,768]{1,0:T(8,128)(2,1)S(1)}, u32[]{:S(2)}, u32[]{:S(2)}) collective-permute-start(bf16[136,768]{1,0:T(8,128)(2,1)S(1)} %pad_maximum_fusion.11), channel_id=1, source_target_pairs={{0,16},{8,24},{16,32},{24,40},{32,48},{40,56},{48,64},{56,72},{64,... | collective-permute-start | bytes 626696 | tf_op jit(solution)/shard_map/ppermute | solution.py:31
  87.8 6.2 %collective-permute-start.11 = (bf16[136,768]{1,0:T(8,128)(2,1)S(1)}, bf16[136,768]{1,0:T(8,128)(2,1)S(1)}, u32[]{:S(2)}, u32[]{:S(2)}) collective-permute-start(bf16[136,768]{1,0:T(8,128)(2,1)S(1)} %pad_maximum_fusion.12), channel_id=1, source_target_pairs={{0,112},{8,120},{16,0},{24,8},{32,16},{40,24},{48,32},{56,40},{64,... | collective-permute-start | bytes 626696 | tf_op jit(solution)/shard_map/ppermute | solution.py:31
  93.5 5.9 %collective-permute-start.10 = (bf16[136,768]{1,0:T(8,128)(2,1)S(1)}, bf16[136,768]{1,0:T(8,128)(2,1)S(1)}, u32[]{:S(2)}, u32[]{:S(2)}) collective-permute-start(bf16[136,768]{1,0:T(8,128)(2,1)S(1)} %pad_maximum_fusion.13), channel_id=1, source_target_pairs={{0,16},{8,24},{16,32},{24,40},{32,48},{40,56},{48,64},{56,72},{64,... | collective-permute-start | bytes 626696 | tf_op jit(solution)/shard_map/ppermute | solution.py:31
  94.0 15.0 %copy-start.1 = (bf16[256,12416]{1,0:T(8,128)(2,1)}, bf16[256,12416]{1,0:T(8,128)(2,1)S(1)}, u32[]{:S(2)}) copy-start(bf16[256,12416]{1,0:T(8,128)(2,1)S(1)} %constant_dynamic-update-slice_fusion) | copy-start | bytes 19070980
  99.6 6.5 %collective-permute-start.13 = (f32[1,128]{1,0:T(1,128)S(1)}, f32[1,128]{1,0:T(1,128)S(1)}, u32[]{:S(2)}, u32[]{:S(2)}) collective-permute-start(f32[1,128]{1,0:T(1,128)S(1)} %get-tuple-element.73), channel_id=1, source_target_pairs={{0,8},{8,0},{16,24},{24,16},{32,40},{40,32},{48,56},{56,48},{64,72... | collective-permute-start | bytes 1544 | tf_op jit(solution)/shard_map/ppermute | solution.py:31
  104.4 3.0 %collective-permute-start.14 = (f32[1,128]{1,0:T(1,128)S(1)}, f32[1,128]{1,0:T(1,128)S(1)}, u32[]{:S(2)}, u32[]{:S(2)}) collective-permute-start(f32[1,128]{1,0:T(1,128)S(1)} %get-tuple-element.73), channel_id=1, source_target_pairs={{0,136},{8,128},{16,152},{24,144},{32,168},{40,160},{48,184},{56,1... | collective-permute-start | bytes 1544 | tf_op jit(solution)/shard_map/ppermute | solution.py:31
  104.7 4.2 %collective-permute-start.12 = (bf16[136,384]{1,0:T(8,128)(2,1)S(1)}, bf16[136,384]{1,0:T(8,128)(2,1)S(1)}, u32[]{:S(2)}, u32[]{:S(2)}) collective-permute-start(bf16[136,384]{1,0:T(8,128)(2,1)S(1)} %pad_maximum_fusion.15), channel_id=1, source_target_pairs={{0,128},{8,136},{16,144},{24,152},{32,160},{40,168},{48,176},{56,1... | collective-permute-start | bytes 313352 | tf_op jit(solution)/shard_map/ppermute | solution.py:31
  110.5 13.9 %all-to-all-start.1 = ((bf16[8,88,384]{2,1,0:T(8,128)(2,1)}), bf16[8,88,384]{2,1,0:T(8,128)(2,1)S(1)}, u32[]{:S(2)}, u32[]{:S(2)}) async-start(bf16[8,88,384]{2,1,0:T(8,128)(2,1)} %fusion.25), calls=%async_computation.1 | async-start | bytes 1081344 | tf_op jit(solution)/shard_map/all_to_all | solution.py:185
  124.7 4.5 %collective-permute-start.16 = (f32[8,3200]{1,0:T(8,128)S(1)}, f32[8,3200]{1,0:T(8,128)S(1)}, u32[]{:S(2)}, u32[]{:S(2)}) collective-permute-start(f32[8,3200]{1,0:T(8,128)S(1)} %select_maximum_fusion), channel_id=1, source_target_pairs={{0,8},{8,0},{16,24},{24,16},{32,40},{40,32},{48,56},{56,48},{64,72... | collective-permute-start | bytes 307208 | tf_op jit(solution)/shard_map/ppermute | solution.py:31
  128.6 1.3 %collective-permute-start.15 = (bf16[128,192]{1,0:T(8,128)(2,1)S(1)}, bf16[128,192]{1,0:T(8,128)(2,1)S(1)}, u32[]{:S(2)}, u32[]{:S(2)}) collective-permute-start(bf16[128,192]{1,0:T(8,128)(2,1)S(1)} %select_convert_fusion), channel_id=1, source_target_pairs={{0,8},{8,0},{16,24},{24,16},{32,40},{40,32},{48,56},{56,48},{64,72... | collective-permute-start | bytes 147464 | tf_op jit(solution)/shard_map/ppermute | solution.py:31
  (3 other events, 4.5 us)

commit v5 on v4

--- a/solution.py
+++ b/solution.py
@@ -59,10 +59,14 @@
     z = (fsdp_index // 2) % Z
     lo = fsdp_index // (2 * Z)
     seg = width // (2 * Z)
+    core_cols = width // 2
     own_cols = width // (4 * Z)
 
     w_in = expert_in[0].T
     w_out = expert_out[0]
+    hidden_own = w_in.shape[0]
+    w_in = jnp.concatenate([w_in, send(w_in, TO_CORE)], axis=0)
+    w_out = jnp.concatenate([w_out, send(w_out, TO_CORE)], axis=0)
 
     key_abs = jnp.where((slots // half == core) & (slots >= 0), choices * half + slots % half, -1)
     places_abs = key_abs[:, :, None] == jnp.arange(rows, dtype=jnp.int32)
@@ -72,7 +76,7 @@
     )
     packed = jnp.concatenate([out_grad, tokens, both_choices], axis=1)
     send_rows = dot(spread_abs, packed, ((0,), (0,))).astype(BF16)
-    send_rows, w_in, router_weight = lax.optimization_barrier((send_rows, w_in, router_weight))
+    send_rows, router_weight = lax.optimization_barrier((send_rows, router_weight))
     mine_rows = lax.all_to_all(
         send_rows.reshape(experts, half, 2 * width + 128), "ep", 0, 0, tiled=True
     ).reshape(rows, 2 * width + 128)
@@ -93,10 +97,7 @@
     orders = [(4, 5), (3, 6), (2, 7), (1, 0)]
     near = [jnp.concatenate(weights(a) + weights(b), axis=1) for a, b in orders]
 
-    mine_rows, w_ext, near, first_gate, second_gate, chosen_hot = lax.optimization_barrier(
-        (mine_rows, w_ext, near, first_gate, second_gate, chosen_hot)
-    )
-    other_rows = send(mine_rows, TO_CORE)
+    mine_rows, w_ext, w_out, near = lax.optimization_barrier((mine_rows, w_ext, w_out, near))
     hidden_count = w_in.shape[0]
 
     def act(part_rows):
@@ -126,10 +127,7 @@
         slopes = slope * ((ids == me).astype(F32) - (ids == second).astype(F32))
         return score, weighted, act_grad, slopes
 
-    done_mine = act(mine_rows)
-    other_rows, done_mine = lax.optimization_barrier((other_rows, done_mine))
-    score_mine, weighted_mine, act_mine, slopes_mine = done_mine
-    score_other, weighted_other, act_other, slopes_other = act(other_rows)
+    score, weighted, act_grad, slopes = act(mine_rows)
 
     def pack(grads, score):
         high = lax.reduce_precision(score, 8, 7)
@@ -141,23 +139,40 @@
         wide = packed.astype(F32)
         return wide[:rows], jnp.sum(wide[rows:, :rows], axis=0, keepdims=True)
 
-    first_other = dot(act_other, near[0], ((1,), (0,)))
-    got, got_score = unpack(send(pack(first_other, score_other), TO_CORE))
-    score = score_mine + got_score
-    part = dot(act_mine, near[0], ((1,), (0,))) + got
+    part = dot(act_grad, near[0], ((1,), (0,)))
     up, down = part[:, : 2 * seg], part[:, 2 * seg :]
     up_score = down_score = score
+    later = (act_grad, weighted, slopes, mine_rows)
+    grads = ()
     for step in range(3):
-        going_up, going_down = lax.optimization_barrier(
-            (pack(up, up_score), pack(down, down_score))
+        going_up, going_down, later, grads = lax.optimization_barrier(
+            (pack(up, up_score), pack(down, down_score), later, grads)
         )
         up, up_score = unpack(send(going_up, TO_UP))
         down, down_score = unpack(send(going_down, TO_DOWN))
-        other = dot(act_other, near[step + 1], ((1,), (0,))).astype(BF16)
-        got = send(other, TO_CORE)
-        part = dot(act_mine, near[step + 1], ((1,), (0,))) + got.astype(F32)
+        act_grad, weighted, slopes, mine_rows = later
+        part = dot(act_grad, near[step + 1], ((1,), (0,)))
         up, up_score = up + part[:, : 2 * seg], up_score + score
         down, down_score = down + part[:, 2 * seg :], down_score + score
+        if step == 0:
+            other_rows = send(mine_rows, TO_CORE)
+            other_acts = send(
+                jnp.concatenate([act_grad[:, hidden_own:], weighted[:, hidden_own:]], axis=1),
+                TO_CORE,
+            )
+            grads = (other_rows, other_acts, send(slopes, TO_CORE))
+        elif step == 1:
+            other_rows, other_acts, other_slopes = grads
+            both = jnp.concatenate([mine_rows, other_rows], axis=0)
+            act_all = jnp.concatenate([act_grad[:, :hidden_own], other_acts[:, :hidden_own]])
+            weighted_all = jnp.concatenate([weighted[:, :hidden_own], other_acts[:, hidden_own:]])
+            half_x = columns(both, width + core * core_cols, core_cols)
+            grads = (both, act_all, weighted_all, jnp.concatenate([slopes, other_slopes]), half_x)
+        else:
+            grad_out = dot(grads[2], grads[0][:, :width], ((0,), (0,))).astype(BF16)
+    both, act_all, _, slopes, half_x = grads
+    up, up_score, act_all, grad_out = lax.optimization_barrier((up, up_score, act_all, grad_out))
+    grad_in = dot(act_all, both[:, width : 2 * width], ((0,), (0,))).astype(BF16)
     last, last_score = unpack(send(pack(up, up_score), TO_UP))
     total, total_score = last + down, last_score + down_score
     side, side_score = unpack(send(pack(total[:, seg:], total_score), TO_SIDE))
@@ -165,12 +180,9 @@
     other_score = send(total_score, TO_CORE) + send(total_score, TO_CROSS)
 
     row_scores = jnp.concatenate([own_score, other_score], axis=1).reshape(2 * rows, 1)
-    slopes = jnp.concatenate([slopes_mine, slopes_other], axis=0)
-    both = jnp.concatenate([mine_rows, other_rows], axis=0)
-    core_cols = width // 2
     router_part = dot(
         jnp.concatenate(split3(slopes * row_scores), axis=1),
-        columns(both, width + core * core_cols, core_cols),
+        half_x,
         ((0,), (0,)),
     )
     router_part = (router_part[:experts] + router_part[experts : 2 * experts]) + router_part[
@@ -222,11 +234,6 @@
     change = first_gate * second_gate * (taken[:, 0] - taken[:, 1])
     logit_grad = change[:, None] * (chosen_hot[:, 0, :] - chosen_hot[:, 1, :])
 
-    weighted = jnp.concatenate([weighted_mine, weighted_other], axis=0)
-    act_grad = jnp.concatenate([act_mine, act_other], axis=0)
-    grad_out = dot(weighted, both[:, :width], ((0,), (0,))).astype(BF16)
-    grad_in = dot(act_grad, both[:, width : 2 * width], ((0,), (0,))).astype(BF16)
-
     router_rows = lax.dynamic_slice_in_dim(router_weight, fsdp_index * own_cols, own_cols, 0)
     grad_tokens = (
         expert_grad + jnp.dot(logit_grad, router_rows.T, precision=lax.Precision.HIGHEST)

time: 133 us -> 128 us (0.962)
  waiting for transfers between devices: 55 us -> 43.5 us
  other arithmetic: 8.5 us -> 19.5 us
  matrix products: 24.8 us -> 21.2 us
    ppermute x17, waiting for transfers between devices: 24.2 us -> 15.8 us  [send(): return lax.ppermute(array, 'fsdp', pairs)]
    concatenate x1 -> x8, other arithmetic: 0.01 us -> 8.14 us  [the longest x3 4.11 us: per_device(): w_in = jnp.concatenate([w_in, send(w_in, TO_CORE)], axis=0)]
    all_to_all x1, waiting for transfers between devices: 29.8 us -> 22.9 us  [per_device(): lax.all_to_all(send_rows.reshape(experts, half, 2 * width + 128), 'ep', 0...]
    all_to_all x1, waiting for transfers between devices: 1 us -> 4.87 us  [per_device(): lax.all_to_all(jnp.concatenate([own.astype(BF16).reshape(experts, half, s...]
    dot_general x18 -> x12, matrix products: 23.7 us -> 20.1 us  [dot(): lax.dot_general(left, right, (dims, ((), ())), preferred_element_type=F32)]
    all_to_all x1, starting transfers between devices: 7.61 us -> 5.05 us  [per_device(): lax.all_to_all(send_rows.reshape(experts, half, 2 * width + 128), 'ep', 0...]
    ppermute x17, starting transfers between devices: 22.9 us -> 25.2 us  [send(): return lax.ppermute(array, 'fsdp', pairs)]
    concatenate x1, local copies, waits for them, and re-layouts: 0.41 us -> 2.31 us  [per_device(): both = jnp.concatenate([mine_rows, other_rows], axis=0)]
  transfers between devices with their start and end apart: 19 -> 19, of which waited for: 13 -> 9; matrix products, arithmetic and copies ran while one was open for 20% -> 25% of each run, Pallas kernels for 0% -> 0%
where the time goes in v5:
time: 128 us; the launch traced here: 127 us
  waiting for transfers between devices  43.5 us (34%)
  starting transfers between devices  35.4 us (28%)
  matrix products  21.2 us (17%)
  other arithmetic  19.5 us (15%)
  local copies, waits for them, and re-layouts  6.13 us (5%)
  between operations  1.62 us (1%)
    ppermute x17, starting transfers between devices, send(): return lax.ppermute(array, 'fsdp', pairs)  25.2 us
    all_to_all x1, waiting for transfers between devices, per_device(): lax.all_to_all(send_rows.reshape(experts, half, 2 * width + 128), 'ep', 0...  22.9 us
    dot_general x12, matrix products, dot(): lax.dot_general(left, right, (dims, ((), ())), preferred_element_type=F32)  20.1 us
    ppermute x17, waiting for transfers between devices, send(): return lax.ppermute(array, 'fsdp', pairs)  15.8 us
    all_to_all x1, starting transfers between devices, per_device(): lax.all_to_all(jnp.concatenate([own.astype(BF16).reshape(experts, half, s...  5.07 us
    all_to_all x1, starting transfers between devices, per_device(): lax.all_to_all(send_rows.reshape(experts, half, 2 * width + 128), 'ep', 0...  5.05 us
    all_to_all x1, waiting for transfers between devices, per_device(): lax.all_to_all(jnp.concatenate([own.astype(BF16).reshape(experts, half, s...  4.87 us
    concatenate x3, other arithmetic, per_device(): w_in = jnp.concatenate([w_in, send(w_in, TO_CORE)], axis=0)  4.11 us
  transfers between devices with their start and end apart: 19, of which 9 were waited for; matrix products, arithmetic and copies ran while one was open for 25% of the time, Pallas kernels for 0%

profile of v5, /device:TPU:1, one launch (start us, length us, event | category | flops | bytes accessed | tf_op | source)
XLA Modules:
  0.0 127.3 jit_solution(18039052604424166791)
XLA Ops:
  0.6 3.3 %collective-permute-start = (bf16[168,6144]{1,0:T(8,128)(2,1)}, bf16[168,6144]{1,0:T(8,128)(2,1)}, u32[]{:S(2)}, u32[]{:S(2)}) collective-permute-start(bf16[168,6144]{1,0:T(8,128)(2,1)} %bitcast.114), channel_id=1, source_target_pairs={{0,8},{8,0},{16,24},{24,16},{32,40},{40,32},{48,56},{56,48},{64,72... | collective-permute-start | bytes 6193160 | tf_op jit(solution)/shard_map/ppermute | solution.py:31
  5.0 4.7 %convolution_convert_fusion = bf16[128,12416]{1,0:T(8,128)(2,1)} fusion(bf16[128,128]{1,0:T(8,128)(2,1)S(1)} %broadcast_in_dim.36, bf16[128,6144]{1,0:T(8,128)(2,1)} %param.7, bf16[128,6144]{1,0:T(8,128)(2,1)} %param.8, pred[128,2,128]{2,0,1:T(32,128)(4,1)S(1)} %iota_compare_fusion.2), kind=kOutput, calls=%fused_computation | convolution fusion | flops 417988608 | bytes 6389760 | tf_op jit(solution)/shard_map/dot_general | solution.py:35
  9.7 5.0 %all-to-all-start = ((bf16[8,16,12416]{2,1,0:T(8,128)(2,1)}), bf16[8,16,12416]{2,1,0:T(8,128)(2,1)}, u32[]{:S(2)}, u32[]{:S(2)}) async-start(bf16[8,16,12416]{2,1,0:T(8,128)(2,1)} %bitcast.119), calls=%async_computation | async-start | bytes 6356992 | tf_op jit(solution)/shard_map/all_to_all | solution.py:80
  19.6 1.5 %pad_maximum_fusion.4 = (bf16[336,1536]{1,0:T(8,128)(2,1)}, bf16[336,1536]{1,0:T(8,128)(2,1)}) fusion(bf16[336,384]{1,0:T(8,128)(2,1)S(1)} %get-tuple-element.112, bf16[336,384]{1,0:T(8,128)(2,1)S(1)} %get-tuple-element.111, bf16[336,384]{1,0:T(8,128)(2,1)S(1)} %get-tuple-element.109, bf16[336,384]{1,0:T(8,128)(2,1)S(1)} %get-tuple-element.108, ...), kind=kLoop, calls=%fused_computation.57 | loop fusion | flops 8257536 | bytes 4128768 | tf_op jit(solution)/shard_map/concatenate | solution.py:98
  22.2 4.0 %pad_maximum_fusion.1 = bf16[336,6144]{1,0:T(8,128)(2,1)} fusion(bf16[168,6144]{1,0:T(8,128)(2,1)} %collective-permute-done.1, bf16[168,6144]{1,0:T(8,128)(2,1)S(1)} %bitcast.121), kind=kLoop, calls=%fused_computation.37 | loop fusion | flops 8257536 | bytes 8257536 | tf_op jit(solution)/shard_map/concatenate | solution.py:69
  26.2 3.5 %pad_maximum_fusion = bf16[360,6144]{1,0:T(8,128)(2,1)} fusion(bf16[24,6144]{1,0:T(8,128)(2,1)S(1)} %fusion.41, bf16[168,6144]{1,0:T(8,128)(2,1)} %collective-permute-done, bf16[168,6144]{1,0:T(8,128)(2,1)S(1)} %bitcast.118), kind=kLoop, calls=%fused_computation.36 | loop fusion | flops 13271040 | bytes 8847360 | tf_op jit(solution)/shard_map/concatenate | solution.py:91
  29.7 22.9 %all-to-all-done = bf16[8,16,12416]{2,1,0:T(8,128)(2,1)} async-done(((bf16[8,16,12416]{2,1,0:T(8,128)(2,1)}), bf16[8,16,12416]{2,1,0:T(8,128)(2,1)}, u32[]{:S(2)}, u32[]{:S(2)}) %all-to-all-start) | async-done | bytes 3178528 | tf_op jit(solution)/shard_map/all_to_all | solution.py:80
  53.6 4.3 %fusion.10 = f32[128,360]{0,1:T(8,128)S(1)} fusion(bf16[360,6144]{1,0:T(8,128)(2,1)} %pad_maximum_fusion, bf16[128,12416]{1,0:T(8,128)(2,1)} %bitcast.2), kind=kOutput, calls=%fused_computation.50 | convolution fusion | flops 566231040 | bytes 6180864 | tf_op jit(solution)/shard_map/dot_general | solution.py:35
  58.0 2.7 %fusion.40 = (bf16[128,336]{0,1:T(8,128)(2,1)S(1)}, bf16[128,336]{0,1:T(8,128)(2,1)S(1)}, bf16[128,336]{0,1:T(8,128)(2,1)S(1)}, f32[128,336]{0,1:T(8,128)S(1)}) fusion(f32[128]{0:T(128)S(1)} %convert_element_type.219, f32[128,360]{0,1:T(8,128)S(1)} %fusion.10, bf16[336,6144]{1,0:T(8,128)(2,1)S(1)} %copy-done.2, bf16[128,12416]{1,0:T(8,128)(2,1)} %bitcast.2), kind=kOutput, calls=%fused_computation.109 | convolution fusion | flops 529127424 | bytes 6304256 | tf_op jit(solution)/shard_map/dot_general | solution.py:35
  63.2 1.7 %collective-permute-start.2 = (bf16[136,768]{1,0:T(8,128)(2,1)S(1)}, bf16[136,768]{1,0:T(8,128)(2,1)S(1)}, u32[]{:S(2)}, u32[]{:S(2)}) collective-permute-start(bf16[136,768]{1,0:T(8,128)(2,1)S(1)} %get-tuple-element.46), channel_id=1, source_target_pairs={{0,16},{8,24},{16,32},{24,40},{32,48},{40,56},{48,64},{56,72},{64,... | collective-permute-start | bytes 626696 | tf_op jit(solution)/shard_map/ppermute | solution.py:31
  64.9 3.9 %collective-permute-start.3 = (bf16[136,768]{1,0:T(8,128)(2,1)S(1)}, bf16[136,768]{1,0:T(8,128)(2,1)S(1)}, u32[]{:S(2)}, u32[]{:S(2)}) collective-permute-start(bf16[136,768]{1,0:T(8,128)(2,1)S(1)} %get-tuple-element.49), channel_id=1, source_target_pairs={{0,112},{8,120},{16,0},{24,8},{32,16},{40,24},{48,32},{56,40},{64,... | collective-permute-start | bytes 626696 | tf_op jit(solution)/shard_map/ppermute | solution.py:31
  69.2 5.0 %collective-permute-done.2 = bf16[136,768]{1,0:T(8,128)(2,1)S(1)} collective-permute-done((bf16[136,768]{1,0:T(8,128)(2,1)S(1)}, bf16[136,768]{1,0:T(8,128)(2,1)S(1)}, u32[]{:S(2)}, u32[]{:S(2)}) %collective-permute-start.2) | collective-permute-done | bytes 208928 | tf_op jit(solution)/shard_map/ppermute | solution.py:31
  75.1 2.7 %collective-permute-start.8 = (bf16[136,768]{1,0:T(8,128)(2,1)S(1)}, bf16[136,768]{1,0:T(8,128)(2,1)S(1)}, u32[]{:S(2)}, u32[]{:S(2)}) collective-permute-start(bf16[136,768]{1,0:T(8,128)(2,1)S(1)} %pad_maximum_fusion.10), channel_id=1, source_target_pairs={{0,112},{8,120},{16,0},{24,8},{32,16},{40,24},{48,32},{56,40},{64,... | collective-permute-start | bytes 626696 | tf_op jit(solution)/shard_map/ppermute | solution.py:31
  77.8 2.1 %constant_dynamic-update-slice_fusion.1 = bf16[256,12416]{1,0:T(8,128)(2,1)S(1)} fusion(bf16[128,12416]{1,0:T(8,128)(2,1)} %bitcast.2), kind=kLoop, calls=%fused_computation.191 | loop fusion | bytes 6356992
  79.9 2.3 %constant_dynamic-update-slice_fusion = bf16[256,12416]{1,0:T(8,128)(2,1)S(1)} fusion(bf16[256,12416]{1,0:T(8,128)(2,1)S(1)} %constant_dynamic-update-slice_fusion.1, bf16[128,12416]{1,0:T(8,128)(2,1)} %collective-permute-done.4), kind=kLoop, calls=%fused_computation.190 | loop fusion | bytes 6356992 | tf_op jit(solution)/shard_map/concatenate | solution.py:166
  83.8 1.8 %collective-permute-start.11 = (bf16[136,768]{1,0:T(8,128)(2,1)S(1)}, bf16[136,768]{1,0:T(8,128)(2,1)S(1)}, u32[]{:S(2)}, u32[]{:S(2)}) collective-permute-start(bf16[136,768]{1,0:T(8,128)(2,1)S(1)} %pad_maximum_fusion.12), channel_id=1, source_target_pairs={{0,112},{8,120},{16,0},{24,8},{32,16},{40,24},{48,32},{56,40},{64,... | collective-permute-start | bytes 626696 | tf_op jit(solution)/shard_map/ppermute | solution.py:31
  85.6 2.0 %convolution_convert_fusion.2 = bf16[168,6144]{1,0:T(8,128)(2,1)} fusion(bf16[256,168]{0,1:T(8,128)(2,1)S(1)} %pad_maximum_fusion.18, bf16[256,12416]{1,0:T(8,128)(2,1)S(1)} %constant_dynamic-update-slice_fusion), kind=kOutput, calls=%fused_computation.34 | convolution fusion | flops 529514496 | bytes 5296128 | tf_op jit(solution)/shard_map/dot_general | solution.py:35
  90.3 5.2 %collective-permute-done.10 = bf16[136,768]{1,0:T(8,128)(2,1)S(1)} collective-permute-done((bf16[136,768]{1,0:T(8,128)(2,1)S(1)}, bf16[136,768]{1,0:T(8,128)(2,1)S(1)}, u32[]{:S(2)}, u32[]{:S(2)}) %collective-permute-start.10) | collective-permute-done | bytes 208928 | tf_op jit(solution)/shard_map/ppermute | solution.py:31
  95.7 3.6 %collective-permute-start.13 = (f32[1,128]{1,0:T(1,128)S(1)}, f32[1,128]{1,0:T(1,128)S(1)}, u32[]{:S(2)}, u32[]{:S(2)}) collective-permute-start(f32[1,128]{1,0:T(1,128)S(1)} %get-tuple-element.93), channel_id=1, source_target_pairs={{0,8},{8,0},{16,24},{24,16},{32,40},{40,32},{48,56},{56,48},{64,72... | collective-permute-start | bytes 1544 | tf_op jit(solution)/shard_map/ppermute | solution.py:31
  102.2 1.5 %collective-permute-done.12 = bf16[136,384]{1,0:T(8,128)(2,1)S(1)} collective-permute-done((bf16[136,384]{1,0:T(8,128)(2,1)S(1)}, bf16[136,384]{1,0:T(8,128)(2,1)S(1)}, u32[]{:S(2)}, u32[]{:S(2)}) %collective-permute-start.12) | collective-permute-done | bytes 104480 | tf_op jit(solution)/shard_map/ppermute | solution.py:31
  105.3 5.1 %all-to-all-start.1 = ((bf16[8,88,384]{2,1,0:T(8,128)(2,1)}), bf16[8,88,384]{2,1,0:T(8,128)(2,1)S(1)}, u32[]{:S(2)}, u32[]{:S(2)}) async-start(bf16[8,88,384]{2,1,0:T(8,128)(2,1)} %fusion.15), calls=%async_computation.1 | async-start | bytes 1081344 | tf_op jit(solution)/shard_map/all_to_all | solution.py:197
  110.4 3.9 %fusion = bf16[1,6144,168]{1,2,0:T(8,128)(2,1)} fusion(bf16[256,168]{0,1:T(8,128)(2,1)S(1)} %pad_maximum_fusion.17, bf16[256,12416]{1,0:T(8,128)(2,1)} %copy-done.1), kind=kOutput, calls=%fused_computation.35 | convolution fusion | flops 529514496 | bytes 5296128 | tf_op jit(solution)/shard_map/dot_general | solution.py:35
  114.3 4.9 %all-to-all-done.1 = bf16[8,88,384]{2,1,0:T(8,128)(2,1)S(1)} async-done(((bf16[8,88,384]{2,1,0:T(8,128)(2,1)}), bf16[8,88,384]{2,1,0:T(8,128)(2,1)S(1)}, u32[]{:S(2)}, u32[]{:S(2)}) %all-to-all-start.1) | async-done | bytes 540704 | tf_op jit(solution)/shard_map/all_to_all | solution.py:197
  119.8 3.6 %collective-permute-start.16 = (f32[8,3200]{1,0:T(8,128)S(1)}, f32[8,3200]{1,0:T(8,128)S(1)}, u32[]{:S(2)}, u32[]{:S(2)}) collective-permute-start(f32[8,3200]{1,0:T(8,128)S(1)} %select_maximum_fusion), channel_id=1, source_target_pairs={{0,8},{8,0},{16,24},{24,16},{32,40},{40,32},{48,56},{56,48},{64,72... | collective-permute-start | bytes 307208 | tf_op jit(solution)/shard_map/ppermute | solution.py:31
  (161 shorter events, 24.6 us)
Async XLA Ops:
  0.6 14.8 %collective-permute-start = (bf16[168,6144]{1,0:T(8,128)(2,1)}, bf16[168,6144]{1,0:T(8,128)(2,1)}, u32[]{:S(2)}, u32[]{:S(2)}) collective-permute-start(bf16[168,6144]{1,0:T(8,128)(2,1)} %bitcast.114), channel_id=1, source_target_pairs={{0,8},{8,0},{16,24},{24,16},{32,40},{40,32},{48,56},{56,48},{64,72... | collective-permute-start | bytes 6193160 | tf_op jit(solution)/shard_map/ppermute | solution.py:31
  4.0 18.3 %collective-permute-start.1 = (bf16[168,6144]{1,0:T(8,128)(2,1)}, bf16[168,6144]{1,0:T(8,128)(2,1)}, u32[]{:S(2)}, u32[]{:S(2)}) collective-permute-start(bf16[168,6144]{1,0:T(8,128)(2,1)} %bitcast.120), channel_id=1, source_target_pairs={{0,8},{8,0},{16,24},{24,16},{32,40},{40,32},{48,56},{56,48},{64,72... | collective-permute-start | bytes 6193160 | tf_op jit(solution)/shard_map/ppermute | solution.py:31
  9.7 5.8 %copy-start = (bf16[1,6144,168]{1,2,0:T(8,128)(2,1)S(1)}, bf16[1,6144,168]{1,2,0:T(8,128)(2,1)}, u32[]{:S(2)}) copy-start(bf16[1,6144,168]{1,2,0:T(8,128)(2,1)} %param.10) | copy-start | bytes 6193156
  9.7 42.9 %all-to-all-start = ((bf16[8,16,12416]{2,1,0:T(8,128)(2,1)}), bf16[8,16,12416]{2,1,0:T(8,128)(2,1)}, u32[]{:S(2)}, u32[]{:S(2)}) async-start(bf16[8,16,12416]{2,1,0:T(8,128)(2,1)} %bitcast.119), calls=%async_computation | async-start | bytes 6356992 | tf_op jit(solution)/shard_map/all_to_all | solution.py:80
  52.6 5.4 %copy-start.2 = (bf16[336,6144]{1,0:T(8,128)(2,1)S(1)}, bf16[336,6144]{1,0:T(8,128)(2,1)}, u32[]{:S(2)}) copy-start(bf16[336,6144]{1,0:T(8,128)(2,1)} %pad_maximum_fusion.1) | copy-start | bytes 12386308
  60.7 8.1 %copy-start.5 = (bf16[336,1536]{1,0:T(8,128)(2,1)S(1)}, bf16[336,1536]{1,0:T(8,128)(2,1)}, u32[]{:S(2)}) copy-start(bf16[336,1536]{1,0:T(8,128)(2,1)} %get-tuple-element.48) | copy-start | bytes 3096580
  61.3 13.3 %collective-permute-start.4 = (bf16[128,12416]{1,0:T(8,128)(2,1)}, bf16[128,12416]{1,0:T(8,128)(2,1)}, u32[]{:S(2)}, u32[]{:S(2)}) collective-permute-start(bf16[128,12416]{1,0:T(8,128)(2,1)} %bitcast.2), channel_id=1, source_target_pairs={{0,8},{8,0},{16,24},{24,16},{32,40},{40,32},{48,56},{56,48},{64,72... | collective-permute-start | bytes 9535496 | tf_op jit(solution)/shard_map/ppermute | solution.py:31
  62.6 12.0 %collective-permute-start.6 = (f32[128,8]{0,1:T(8,128)S(1)}, f32[128,8]{0,1:T(8,128)S(1)}, u32[]{:S(2)}, u32[]{:S(2)}) collective-permute-start(f32[128,8]{0,1:T(8,128)S(1)} %subtract_multiply_fusion), channel_id=1, source_target_pairs={{0,8},{8,0},{16,24},{24,16},{32,40},{40,32},{48,56},{56,48},{64,72... | collective-permute-start | bytes 12296 | tf_op jit(solution)/shard_map/ppermute | solution.py:31
  62.7 11.9 %copy-start.4 = (bf16[336,1536]{1,0:T(8,128)(2,1)S(1)}, bf16[336,1536]{1,0:T(8,128)(2,1)}, u32[]{:S(2)}) copy-start(bf16[336,1536]{1,0:T(8,128)(2,1)} %get-tuple-element.55) | copy-start | bytes 3096580
  62.7 11.8 %collective-permute-start.5 = (bf16[128,336]{0,1:T(8,128)(2,1)S(1)}, bf16[128,336]{0,1:T(8,128)(2,1)S(1)}, u32[]{:S(2)}, u32[]{:S(2)}) collective-permute-start(bf16[128,336]{0,1:T(8,128)(2,1)S(1)} %pad_maximum_fusion.16), channel_id=1, source_target_pairs={{0,8},{8,0},{16,24},{24,16},{32,40},{40,32},{48,56},{56,48},{64,72... | collective-permute-start | bytes 258056 | tf_op jit(solution)/shard_map/ppermute | solution.py:31
  63.2 11.0 %collective-permute-start.2 = (bf16[136,768]{1,0:T(8,128)(2,1)S(1)}, bf16[136,768]{1,0:T(8,128)(2,1)S(1)}, u32[]{:S(2)}, u32[]{:S(2)}) collective-permute-start(bf16[136,768]{1,0:T(8,128)(2,1)S(1)} %get-tuple-element.46), channel_id=1, source_target_pairs={{0,16},{8,24},{16,32},{24,40},{32,48},{40,56},{48,64},{56,72},{64,... | collective-permute-start | bytes 626696 | tf_op jit(solution)/shard_map/ppermute | solution.py:31
  64.9 9.4 %collective-permute-start.3 = (bf16[136,768]{1,0:T(8,128)(2,1)S(1)}, bf16[136,768]{1,0:T(8,128)(2,1)S(1)}, u32[]{:S(2)}, u32[]{:S(2)}) collective-permute-start(bf16[136,768]{1,0:T(8,128)(2,1)S(1)} %get-tuple-element.49), channel_id=1, source_target_pairs={{0,112},{8,120},{16,0},{24,8},{32,16},{40,24},{48,32},{56,40},{64,... | collective-permute-start | bytes 626696 | tf_op jit(solution)/shard_map/ppermute | solution.py:31
  75.0 7.4 %collective-permute-start.7 = (bf16[136,768]{1,0:T(8,128)(2,1)S(1)}, bf16[136,768]{1,0:T(8,128)(2,1)S(1)}, u32[]{:S(2)}, u32[]{:S(2)}) collective-permute-start(bf16[136,768]{1,0:T(8,128)(2,1)S(1)} %pad_maximum_fusion.9), channel_id=1, source_target_pairs={{0,16},{8,24},{16,32},{24,40},{32,48},{40,56},{48,64},{56,72},{64,... | collective-permute-start | bytes 626696 | tf_op jit(solution)/shard_map/ppermute | solution.py:31
  75.1 7.4 %collective-permute-start.8 = (bf16[136,768]{1,0:T(8,128)(2,1)S(1)}, bf16[136,768]{1,0:T(8,128)(2,1)S(1)}, u32[]{:S(2)}, u32[]{:S(2)}) collective-permute-start(bf16[136,768]{1,0:T(8,128)(2,1)S(1)} %pad_maximum_fusion.10), channel_id=1, source_target_pairs={{0,112},{8,120},{16,0},{24,8},{32,16},{40,24},{48,32},{56,40},{64,... | collective-permute-start | bytes 626696 | tf_op jit(solution)/shard_map/ppermute | solution.py:31
  82.8 6.5 %collective-permute-start.9 = (bf16[136,768]{1,0:T(8,128)(2,1)S(1)}, bf16[136,768]{1,0:T(8,128)(2,1)S(1)}, u32[]{:S(2)}, u32[]{:S(2)}) collective-permute-start(bf16[136,768]{1,0:T(8,128)(2,1)S(1)} %pad_maximum_fusion.11), channel_id=1, source_target_pairs={{0,16},{8,24},{16,32},{24,40},{32,48},{40,56},{48,64},{56,72},{64,... | collective-permute-start | bytes 626696 | tf_op jit(solution)/shard_map/ppermute | solution.py:31
  83.8 6.4 %collective-permute-start.11 = (bf16[136,768]{1,0:T(8,128)(2,1)S(1)}, bf16[136,768]{1,0:T(8,128)(2,1)S(1)}, u32[]{:S(2)}, u32[]{:S(2)}) collective-permute-start(bf16[136,768]{1,0:T(8,128)(2,1)S(1)} %pad_maximum_fusion.12), channel_id=1, source_target_pairs={{0,112},{8,120},{16,0},{24,8},{32,16},{40,24},{48,32},{56,40},{64,... | collective-permute-start | bytes 626696 | tf_op jit(solution)/shard_map/ppermute | solution.py:31
  89.4 11.4 %copy-start.13 = (s32[128,2]{0,1:T(2,128)S(1)}, s32[128,2]{0,1:T(2,128)}, u32[]{:S(2)}) copy-start(s32[128,2]{0,1:T(2,128)} %param.12) | copy-start | bytes 3076
  89.6 5.9 %collective-permute-start.10 = (bf16[136,768]{1,0:T(8,128)(2,1)S(1)}, bf16[136,768]{1,0:T(8,128)(2,1)S(1)}, u32[]{:S(2)}, u32[]{:S(2)}) collective-permute-start(bf16[136,768]{1,0:T(8,128)(2,1)S(1)} %pad_maximum_fusion.13), channel_id=1, source_target_pairs={{0,16},{8,24},{16,32},{24,40},{32,48},{40,56},{48,64},{56,72},{64,... | collective-permute-start | bytes 626696 | tf_op jit(solution)/shard_map/ppermute | solution.py:31
  95.7 5.2 %collective-permute-start.13 = (f32[1,128]{1,0:T(1,128)S(1)}, f32[1,128]{1,0:T(1,128)S(1)}, u32[]{:S(2)}, u32[]{:S(2)}) collective-permute-start(f32[1,128]{1,0:T(1,128)S(1)} %get-tuple-element.93), channel_id=1, source_target_pairs={{0,8},{8,0},{16,24},{24,16},{32,40},{40,32},{48,56},{56,48},{64,72... | collective-permute-start | bytes 1544 | tf_op jit(solution)/shard_map/ppermute | solution.py:31
  99.2 3.0 %collective-permute-start.14 = (f32[1,128]{1,0:T(1,128)S(1)}, f32[1,128]{1,0:T(1,128)S(1)}, u32[]{:S(2)}, u32[]{:S(2)}) collective-permute-start(f32[1,128]{1,0:T(1,128)S(1)} %get-tuple-element.93), channel_id=1, source_target_pairs={{0,136},{8,128},{16,152},{24,144},{32,168},{40,160},{48,184},{56,1... | collective-permute-start | bytes 1544 | tf_op jit(solution)/shard_map/ppermute | solution.py:31
  99.6 4.2 %collective-permute-start.12 = (bf16[136,384]{1,0:T(8,128)(2,1)S(1)}, bf16[136,384]{1,0:T(8,128)(2,1)S(1)}, u32[]{:S(2)}, u32[]{:S(2)}) collective-permute-start(bf16[136,384]{1,0:T(8,128)(2,1)S(1)} %pad_maximum_fusion.15), channel_id=1, source_target_pairs={{0,128},{8,136},{16,144},{24,152},{32,160},{40,168},{48,176},{56,1... | collective-permute-start | bytes 313352 | tf_op jit(solution)/shard_map/ppermute | solution.py:31
  105.3 13.9 %all-to-all-start.1 = ((bf16[8,88,384]{2,1,0:T(8,128)(2,1)}), bf16[8,88,384]{2,1,0:T(8,128)(2,1)S(1)}, u32[]{:S(2)}, u32[]{:S(2)}) async-start(bf16[8,88,384]{2,1,0:T(8,128)(2,1)} %fusion.15), calls=%async_computation.1 | async-start | bytes 1081344 | tf_op jit(solution)/shard_map/all_to_all | solution.py:197
  119.8 4.5 %collective-permute-start.16 = (f32[8,3200]{1,0:T(8,128)S(1)}, f32[8,3200]{1,0:T(8,128)S(1)}, u32[]{:S(2)}, u32[]{:S(2)}) collective-permute-start(f32[8,3200]{1,0:T(8,128)S(1)} %select_maximum_fusion), channel_id=1, source_target_pairs={{0,8},{8,0},{16,24},{24,16},{32,40},{40,32},{48,56},{56,48},{64,72... | collective-permute-start | bytes 307208 | tf_op jit(solution)/shard_map/ppermute | solution.py:31
  123.4 1.3 %collective-permute-start.15 = (bf16[128,192]{1,0:T(8,128)(2,1)S(1)}, bf16[128,192]{1,0:T(8,128)(2,1)S(1)}, u32[]{:S(2)}, u32[]{:S(2)}) collective-permute-start(bf16[128,192]{1,0:T(8,128)(2,1)S(1)} %select_convert_fusion), channel_id=1, source_target_pairs={{0,8},{8,0},{16,24},{24,16},{32,40},{40,32},{48,56},{56,48},{64,72... | collective-permute-start | bytes 147464 | tf_op jit(solution)/shard_map/ppermute | solution.py:31
  (9 other events, 23.4 us)

commit v6 on v5

--- a/solution.py
+++ b/solution.py
@@ -89,6 +89,8 @@
     second_gate = 1.0 / (1.0 + jnp.exp(chosen[:, 0] - chosen[:, 1]))
 
     w_ext = jnp.concatenate([w_in, router_parts.T], axis=0)
+    id_row = jnp.where(jnp.arange(width + 128)[None] == width, 1.0, 0.0).astype(BF16)
+    w_ext = jnp.concatenate([jnp.pad(w_ext, ((0, 0), (0, 128))), id_row], axis=0)
 
     def weights(k):
         at = (z + k) % Z
@@ -101,14 +103,14 @@
     hidden_count = w_in.shape[0]
 
     def act(part_rows):
-        ext = dot(part_rows[:, width : 2 * width], w_ext, ((1,), (1,)))
+        ext = dot(part_rows[:, width:], w_ext, ((1,), (1,)))
         back = dot(part_rows[:, :width], w_out, ((1,), (1,)))
         pre = ext[:, :hidden_count]
         row_logits = ext[:, hidden_count : hidden_count + experts] + (
             ext[:, hidden_count + experts : hidden_count + 2 * experts]
-            + ext[:, hidden_count + 2 * experts :]
+            + ext[:, hidden_count + 2 * experts : hidden_count + 3 * experts]
         )
-        second = part_rows[:, 2 * width : 2 * width + 1].astype(jnp.int32) - me
+        second = ext[:, hidden_count + 3 * experts :].astype(jnp.int32) - me
         ids = jnp.arange(experts, dtype=jnp.int32)[None, :]
         gap = jnp.sum(
             jnp.where(ids == second, row_logits, 0.0) - jnp.where(ids == me, row_logits, 0.0),
@@ -212,11 +214,11 @@
     back_scores = jnp.sum(home[:, half : half + 8, :half].astype(F32), axis=1)
     router_mine = jnp.sum(home[:, half + 8 :].astype(F32), axis=0) / (tok_rows * EP)
     router_mine = router_mine.reshape(experts, core_cols)
-    merged = dot(spread_abs, returned, ((1,), (0,)))
+    merged = dot(returned, spread_abs, ((0,), (1,)))
     taken = jnp.sum(
         jnp.where(places_abs, back_scores.reshape(1, 1, rows), 0.0), axis=2
     )
-    low_cols, high_cols = merged[:, :own_cols], merged[:, own_cols:]
+    low_cols, high_cols = merged[:own_cols], merged[own_cols:]
     keep = jnp.where(core == 0, low_cols, high_cols)
     give = jnp.where(core == 0, high_cols, low_cols)
     expert_grad = keep + send(give.astype(BF16), TO_CORE).astype(F32)
@@ -236,9 +238,10 @@
 
     router_rows = lax.dynamic_slice_in_dim(router_weight, fsdp_index * own_cols, own_cols, 0)
     grad_tokens = (
-        expert_grad + jnp.dot(logit_grad, router_rows.T, precision=lax.Precision.HIGHEST)
+        expert_grad
+        + sum(router_rows[:, e : e + 1] * logit_grad.T[e : e + 1] for e in range(experts))
     ).astype(BF16)
-    return grad_tokens, grad_in.T[None], grad_out[None], grad_router.T
+    return grad_tokens.T, grad_in.T[None], grad_out[None], grad_router.T
 
 
 def solution(mesh):

time: 128 us -> 127 us (level)
  waiting for transfers between devices: 43.5 us -> 41 us
  other arithmetic: 19.5 us -> 21.5 us
  starting transfers between devices: 35.4 us -> 33.7 us
    concatenate x0 -> x1, other arithmetic: none -> 2.42 us  [per_device(): jnp.concatenate([jnp.pad(w_ext, ((0, 0), (0, 128))), id_row], axis=0)]
    all_to_all x1, waiting for transfers between devices: 22.9 us -> 20.6 us  [per_device(): lax.all_to_all(send_rows.reshape(experts, half, 2 * width + 128), 'ep', 0...]
    dot_general x12, matrix products: 20.1 us -> 21.5 us  [dot(): lax.dot_general(left, right, (dims, ((), ())), preferred_element_type=F32)]
    unnamed x31 -> x28, local copies, waits for them, and re-layouts: 3.23 us -> 2.49 us
  transfers between devices with their start and end apart: 19 -> 19, of which waited for: 9 -> 7; matrix products, arithmetic and copies ran while one was open for 25% -> 30% of each run, Pallas kernels for 0% -> 0%
where the time goes in v6:
time: 127 us; the launch traced here: 126 us
  waiting for transfers between devices  41 us (32%)
  starting transfers between devices  33.7 us (27%)
  other arithmetic  21.5 us (17%)
  matrix products  21.5 us (17%)
  local copies, waits for them, and re-layouts  6.48 us (5%)
  between operations  1.65 us (1%)
    ppermute x17, starting transfers between devices, send(): return lax.ppermute(array, 'fsdp', pairs)  24.2 us
    dot_general x12, matrix products, dot(): lax.dot_general(left, right, (dims, ((), ())), preferred_element_type=F32)  21.5 us
    all_to_all x1, waiting for transfers between devices, per_device(): lax.all_to_all(send_rows.reshape(experts, half, 2 * width + 128), 'ep', 0...  20.6 us
    ppermute x17, waiting for transfers between devices, send(): return lax.ppermute(array, 'fsdp', pairs)  15.6 us
    all_to_all x1, starting transfers between devices, per_device(): lax.all_to_all(send_rows.reshape(experts, half, 2 * width + 128), 'ep', 0...  5.05 us
    all_to_all x1, waiting for transfers between devices, per_device(): lax.all_to_all(jnp.concatenate([own.astype(BF16).reshape(experts, half, s...  4.71 us
    all_to_all x1, starting transfers between devices, per_device(): lax.all_to_all(jnp.concatenate([own.astype(BF16).reshape(experts, half, s...  4.5 us
    concatenate x3, other arithmetic, per_device(): w_in = jnp.concatenate([w_in, send(w_in, TO_CORE)], axis=0)  4.11 us
  transfers between devices with their start and end apart: 19, of which 7 were waited for; matrix products, arithmetic and copies ran while one was open for 30% of the time, Pallas kernels for 0%

profile of v6, /device:TPU:1, one launch (start us, length us, event | category | flops | bytes accessed | tf_op | source)
XLA Modules:
  0.0 125.9 jit_solution(5186843582449744203)
XLA Ops:
  0.6 3.3 %collective-permute-start = (bf16[168,6144]{1,0:T(8,128)(2,1)}, bf16[168,6144]{1,0:T(8,128)(2,1)}, u32[]{:S(2)}, u32[]{:S(2)}) collective-permute-start(bf16[168,6144]{1,0:T(8,128)(2,1)} %bitcast.145), channel_id=1, source_target_pairs={{0,8},{8,0},{16,24},{24,16},{32,40},{40,32},{48,56},{56,48},{64,72... | collective-permute-start | bytes 6193160 | tf_op jit(solution)/shard_map/ppermute | solution.py:31
  5.0 4.6 %convolution_convert_fusion = bf16[128,12416]{1,0:T(8,128)(2,1)} fusion(bf16[128,128]{1,0:T(8,128)(2,1)S(1)} %broadcast_in_dim.48, bf16[128,6144]{1,0:T(8,128)(2,1)} %param.7, bf16[128,6144]{1,0:T(8,128)(2,1)} %param.8, pred[128,2,128]{2,0,1:T(32,128)(4,1)S(1)} %iota_compare_fusion.3), kind=kOutput, calls=%fused_computation | convolution fusion | flops 417988608 | bytes 6389760 | tf_op jit(solution)/shard_map/dot_general | solution.py:35
  9.6 5.0 %all-to-all-start = ((bf16[8,16,12416]{2,1,0:T(8,128)(2,1)}), bf16[8,16,12416]{2,1,0:T(8,128)(2,1)}, u32[]{:S(2)}, u32[]{:S(2)}) async-start(bf16[8,16,12416]{2,1,0:T(8,128)(2,1)} %bitcast.150), calls=%async_computation | async-start | bytes 6356992 | tf_op jit(solution)/shard_map/all_to_all | solution.py:80
  22.2 4.0 %pad_maximum_fusion.1 = bf16[336,6144]{1,0:T(8,128)(2,1)} fusion(bf16[168,6144]{1,0:T(8,128)(2,1)} %collective-permute-done.1, bf16[168,6144]{1,0:T(8,128)(2,1)S(1)} %bitcast.152), kind=kLoop, calls=%fused_computation.43 | loop fusion | flops 8257536 | bytes 8257536 | tf_op jit(solution)/shard_map/concatenate | solution.py:69
  26.2 3.2 %fusion.5 = bf16[360,6272]{1,0:T(8,128)(2,1)S(1)} fusion(bf16[24,6144]{1,0:T(8,128)(2,1)S(1)} %fusion.46, bf16[168,6144]{1,0:T(8,128)(2,1)} %collective-permute-done, bf16[168,6144]{1,0:T(8,128)(2,1)S(1)} %bitcast.149), kind=kLoop, calls=%fused_computation.42 | loop fusion | flops 22579200 | bytes 8939520 | tf_op jit(solution)/shard_map/concatenate | solution.py:91
  29.5 2.4 %pad_maximum_fusion = bf16[361,6272]{1,0:T(8,128)(2,1)} fusion(bf16[1,6272]{1,0:T(2,128)(2,1)S(1)} %fusion.50, bf16[360,6272]{1,0:T(8,128)(2,1)S(1)} %fusion.5), kind=kLoop, calls=%fused_computation.40 | loop fusion | flops 9056768 | bytes 9056768 | tf_op jit(solution)/shard_map/concatenate | solution.py:93
  31.9 20.6 %all-to-all-done = bf16[8,16,12416]{2,1,0:T(8,128)(2,1)} async-done(((bf16[8,16,12416]{2,1,0:T(8,128)(2,1)}), bf16[8,16,12416]{2,1,0:T(8,128)(2,1)}, u32[]{:S(2)}, u32[]{:S(2)}) %all-to-all-start) | async-done | bytes 3178528 | tf_op jit(solution)/shard_map/all_to_all | solution.py:80
  52.5 4.3 %fusion.13 = f32[128,361]{0,1:T(8,128)S(1)} fusion(bf16[361,6272]{1,0:T(8,128)(2,1)} %pad_maximum_fusion, bf16[128,12416]{1,0:T(8,128)(2,1)} %bitcast.2), kind=kOutput, calls=%fused_computation.54 | convolution fusion | flops 579633152 | bytes 6406656 | tf_op jit(solution)/shard_map/dot_general | solution.py:35
  57.0 2.7 %fusion.45 = (bf16[128,336]{0,1:T(8,128)(2,1)S(1)}, bf16[128,336]{0,1:T(8,128)(2,1)S(1)}, bf16[128,336]{0,1:T(8,128)(2,1)S(1)}, f32[128,336]{0,1:T(8,128)S(1)}) fusion(f32[128]{0:T(128)S(1)} %convert_element_type.242, f32[128,361]{0,1:T(8,128)S(1)} %fusion.13, bf16[336,6144]{1,0:T(8,128)(2,1)S(1)} %copy-done.2, bf16[128,12416]{1,0:T(8,128)(2,1)} %bitcast.2), kind=kOutput, calls=%fused_computation.115 | convolution fusion | flops 529127424 | bytes 6304256 | tf_op jit(solution)/shard_map/dot_general | solution.py:35
  61.6 1.9 %convolution_bitcast_fusion = f32[128,24]{0,1:T(8,128)S(1)} fusion(bf16[128,6144]{1,0:T(8,128)(2,1)} %param.7, bf16[6144,8]{0,1:T(8,128)(2,1)S(1)} %copy-done.8, bf16[6144,8]{0,1:T(8,128)(2,1)S(1)} %copy-done.10, bf16[6144,8]{0,1:T(8,128)(2,1)S(1)} %get-tuple-element.114), kind=kOutput, calls=%fused_computation.58 | convolution fusion | flops 38633472 | bytes 1880064 | tf_op jit(solution)/shard_map/dot_general | solution.py:35
  65.8 4.0 %collective-permute-start.3 = (bf16[136,768]{1,0:T(8,128)(2,1)S(1)}, bf16[136,768]{1,0:T(8,128)(2,1)S(1)}, u32[]{:S(2)}, u32[]{:S(2)}) collective-permute-start(bf16[136,768]{1,0:T(8,128)(2,1)S(1)} %get-tuple-element.49), channel_id=1, source_target_pairs={{0,112},{8,120},{16,0},{24,8},{32,16},{40,24},{48,32},{56,40},{64,... | collective-permute-start | bytes 626696 | tf_op jit(solution)/shard_map/ppermute | solution.py:31
  70.2 5.0 %collective-permute-done.2 = bf16[136,768]{1,0:T(8,128)(2,1)S(1)} collective-permute-done((bf16[136,768]{1,0:T(8,128)(2,1)S(1)}, bf16[136,768]{1,0:T(8,128)(2,1)S(1)}, u32[]{:S(2)}, u32[]{:S(2)}) %collective-permute-start.2) | collective-permute-done | bytes 208928 | tf_op jit(solution)/shard_map/ppermute | solution.py:31
  76.1 2.7 %collective-permute-start.8 = (bf16[136,768]{1,0:T(8,128)(2,1)S(1)}, bf16[136,768]{1,0:T(8,128)(2,1)S(1)}, u32[]{:S(2)}, u32[]{:S(2)}) collective-permute-start(bf16[136,768]{1,0:T(8,128)(2,1)S(1)} %pad_maximum_fusion.10), channel_id=1, source_target_pairs={{0,112},{8,120},{16,0},{24,8},{32,16},{40,24},{48,32},{56,40},{64,... | collective-permute-start | bytes 626696 | tf_op jit(solution)/shard_map/ppermute | solution.py:31
  78.8 2.1 %constant_dynamic-update-slice_fusion.1 = bf16[256,12416]{1,0:T(8,128)(2,1)S(1)} fusion(bf16[128,12416]{1,0:T(8,128)(2,1)} %bitcast.2), kind=kLoop, calls=%fused_computation.198 | loop fusion | bytes 6356992
  80.9 2.3 %constant_dynamic-update-slice_fusion = bf16[256,12416]{1,0:T(8,128)(2,1)S(1)} fusion(bf16[256,12416]{1,0:T(8,128)(2,1)S(1)} %constant_dynamic-update-slice_fusion.1, bf16[128,12416]{1,0:T(8,128)(2,1)} %collective-permute-done.4), kind=kLoop, calls=%fused_computation.197 | loop fusion | bytes 6356992 | tf_op jit(solution)/shard_map/concatenate | solution.py:168
  84.5 2.1 %collective-permute-start.11 = (bf16[136,768]{1,0:T(8,128)(2,1)S(1)}, bf16[136,768]{1,0:T(8,128)(2,1)S(1)}, u32[]{:S(2)}, u32[]{:S(2)}) collective-permute-start(bf16[136,768]{1,0:T(8,128)(2,1)S(1)} %pad_maximum_fusion.12), channel_id=1, source_target_pairs={{0,112},{8,120},{16,0},{24,8},{32,16},{40,24},{48,32},{56,40},{64,... | collective-permute-start | bytes 626696 | tf_op jit(solution)/shard_map/ppermute | solution.py:31
  86.6 2.0 %convolution_convert_fusion.2 = bf16[168,6144]{1,0:T(8,128)(2,1)} fusion(bf16[256,168]{0,1:T(8,128)(2,1)S(1)} %pad_maximum_fusion.18, bf16[256,12416]{1,0:T(8,128)(2,1)S(1)} %constant_dynamic-update-slice_fusion), kind=kOutput, calls=%fused_computation.38 | convolution fusion | flops 529514496 | bytes 5296128 | tf_op jit(solution)/shard_map/dot_general | solution.py:35
  90.7 5.8 %collective-permute-done.10 = bf16[136,768]{1,0:T(8,128)(2,1)S(1)} collective-permute-done((bf16[136,768]{1,0:T(8,128)(2,1)S(1)}, bf16[136,768]{1,0:T(8,128)(2,1)S(1)}, u32[]{:S(2)}, u32[]{:S(2)}) %collective-permute-start.10) | collective-permute-done | bytes 208928 | tf_op jit(solution)/shard_map/ppermute | solution.py:31
  97.1 3.8 %collective-permute-start.13 = (f32[1,128]{1,0:T(1,128)S(1)}, f32[1,128]{1,0:T(1,128)S(1)}, u32[]{:S(2)}, u32[]{:S(2)}) collective-permute-start(f32[1,128]{1,0:T(1,128)S(1)} %get-tuple-element.77), channel_id=1, source_target_pairs={{0,8},{8,0},{16,24},{24,16},{32,40},{40,32},{48,56},{56,48},{64,72... | collective-permute-start | bytes 1544 | tf_op jit(solution)/shard_map/ppermute | solution.py:31
  101.9 2.6 %collective-permute-done.14 = f32[1,128]{1,0:T(1,128)S(1)} collective-permute-done((f32[1,128]{1,0:T(1,128)S(1)}, f32[1,128]{1,0:T(1,128)S(1)}, u32[]{:S(2)}, u32[]{:S(2)}) %collective-permute-start.14) | collective-permute-done | bytes 544 | tf_op jit(solution)/shard_map/ppermute | solution.py:31
  106.0 4.5 %all-to-all-start.1 = ((bf16[8,88,384]{2,1,0:T(8,128)(2,1)}), bf16[8,88,384]{2,1,0:T(8,128)(2,1)S(1)}, u32[]{:S(2)}, u32[]{:S(2)}) async-start(bf16[8,88,384]{2,1,0:T(8,128)(2,1)} %fusion.20), calls=%async_computation.1 | async-start | bytes 1081344 | tf_op jit(solution)/shard_map/all_to_all | solution.py:199
  111.7 3.9 %fusion.3 = bf16[1,6144,168]{1,2,0:T(8,128)(2,1)} fusion(bf16[256,168]{0,1:T(8,128)(2,1)S(1)} %pad_maximum_fusion.17, bf16[256,12416]{1,0:T(8,128)(2,1)} %copy-done.1), kind=kOutput, calls=%fused_computation.39 | convolution fusion | flops 529514496 | bytes 5296128 | tf_op jit(solution)/shard_map/dot_general | solution.py:35
  115.5 4.7 %all-to-all-done.1 = bf16[8,88,384]{2,1,0:T(8,128)(2,1)S(1)} async-done(((bf16[8,88,384]{2,1,0:T(8,128)(2,1)}), bf16[8,88,384]{2,1,0:T(8,128)(2,1)S(1)}, u32[]{:S(2)}, u32[]{:S(2)}) %all-to-all-start.1) | async-done | bytes 540704 | tf_op jit(solution)/shard_map/all_to_all | solution.py:199
  120.9 2.4 %collective-permute-start.16 = (f32[8,3200]{1,0:T(8,128)S(1)}, f32[8,3200]{1,0:T(8,128)S(1)}, u32[]{:S(2)}, u32[]{:S(2)}) collective-permute-start(f32[8,3200]{1,0:T(8,128)S(1)} %select_maximum_fusion), channel_id=1, source_target_pairs={{0,8},{8,0},{16,24},{24,16},{32,40},{40,32},{48,56},{56,48},{64,72... | collective-permute-start | bytes 307208 | tf_op jit(solution)/shard_map/ppermute | solution.py:31
  (163 shorter events, 24.2 us)
Async XLA Ops:
  0.6 14.8 %collective-permute-start = (bf16[168,6144]{1,0:T(8,128)(2,1)}, bf16[168,6144]{1,0:T(8,128)(2,1)}, u32[]{:S(2)}, u32[]{:S(2)}) collective-permute-start(bf16[168,6144]{1,0:T(8,128)(2,1)} %bitcast.145), channel_id=1, source_target_pairs={{0,8},{8,0},{16,24},{24,16},{32,40},{40,32},{48,56},{56,48},{64,72... | collective-permute-start | bytes 6193160 | tf_op jit(solution)/shard_map/ppermute | solution.py:31
  4.0 18.2 %collective-permute-start.1 = (bf16[168,6144]{1,0:T(8,128)(2,1)}, bf16[168,6144]{1,0:T(8,128)(2,1)}, u32[]{:S(2)}, u32[]{:S(2)}) collective-permute-start(bf16[168,6144]{1,0:T(8,128)(2,1)} %bitcast.151), channel_id=1, source_target_pairs={{0,8},{8,0},{16,24},{24,16},{32,40},{40,32},{48,56},{56,48},{64,72... | collective-permute-start | bytes 6193160 | tf_op jit(solution)/shard_map/ppermute | solution.py:31
  9.6 5.1 %copy-start.11 = (f32[6144,8]{0,1:T(8,128)S(1)}, f32[6144,8]{0,1:T(8,128)}, u32[]{:S(2)}) copy-start(f32[6144,8]{0,1:T(8,128)} %param.9) | copy-start | bytes 589828
  9.6 5.8 %copy-start = (bf16[1,6144,168]{1,2,0:T(8,128)(2,1)S(1)}, bf16[1,6144,168]{1,2,0:T(8,128)(2,1)}, u32[]{:S(2)}) copy-start(bf16[1,6144,168]{1,2,0:T(8,128)(2,1)} %param.10) | copy-start | bytes 6193156
  9.6 42.9 %all-to-all-start = ((bf16[8,16,12416]{2,1,0:T(8,128)(2,1)}), bf16[8,16,12416]{2,1,0:T(8,128)(2,1)}, u32[]{:S(2)}, u32[]{:S(2)}) async-start(bf16[8,16,12416]{2,1,0:T(8,128)(2,1)} %bitcast.150), calls=%async_computation | async-start | bytes 6356992 | tf_op jit(solution)/shard_map/all_to_all | solution.py:80
  59.7 10.1 %copy-start.5 = (bf16[336,1536]{1,0:T(8,128)(2,1)S(1)}, bf16[336,1536]{1,0:T(8,128)(2,1)}, u32[]{:S(2)}) copy-start(bf16[336,1536]{1,0:T(8,128)(2,1)} %get-tuple-element.48) | copy-start | bytes 3096580
  60.3 15.2 %collective-permute-start.4 = (bf16[128,12416]{1,0:T(8,128)(2,1)}, bf16[128,12416]{1,0:T(8,128)(2,1)}, u32[]{:S(2)}, u32[]{:S(2)}) collective-permute-start(bf16[128,12416]{1,0:T(8,128)(2,1)} %bitcast.2), channel_id=1, source_target_pairs={{0,8},{8,0},{16,24},{24,16},{32,40},{40,32},{48,56},{56,48},{64,72... | collective-permute-start | bytes 9535496 | tf_op jit(solution)/shard_map/ppermute | solution.py:31
  63.5 12.0 %collective-permute-start.6 = (f32[128,8]{0,1:T(8,128)S(1)}, f32[128,8]{0,1:T(8,128)S(1)}, u32[]{:S(2)}, u32[]{:S(2)}) collective-permute-start(f32[128,8]{0,1:T(8,128)S(1)} %subtract_multiply_fusion), channel_id=1, source_target_pairs={{0,8},{8,0},{16,24},{24,16},{32,40},{40,32},{48,56},{56,48},{64,72... | collective-permute-start | bytes 12296 | tf_op jit(solution)/shard_map/ppermute | solution.py:31
  63.7 11.8 %copy-start.4 = (bf16[336,1536]{1,0:T(8,128)(2,1)S(1)}, bf16[336,1536]{1,0:T(8,128)(2,1)}, u32[]{:S(2)}) copy-start(bf16[336,1536]{1,0:T(8,128)(2,1)} %get-tuple-element.55) | copy-start | bytes 3096580
  63.8 11.8 %collective-permute-start.5 = (bf16[128,336]{0,1:T(8,128)(2,1)S(1)}, bf16[128,336]{0,1:T(8,128)(2,1)S(1)}, u32[]{:S(2)}, u32[]{:S(2)}) collective-permute-start(bf16[128,336]{0,1:T(8,128)(2,1)S(1)} %pad_maximum_fusion.16), channel_id=1, source_target_pairs={{0,8},{8,0},{16,24},{24,16},{32,40},{40,32},{48,56},{56,48},{64,72... | collective-permute-start | bytes 258056 | tf_op jit(solution)/shard_map/ppermute | solution.py:31
  64.2 11.0 %collective-permute-start.2 = (bf16[136,768]{1,0:T(8,128)(2,1)S(1)}, bf16[136,768]{1,0:T(8,128)(2,1)S(1)}, u32[]{:S(2)}, u32[]{:S(2)}) collective-permute-start(bf16[136,768]{1,0:T(8,128)(2,1)S(1)} %get-tuple-element.46), channel_id=1, source_target_pairs={{0,16},{8,24},{16,32},{24,40},{32,48},{40,56},{48,64},{56,72},{64,... | collective-permute-start | bytes 626696 | tf_op jit(solution)/shard_map/ppermute | solution.py:31
  65.8 9.4 %collective-permute-start.3 = (bf16[136,768]{1,0:T(8,128)(2,1)S(1)}, bf16[136,768]{1,0:T(8,128)(2,1)S(1)}, u32[]{:S(2)}, u32[]{:S(2)}) collective-permute-start(bf16[136,768]{1,0:T(8,128)(2,1)S(1)} %get-tuple-element.49), channel_id=1, source_target_pairs={{0,112},{8,120},{16,0},{24,8},{32,16},{40,24},{48,32},{56,40},{64,... | collective-permute-start | bytes 626696 | tf_op jit(solution)/shard_map/ppermute | solution.py:31
  76.0 7.4 %collective-permute-start.7 = (bf16[136,768]{1,0:T(8,128)(2,1)S(1)}, bf16[136,768]{1,0:T(8,128)(2,1)S(1)}, u32[]{:S(2)}, u32[]{:S(2)}) collective-permute-start(bf16[136,768]{1,0:T(8,128)(2,1)S(1)} %pad_maximum_fusion.9), channel_id=1, source_target_pairs={{0,16},{8,24},{16,32},{24,40},{32,48},{40,56},{48,64},{56,72},{64,... | collective-permute-start | bytes 626696 | tf_op jit(solution)/shard_map/ppermute | solution.py:31
  76.1 7.4 %collective-permute-start.8 = (bf16[136,768]{1,0:T(8,128)(2,1)S(1)}, bf16[136,768]{1,0:T(8,128)(2,1)S(1)}, u32[]{:S(2)}, u32[]{:S(2)}) collective-permute-start(bf16[136,768]{1,0:T(8,128)(2,1)S(1)} %pad_maximum_fusion.10), channel_id=1, source_target_pairs={{0,112},{8,120},{16,0},{24,8},{32,16},{40,24},{48,32},{56,40},{64,... | collective-permute-start | bytes 626696 | tf_op jit(solution)/shard_map/ppermute | solution.py:31
  83.7 4.9 %copy-start.3 = (bf16[336,1536]{1,0:T(8,128)(2,1)S(1)}, bf16[336,1536]{1,0:T(8,128)(2,1)}, u32[]{:S(2)}) copy-start(bf16[336,1536]{1,0:T(8,128)(2,1)} %get-tuple-element.65) | copy-start | bytes 3096580
  83.8 6.5 %collective-permute-start.9 = (bf16[136,768]{1,0:T(8,128)(2,1)S(1)}, bf16[136,768]{1,0:T(8,128)(2,1)S(1)}, u32[]{:S(2)}, u32[]{:S(2)}) collective-permute-start(bf16[136,768]{1,0:T(8,128)(2,1)S(1)} %pad_maximum_fusion.11), channel_id=1, source_target_pairs={{0,16},{8,24},{16,32},{24,40},{32,48},{40,56},{48,64},{56,72},{64,... | collective-permute-start | bytes 626696 | tf_op jit(solution)/shard_map/ppermute | solution.py:31
  84.5 6.1 %collective-permute-start.11 = (bf16[136,768]{1,0:T(8,128)(2,1)S(1)}, bf16[136,768]{1,0:T(8,128)(2,1)S(1)}, u32[]{:S(2)}, u32[]{:S(2)}) collective-permute-start(bf16[136,768]{1,0:T(8,128)(2,1)S(1)} %pad_maximum_fusion.12), channel_id=1, source_target_pairs={{0,112},{8,120},{16,0},{24,8},{32,16},{40,24},{48,32},{56,40},{64,... | collective-permute-start | bytes 626696 | tf_op jit(solution)/shard_map/ppermute | solution.py:31
  90.5 5.9 %collective-permute-start.10 = (bf16[136,768]{1,0:T(8,128)(2,1)S(1)}, bf16[136,768]{1,0:T(8,128)(2,1)S(1)}, u32[]{:S(2)}, u32[]{:S(2)}) collective-permute-start(bf16[136,768]{1,0:T(8,128)(2,1)S(1)} %pad_maximum_fusion.13), channel_id=1, source_target_pairs={{0,16},{8,24},{16,32},{24,40},{32,48},{40,56},{48,64},{56,72},{64,... | collective-permute-start | bytes 626696 | tf_op jit(solution)/shard_map/ppermute | solution.py:31
  96.7 7.9 %collective-permute-start.12 = (bf16[136,384]{1,0:T(8,128)(2,1)S(1)}, bf16[136,384]{1,0:T(8,128)(2,1)S(1)}, u32[]{:S(2)}, u32[]{:S(2)}) collective-permute-start(bf16[136,384]{1,0:T(8,128)(2,1)S(1)} %pad_maximum_fusion.15), channel_id=1, source_target_pairs={{0,128},{8,136},{16,144},{24,152},{32,160},{40,168},{48,176},{56,1... | collective-permute-start | bytes 313352 | tf_op jit(solution)/shard_map/ppermute | solution.py:31
  97.1 4.8 %collective-permute-start.13 = (f32[1,128]{1,0:T(1,128)S(1)}, f32[1,128]{1,0:T(1,128)S(1)}, u32[]{:S(2)}, u32[]{:S(2)}) collective-permute-start(f32[1,128]{1,0:T(1,128)S(1)} %get-tuple-element.77), channel_id=1, source_target_pairs={{0,8},{8,0},{16,24},{24,16},{32,40},{40,32},{48,56},{56,48},{64,72... | collective-permute-start | bytes 1544 | tf_op jit(solution)/shard_map/ppermute | solution.py:31
  100.8 3.7 %collective-permute-start.14 = (f32[1,128]{1,0:T(1,128)S(1)}, f32[1,128]{1,0:T(1,128)S(1)}, u32[]{:S(2)}, u32[]{:S(2)}) collective-permute-start(f32[1,128]{1,0:T(1,128)S(1)} %get-tuple-element.77), channel_id=1, source_target_pairs={{0,136},{8,128},{16,152},{24,144},{32,168},{40,160},{48,184},{56,1... | collective-permute-start | bytes 1544 | tf_op jit(solution)/shard_map/ppermute | solution.py:31
  106.0 14.2 %all-to-all-start.1 = ((bf16[8,88,384]{2,1,0:T(8,128)(2,1)}), bf16[8,88,384]{2,1,0:T(8,128)(2,1)S(1)}, u32[]{:S(2)}, u32[]{:S(2)}) async-start(bf16[8,88,384]{2,1,0:T(8,128)(2,1)} %fusion.20), calls=%async_computation.1 | async-start | bytes 1081344 | tf_op jit(solution)/shard_map/all_to_all | solution.py:199
  120.9 3.3 %collective-permute-start.16 = (f32[8,3200]{1,0:T(8,128)S(1)}, f32[8,3200]{1,0:T(8,128)S(1)}, u32[]{:S(2)}, u32[]{:S(2)}) collective-permute-start(f32[8,3200]{1,0:T(8,128)S(1)} %select_maximum_fusion), channel_id=1, source_target_pairs={{0,8},{8,0},{16,24},{24,16},{32,40},{40,32},{48,56},{56,48},{64,72... | collective-permute-start | bytes 307208 | tf_op jit(solution)/shard_map/ppermute | solution.py:31
  123.3 1.7 %collective-permute-start.15 = (bf16[192,128]{1,0:T(8,128)(2,1)S(1)}, bf16[192,128]{1,0:T(8,128)(2,1)S(1)}, u32[]{:S(2)}, u32[]{:S(2)}) collective-permute-start(bf16[192,128]{1,0:T(8,128)(2,1)S(1)} %select_convert_fusion), channel_id=1, source_target_pairs={{0,8},{8,0},{16,24},{24,16},{32,40},{40,32},{48,56},{56,48},{64,72... | collective-permute-start | bytes 147464 | tf_op jit(solution)/shard_map/ppermute | solution.py:31
  (8 other events, 17.7 us)

commit v7 on v6

--- a/solution.py
+++ b/solution.py
@@ -99,11 +99,16 @@
     orders = [(4, 5), (3, 6), (2, 7), (1, 0)]
     near = [jnp.concatenate(weights(a) + weights(b), axis=1) for a, b in orders]
 
-    mine_rows, w_ext, w_out, near = lax.optimization_barrier((mine_rows, w_ext, w_out, near))
+    w_ext = (w_ext[:, :core_cols], w_ext[:, core_cols:])
+    ready = (w_ext, w_out, near, first_gate, second_gate, chosen_hot)
+    mine_rows, ready = lax.optimization_barrier((mine_rows, ready))
+    w_ext, w_out, near, first_gate, second_gate, chosen_hot = ready
     hidden_count = w_in.shape[0]
 
     def act(part_rows):
-        ext = dot(part_rows[:, width:], w_ext, ((1,), (1,)))
+        middle = width + core_cols
+        ext = dot(part_rows[:, width:middle], w_ext[0], ((1,), (1,)))
+        ext = ext + dot(part_rows[:, middle:], w_ext[1], ((1,), (1,)))
         back = dot(part_rows[:, :width], w_out, ((1,), (1,)))
         pre = ext[:, :hidden_count]
         row_logits = ext[:, hidden_count : hidden_count + experts] + (

time: 127 us -> 125 us (0.984)
  starting transfers between devices: 33.7 us -> 32.3 us
    all_to_all x1, waiting for transfers between devices: 20.6 us -> 13.8 us  [per_device(): lax.all_to_all(send_rows.reshape(experts, half, 2 * width + 128), 'ep', 0...]
    ppermute x17, waiting for transfers between devices: 15.6 us -> 22.2 us  [send(): return lax.ppermute(array, 'fsdp', pairs)]
    ppermute x17, starting transfers between devices: 24.2 us -> 20.2 us  [send(): return lax.ppermute(array, 'fsdp', pairs)]
    all_to_all x1, starting transfers between devices: 5.05 us -> 7.61 us  [per_device(): lax.all_to_all(send_rows.reshape(experts, half, 2 * width + 128), 'ep', 0...]
    concatenate x1, other arithmetic: 2.42 us -> 0.17 us  [per_device(): jnp.concatenate([jnp.pad(w_ext, ((0, 0), (0, 128))), id_row], axis=0)]
    slice x0 -> x1, other arithmetic: none -> 1.68 us  [per_device(): w_ext = (w_ext[:, :core_cols], w_ext[:, core_cols:])]
    unnamed x28 -> x22, local copies, waits for them, and re-layouts: 2.49 us -> 3.65 us
    dot_general x12 -> x13, matrix products: 21.5 us -> 21.2 us  [dot(): lax.dot_general(left, right, (dims, ((), ())), preferred_element_type=F32)]
  transfers between devices with their start and end apart: 19 -> 19, of which waited for: 7 -> 10; matrix products, arithmetic and copies ran while one was open for 30% -> 26% of each run, Pallas kernels for 0% -> 0%
where the time goes in v7:
time: 125 us; the launch traced here: 124 us
  waiting for transfers between devices  40.7 us (33%)
  starting transfers between devices  32.3 us (26%)
  matrix products  21.2 us (17%)
  other arithmetic  20.9 us (17%)
  local copies, waits for them, and re-layouts  7.64 us (6%)
  between operations  1.6 us (1%)
    ppermute x17, waiting for transfers between devices, send(): return lax.ppermute(array, 'fsdp', pairs)  22.2 us
    dot_general x13, matrix products, dot(): lax.dot_general(left, right, (dims, ((), ())), preferred_element_type=F32)  21.2 us
    ppermute x17, starting transfers between devices, send(): return lax.ppermute(array, 'fsdp', pairs)  20.2 us
    all_to_all x1, waiting for transfers between devices, per_device(): lax.all_to_all(send_rows.reshape(experts, half, 2 * width + 128), 'ep', 0...  13.8 us
    all_to_all x1, starting transfers between devices, per_device(): lax.all_to_all(send_rows.reshape(experts, half, 2 * width + 128), 'ep', 0...  7.61 us
    all_to_all x1, waiting for transfers between devices, per_device(): lax.all_to_all(jnp.concatenate([own.astype(BF16).reshape(experts, half, s...  4.73 us
    all_to_all x1, starting transfers between devices, per_device(): lax.all_to_all(jnp.concatenate([own.astype(BF16).reshape(experts, half, s...  4.5 us
    concatenate x3, other arithmetic, per_device(): w_in = jnp.concatenate([w_in, send(w_in, TO_CORE)], axis=0)  4.08 us
  transfers between devices with their start and end apart: 19, of which 10 were waited for; matrix products, arithmetic and copies ran while one was open for 26% of the time, Pallas kernels for 0%

profile of v7, /device:TPU:1, one launch (start us, length us, event | category | flops | bytes accessed | tf_op | source)
XLA Modules:
  0.0 124.4 jit_solution(10980715546551109764)
XLA Ops:
  1.6 4.6 %convolution_convert_fusion = bf16[128,12416]{1,0:T(8,128)(2,1)} fusion(bf16[128,128]{1,0:T(8,128)(2,1)S(1)} %broadcast_in_dim.48, bf16[128,6144]{1,0:T(8,128)(2,1)} %param.7, bf16[128,6144]{1,0:T(8,128)(2,1)} %param.8, pred[128,2,128]{2,0,1:T(32,128)(4,1)S(1)} %iota_compare_fusion.3), kind=kOutput, calls=%fused_computation | convolution fusion | flops 417988608 | bytes 6389760 | tf_op jit(solution)/shard_map/dot_general | solution.py:35
  6.2 7.6 %all-to-all-start = ((bf16[8,16,12416]{2,1,0:T(8,128)(2,1)}), bf16[8,16,12416]{2,1,0:T(8,128)(2,1)}, u32[]{:S(2)}, u32[]{:S(2)}) async-start(bf16[8,16,12416]{2,1,0:T(8,128)(2,1)} %bitcast.153), calls=%async_computation | async-start | bytes 6356992 | tf_op jit(solution)/shard_map/all_to_all | solution.py:80
  15.0 1.9 %convolution_bitcast_fusion = f32[128,24]{0,1:T(8,128)S(1)} fusion(bf16[128,6144]{1,0:T(8,128)(2,1)} %param.7, bf16[6144,8]{0,1:T(8,128)(2,1)S(1)} %get-tuple-element.123, bf16[6144,8]{0,1:T(8,128)(2,1)S(1)} %get-tuple-element.124, bf16[6144,8]{0,1:T(8,128)(2,1)S(1)} %get-tuple-element.122), kind=kOutput, calls=%fused_computation.58 | convolution fusion | flops 38633472 | bytes 1880064 | tf_op jit(solution)/shard_map/dot_general | solution.py:35
  17.4 3.3 %collective-permute-done = bf16[168,6144]{1,0:T(8,128)(2,1)} collective-permute-done((bf16[168,6144]{1,0:T(8,128)(2,1)S(1)}, bf16[168,6144]{1,0:T(8,128)(2,1)}, u32[]{:S(2)}, u32[]{:S(2)}) %collective-permute-start) | collective-permute-done | bytes 2064416 | tf_op jit(solution)/shard_map/ppermute | solution.py:31
  27.4 3.2 %fusion.5 = bf16[360,6272]{1,0:T(8,128)(2,1)S(1)} fusion(bf16[24,6144]{1,0:T(8,128)(2,1)S(1)} %fusion.47, bf16[168,6144]{1,0:T(8,128)(2,1)} %collective-permute-done, bf16[168,6144]{1,0:T(8,128)(2,1)S(1)} %bitcast.152), kind=kLoop, calls=%fused_computation.41 | loop fusion | flops 22579200 | bytes 8939520 | tf_op jit(solution)/shard_map/concatenate | solution.py:91
  33.9 4.0 %pad_maximum_fusion = bf16[336,6144]{1,0:T(8,128)(2,1)} fusion(bf16[168,6144]{1,0:T(8,128)(2,1)} %collective-permute-done.1, bf16[168,6144]{1,0:T(8,128)(2,1)S(1)} %bitcast.155), kind=kLoop, calls=%fused_computation.42 | loop fusion | flops 8257536 | bytes 8257536 | tf_op jit(solution)/shard_map/concatenate | solution.py:69
  37.9 13.8 %all-to-all-done = bf16[8,16,12416]{2,1,0:T(8,128)(2,1)} async-done(((bf16[8,16,12416]{2,1,0:T(8,128)(2,1)}), bf16[8,16,12416]{2,1,0:T(8,128)(2,1)}, u32[]{:S(2)}, u32[]{:S(2)}) %all-to-all-start) | async-done | bytes 3178528 | tf_op jit(solution)/shard_map/all_to_all | solution.py:80
  51.7 2.1 %fusion.17 = f32[128,361]{0,1:T(8,128)S(1)} fusion(bf16[361,3200]{1,0:T(8,128)(2,1)S(1)} %pad_maximum_fusion.1, bf16[128,12416]{1,0:T(8,128)(2,1)} %bitcast.2), kind=kOutput, calls=%fused_computation.65 | convolution fusion | flops 295731200 | bytes 3314432 | tf_op jit(solution)/shard_map/dot_general | solution.py:35
  53.8 1.9 %convolution_add_fusion = f32[128,361]{0,1:T(8,128)S(1)} fusion(f32[128,361]{0,1:T(8,128)S(1)} %fusion.17, bf16[361,3072]{1,0:T(8,128)(2,1)S(1)} %copy-done.2, bf16[128,12416]{1,0:T(8,128)(2,1)} %bitcast.2), kind=kOutput, calls=%fused_computation.57 | convolution fusion | flops 283948160 | bytes 3374080 | tf_op jit(solution)/shard_map/dot_general | solution.py:35
  55.8 2.7 %fusion.46 = (bf16[128,336]{0,1:T(8,128)(2,1)S(1)}, bf16[128,336]{0,1:T(8,128)(2,1)S(1)}, bf16[128,336]{0,1:T(8,128)(2,1)S(1)}, f32[128,336]{0,1:T(8,128)S(1)}) fusion(f32[128]{0:T(128)S(1)} %convert_element_type.242, f32[128,361]{0,1:T(8,128)S(1)} %convolution_add_fusion, bf16[336,6144]{1,0:T(8,128)(2,1)S(1)} %copy-done.3, bf16[128,12416]{1,0:T(8,128)(2,1)} %bitcast.2), kind=kOutput, calls=%fused_computation.118 | convolution fusion | flops 529127424 | bytes 6304256 | tf_op jit(solution)/shard_map/dot_general | solution.py:35
  60.4 5.6 %collective-permute-start.3 = (bf16[136,768]{1,0:T(8,128)(2,1)S(1)}, bf16[136,768]{1,0:T(8,128)(2,1)S(1)}, u32[]{:S(2)}, u32[]{:S(2)}) collective-permute-start(bf16[136,768]{1,0:T(8,128)(2,1)S(1)} %get-tuple-element.54), channel_id=1, source_target_pairs={{0,112},{8,120},{16,0},{24,8},{32,16},{40,24},{48,32},{56,40},{64,... | collective-permute-start | bytes 626696 | tf_op jit(solution)/shard_map/ppermute | solution.py:31
  67.2 3.3 %collective-permute-done.3 = bf16[136,768]{1,0:T(8,128)(2,1)S(1)} collective-permute-done((bf16[136,768]{1,0:T(8,128)(2,1)S(1)}, bf16[136,768]{1,0:T(8,128)(2,1)S(1)}, u32[]{:S(2)}, u32[]{:S(2)}) %collective-permute-start.3) | collective-permute-done | bytes 208928 | tf_op jit(solution)/shard_map/ppermute | solution.py:31
  70.6 3.1 %collective-permute-done.2 = bf16[136,768]{1,0:T(8,128)(2,1)S(1)} collective-permute-done((bf16[136,768]{1,0:T(8,128)(2,1)S(1)}, bf16[136,768]{1,0:T(8,128)(2,1)S(1)}, u32[]{:S(2)}, u32[]{:S(2)}) %collective-permute-start.2) | collective-permute-done | bytes 208928 | tf_op jit(solution)/shard_map/ppermute | solution.py:31
  75.9 2.1 %constant_dynamic-update-slice_fusion.1 = bf16[256,12416]{1,0:T(8,128)(2,1)S(1)} fusion(bf16[128,12416]{1,0:T(8,128)(2,1)} %bitcast.2), kind=kLoop, calls=%fused_computation.201 | loop fusion | bytes 6356992
  78.0 2.3 %constant_dynamic-update-slice_fusion = bf16[256,12416]{1,0:T(8,128)(2,1)S(1)} fusion(bf16[256,12416]{1,0:T(8,128)(2,1)S(1)} %constant_dynamic-update-slice_fusion.1, bf16[128,12416]{1,0:T(8,128)(2,1)} %collective-permute-done.4), kind=kLoop, calls=%fused_computation.200 | loop fusion | bytes 6356992 | tf_op jit(solution)/shard_map/concatenate | solution.py:173
  83.0 2.0 %convolution_convert_fusion.2 = bf16[168,6144]{1,0:T(8,128)(2,1)} fusion(bf16[256,168]{0,1:T(8,128)(2,1)S(1)} %pad_maximum_fusion.19, bf16[256,12416]{1,0:T(8,128)(2,1)S(1)} %constant_dynamic-update-slice_fusion), kind=kOutput, calls=%fused_computation.38 | convolution fusion | flops 529514496 | bytes 5296128 | tf_op jit(solution)/shard_map/dot_general | solution.py:35
  85.5 3.0 %collective-permute-done.9 = bf16[136,768]{1,0:T(8,128)(2,1)S(1)} collective-permute-done((bf16[136,768]{1,0:T(8,128)(2,1)S(1)}, bf16[136,768]{1,0:T(8,128)(2,1)S(1)}, u32[]{:S(2)}, u32[]{:S(2)}) %collective-permute-start.9) | collective-permute-done | bytes 208928 | tf_op jit(solution)/shard_map/ppermute | solution.py:31
  88.8 5.8 %collective-permute-done.10 = bf16[136,768]{1,0:T(8,128)(2,1)S(1)} collective-permute-done((bf16[136,768]{1,0:T(8,128)(2,1)S(1)}, bf16[136,768]{1,0:T(8,128)(2,1)S(1)}, u32[]{:S(2)}, u32[]{:S(2)}) %collective-permute-start.10) | collective-permute-done | bytes 208928 | tf_op jit(solution)/shard_map/ppermute | solution.py:31
  95.2 4.4 %collective-permute-start.13 = (f32[1,128]{1,0:T(1,128)S(1)}, f32[1,128]{1,0:T(1,128)S(1)}, u32[]{:S(2)}, u32[]{:S(2)}) collective-permute-start(f32[1,128]{1,0:T(1,128)S(1)} %get-tuple-element.85), channel_id=1, source_target_pairs={{0,8},{8,0},{16,24},{24,16},{32,40},{40,32},{48,56},{56,48},{64,72... | collective-permute-start | bytes 1544 | tf_op jit(solution)/shard_map/ppermute | solution.py:31
  100.6 2.6 %collective-permute-done.14 = f32[1,128]{1,0:T(1,128)S(1)} collective-permute-done((f32[1,128]{1,0:T(1,128)S(1)}, f32[1,128]{1,0:T(1,128)S(1)}, u32[]{:S(2)}, u32[]{:S(2)}) %collective-permute-start.14) | collective-permute-done | bytes 544 | tf_op jit(solution)/shard_map/ppermute | solution.py:31
  104.8 4.5 %all-to-all-start.1 = ((bf16[8,88,384]{2,1,0:T(8,128)(2,1)}), bf16[8,88,384]{2,1,0:T(8,128)(2,1)S(1)}, u32[]{:S(2)}, u32[]{:S(2)}) async-start(bf16[8,88,384]{2,1,0:T(8,128)(2,1)} %fusion.21), calls=%async_computation.1 | async-start | bytes 1081344 | tf_op jit(solution)/shard_map/all_to_all | solution.py:204
  110.4 3.9 %fusion.3 = bf16[1,6144,168]{1,2,0:T(8,128)(2,1)} fusion(bf16[256,168]{0,1:T(8,128)(2,1)S(1)} %pad_maximum_fusion.18, bf16[256,12416]{1,0:T(8,128)(2,1)} %copy-done.1), kind=kOutput, calls=%fused_computation.39 | convolution fusion | flops 529514496 | bytes 5296128 | tf_op jit(solution)/shard_map/dot_general | solution.py:35
  114.3 4.7 %all-to-all-done.1 = bf16[8,88,384]{2,1,0:T(8,128)(2,1)S(1)} async-done(((bf16[8,88,384]{2,1,0:T(8,128)(2,1)}), bf16[8,88,384]{2,1,0:T(8,128)(2,1)S(1)}, u32[]{:S(2)}, u32[]{:S(2)}) %all-to-all-start.1) | async-done | bytes 540704 | tf_op jit(solution)/shard_map/all_to_all | solution.py:204
  119.4 2.4 %collective-permute-start.16 = (f32[8,3200]{1,0:T(8,128)S(1)}, f32[8,3200]{1,0:T(8,128)S(1)}, u32[]{:S(2)}, u32[]{:S(2)}) collective-permute-start(f32[8,3200]{1,0:T(8,128)S(1)} %select_maximum_fusion), channel_id=1, source_target_pairs={{0,8},{8,0},{16,24},{24,16},{32,40},{40,32},{48,56},{56,48},{64,72... | collective-permute-start | bytes 307208 | tf_op jit(solution)/shard_map/ppermute | solution.py:31
  (160 shorter events, 27.9 us)
Async XLA Ops:
  6.2 7.6 %copy-start = (bf16[1,6144,168]{1,2,0:T(8,128)(2,1)S(1)}, bf16[1,6144,168]{1,2,0:T(8,128)(2,1)}, u32[]{:S(2)}) copy-start(bf16[1,6144,168]{1,2,0:T(8,128)(2,1)} %param.10) | copy-start | bytes 6193156
  6.2 8.8 %copy-start.8 = (f32[6144,8]{0,1:T(8,128)S(1)}, f32[6144,8]{0,1:T(8,128)}, u32[]{:S(2)}) copy-start(f32[6144,8]{0,1:T(8,128)} %param.9) | copy-start | bytes 589828
  6.2 11.0 %copy-start.9 = (s32[128,2]{0,1:T(2,128)S(1)}, s32[128,2]{0,1:T(2,128)}, u32[]{:S(2)}) copy-start(s32[128,2]{0,1:T(2,128)} %param.12) | copy-start | bytes 3076
  6.2 45.4 %all-to-all-start = ((bf16[8,16,12416]{2,1,0:T(8,128)(2,1)}), bf16[8,16,12416]{2,1,0:T(8,128)(2,1)}, u32[]{:S(2)}, u32[]{:S(2)}) async-start(bf16[8,16,12416]{2,1,0:T(8,128)(2,1)} %bitcast.153), calls=%async_computation | async-start | bytes 6356992 | tf_op jit(solution)/shard_map/all_to_all | solution.py:80
  13.8 6.9 %collective-permute-start = (bf16[168,6144]{1,0:T(8,128)(2,1)S(1)}, bf16[168,6144]{1,0:T(8,128)(2,1)}, u32[]{:S(2)}, u32[]{:S(2)}) collective-permute-start(bf16[168,6144]{1,0:T(8,128)(2,1)S(1)} %bitcast.148), channel_id=1, source_target_pairs={{0,8},{8,0},{16,24},{24,16},{32,40},{40,32},{48,56},{56,48},{64,72... | collective-permute-start | bytes 6193160 | tf_op jit(solution)/shard_map/ppermute | solution.py:31
  14.9 17.7 %collective-permute-start.1 = (bf16[168,6144]{1,0:T(8,128)(2,1)}, bf16[168,6144]{1,0:T(8,128)(2,1)}, u32[]{:S(2)}, u32[]{:S(2)}) collective-permute-start(bf16[168,6144]{1,0:T(8,128)(2,1)} %bitcast.154), channel_id=1, source_target_pairs={{0,8},{8,0},{16,24},{24,16},{32,40},{40,32},{48,56},{56,48},{64,72... | collective-permute-start | bytes 6193160 | tf_op jit(solution)/shard_map/ppermute | solution.py:31
  58.5 8.3 %copy-start.6 = (bf16[336,1536]{1,0:T(8,128)(2,1)S(1)}, bf16[336,1536]{1,0:T(8,128)(2,1)}, u32[]{:S(2)}) copy-start(bf16[336,1536]{1,0:T(8,128)(2,1)} %get-tuple-element.53) | copy-start | bytes 3096580
  59.1 14.8 %collective-permute-start.4 = (bf16[128,12416]{1,0:T(8,128)(2,1)}, bf16[128,12416]{1,0:T(8,128)(2,1)}, u32[]{:S(2)}, u32[]{:S(2)}) collective-permute-start(bf16[128,12416]{1,0:T(8,128)(2,1)} %bitcast.2), channel_id=1, source_target_pairs={{0,8},{8,0},{16,24},{24,16},{32,40},{40,32},{48,56},{56,48},{64,72... | collective-permute-start | bytes 9535496 | tf_op jit(solution)/shard_map/ppermute | solution.py:31
  60.4 10.1 %collective-permute-start.3 = (bf16[136,768]{1,0:T(8,128)(2,1)S(1)}, bf16[136,768]{1,0:T(8,128)(2,1)S(1)}, u32[]{:S(2)}, u32[]{:S(2)}) collective-permute-start(bf16[136,768]{1,0:T(8,128)(2,1)S(1)} %get-tuple-element.54), channel_id=1, source_target_pairs={{0,112},{8,120},{16,0},{24,8},{32,16},{40,24},{48,32},{56,40},{64,... | collective-permute-start | bytes 626696 | tf_op jit(solution)/shard_map/ppermute | solution.py:31
  66.0 7.6 %collective-permute-start.2 = (bf16[136,768]{1,0:T(8,128)(2,1)S(1)}, bf16[136,768]{1,0:T(8,128)(2,1)S(1)}, u32[]{:S(2)}, u32[]{:S(2)}) collective-permute-start(bf16[136,768]{1,0:T(8,128)(2,1)S(1)} %get-tuple-element.51), channel_id=1, source_target_pairs={{0,16},{8,24},{16,32},{24,40},{32,48},{40,56},{48,64},{56,72},{64,... | collective-permute-start | bytes 626696 | tf_op jit(solution)/shard_map/ppermute | solution.py:31
  66.0 9.5 %copy-start.5 = (bf16[336,1536]{1,0:T(8,128)(2,1)S(1)}, bf16[336,1536]{1,0:T(8,128)(2,1)}, u32[]{:S(2)}) copy-start(bf16[336,1536]{1,0:T(8,128)(2,1)} %get-tuple-element.60) | copy-start | bytes 3096580
  66.1 7.9 %collective-permute-start.5 = (bf16[128,336]{0,1:T(8,128)(2,1)S(1)}, bf16[128,336]{0,1:T(8,128)(2,1)S(1)}, u32[]{:S(2)}, u32[]{:S(2)}) collective-permute-start(bf16[128,336]{0,1:T(8,128)(2,1)S(1)} %pad_maximum_fusion.17), channel_id=1, source_target_pairs={{0,8},{8,0},{16,24},{24,16},{32,40},{40,32},{48,56},{56,48},{64,72... | collective-permute-start | bytes 258056 | tf_op jit(solution)/shard_map/ppermute | solution.py:31
  66.5 7.4 %collective-permute-start.6 = (f32[128,8]{0,1:T(8,128)S(1)}, f32[128,8]{0,1:T(8,128)S(1)}, u32[]{:S(2)}, u32[]{:S(2)}) collective-permute-start(f32[128,8]{0,1:T(8,128)S(1)} %subtract_multiply_fusion), channel_id=1, source_target_pairs={{0,8},{8,0},{16,24},{24,16},{32,40},{40,32},{48,56},{56,48},{64,72... | collective-permute-start | bytes 12296 | tf_op jit(solution)/shard_map/ppermute | solution.py:31
  74.0 6.7 %collective-permute-start.8 = (bf16[136,768]{1,0:T(8,128)(2,1)S(1)}, bf16[136,768]{1,0:T(8,128)(2,1)S(1)}, u32[]{:S(2)}, u32[]{:S(2)}) collective-permute-start(bf16[136,768]{1,0:T(8,128)(2,1)S(1)} %pad_maximum_fusion.11), channel_id=1, source_target_pairs={{0,112},{8,120},{16,0},{24,8},{32,16},{40,24},{48,32},{56,40},{64,... | collective-permute-start | bytes 626696 | tf_op jit(solution)/shard_map/ppermute | solution.py:31
  74.4 6.7 %collective-permute-start.7 = (bf16[136,768]{1,0:T(8,128)(2,1)S(1)}, bf16[136,768]{1,0:T(8,128)(2,1)S(1)}, u32[]{:S(2)}, u32[]{:S(2)}) collective-permute-start(bf16[136,768]{1,0:T(8,128)(2,1)S(1)} %pad_maximum_fusion.10), channel_id=1, source_target_pairs={{0,16},{8,24},{16,32},{24,40},{32,48},{40,56},{48,64},{56,72},{64,... | collective-permute-start | bytes 626696 | tf_op jit(solution)/shard_map/ppermute | solution.py:31
  81.4 7.4 %collective-permute-start.11 = (bf16[136,768]{1,0:T(8,128)(2,1)S(1)}, bf16[136,768]{1,0:T(8,128)(2,1)S(1)}, u32[]{:S(2)}, u32[]{:S(2)}) collective-permute-start(bf16[136,768]{1,0:T(8,128)(2,1)S(1)} %pad_maximum_fusion.13), channel_id=1, source_target_pairs={{0,112},{8,120},{16,0},{24,8},{32,16},{40,24},{48,32},{56,40},{64,... | collective-permute-start | bytes 626696 | tf_op jit(solution)/shard_map/ppermute | solution.py:31
  82.6 5.9 %collective-permute-start.9 = (bf16[136,768]{1,0:T(8,128)(2,1)S(1)}, bf16[136,768]{1,0:T(8,128)(2,1)S(1)}, u32[]{:S(2)}, u32[]{:S(2)}) collective-permute-start(bf16[136,768]{1,0:T(8,128)(2,1)S(1)} %pad_maximum_fusion.12), channel_id=1, source_target_pairs={{0,16},{8,24},{16,32},{24,40},{32,48},{40,56},{48,64},{56,72},{64,... | collective-permute-start | bytes 626696 | tf_op jit(solution)/shard_map/ppermute | solution.py:31
  88.7 5.9 %collective-permute-start.10 = (bf16[136,768]{1,0:T(8,128)(2,1)S(1)}, bf16[136,768]{1,0:T(8,128)(2,1)S(1)}, u32[]{:S(2)}, u32[]{:S(2)}) collective-permute-start(bf16[136,768]{1,0:T(8,128)(2,1)S(1)} %pad_maximum_fusion.14), channel_id=1, source_target_pairs={{0,16},{8,24},{16,32},{24,40},{32,48},{40,56},{48,64},{56,72},{64,... | collective-permute-start | bytes 626696 | tf_op jit(solution)/shard_map/ppermute | solution.py:31
  94.8 8.4 %collective-permute-start.12 = (bf16[136,384]{1,0:T(8,128)(2,1)S(1)}, bf16[136,384]{1,0:T(8,128)(2,1)S(1)}, u32[]{:S(2)}, u32[]{:S(2)}) collective-permute-start(bf16[136,384]{1,0:T(8,128)(2,1)S(1)} %pad_maximum_fusion.16), channel_id=1, source_target_pairs={{0,128},{8,136},{16,144},{24,152},{32,160},{40,168},{48,176},{56,1... | collective-permute-start | bytes 313352 | tf_op jit(solution)/shard_map/ppermute | solution.py:31
  95.2 5.4 %collective-permute-start.13 = (f32[1,128]{1,0:T(1,128)S(1)}, f32[1,128]{1,0:T(1,128)S(1)}, u32[]{:S(2)}, u32[]{:S(2)}) collective-permute-start(f32[1,128]{1,0:T(1,128)S(1)} %get-tuple-element.85), channel_id=1, source_target_pairs={{0,8},{8,0},{16,24},{24,16},{32,40},{40,32},{48,56},{56,48},{64,72... | collective-permute-start | bytes 1544 | tf_op jit(solution)/shard_map/ppermute | solution.py:31
  99.6 3.7 %collective-permute-start.14 = (f32[1,128]{1,0:T(1,128)S(1)}, f32[1,128]{1,0:T(1,128)S(1)}, u32[]{:S(2)}, u32[]{:S(2)}) collective-permute-start(f32[1,128]{1,0:T(1,128)S(1)} %get-tuple-element.85), channel_id=1, source_target_pairs={{0,136},{8,128},{16,152},{24,144},{32,168},{40,160},{48,184},{56,1... | collective-permute-start | bytes 1544 | tf_op jit(solution)/shard_map/ppermute | solution.py:31
  104.8 14.2 %all-to-all-start.1 = ((bf16[8,88,384]{2,1,0:T(8,128)(2,1)}), bf16[8,88,384]{2,1,0:T(8,128)(2,1)S(1)}, u32[]{:S(2)}, u32[]{:S(2)}) async-start(bf16[8,88,384]{2,1,0:T(8,128)(2,1)} %fusion.21), calls=%async_computation.1 | async-start | bytes 1081344 | tf_op jit(solution)/shard_map/all_to_all | solution.py:204
  119.4 3.3 %collective-permute-start.16 = (f32[8,3200]{1,0:T(8,128)S(1)}, f32[8,3200]{1,0:T(8,128)S(1)}, u32[]{:S(2)}, u32[]{:S(2)}) collective-permute-start(f32[8,3200]{1,0:T(8,128)S(1)} %select_maximum_fusion), channel_id=1, source_target_pairs={{0,8},{8,0},{16,24},{24,16},{32,40},{40,32},{48,56},{56,48},{64,72... | collective-permute-start | bytes 307208 | tf_op jit(solution)/shard_map/ppermute | solution.py:31
  122.0 1.4 %collective-permute-start.15 = (bf16[192,128]{1,0:T(8,128)(2,1)S(1)}, bf16[192,128]{1,0:T(8,128)(2,1)S(1)}, u32[]{:S(2)}, u32[]{:S(2)}) collective-permute-start(bf16[192,128]{1,0:T(8,128)(2,1)S(1)} %select_convert_fusion), channel_id=1, source_target_pairs={{0,8},{8,0},{16,24},{24,16},{32,40},{40,32},{48,56},{56,48},{64,72... | collective-permute-start | bytes 147464 | tf_op jit(solution)/shard_map/ppermute | solution.py:31
  (5 other events, 14.3 us)
